TPU v7x, 256 devices: a whole 4x4x8 slice. The times are simulated.
256 devices in a mesh: pipe: 2 (over z_lo), replica: 32 (over x, y, core), space: 4 (over z_hi).
Axes of the slice: x: 4, y: 4, z: 8 (z_hi: 4, z_lo: 2; z = z_hi * 2 + z_lo), core: 2. Of those that a mesh axis runs over, the one named last changes fastest.
Arguments:
- views: bfloat16 [2, 32, 32, 100, 176], P('pipe', 'replica', 'space'), may hold values from -1.6953125 to 1.6953125
- w_expand: bfloat16 [2, 176, 1056], P('pipe'), may hold values from -0.12988281 to 0.12988281
- w_depth: bfloat16 [2, 5, 5, 1056], P('pipe'), may hold values from -0.34960938 to 0.34960938
- w_reduce: bfloat16 [2, 1056, 44], P('pipe'), may hold values from -0.19921875 to 0.19921875
- w_excite: bfloat16 [2, 44, 1056], P('pipe'), may hold values from -0.5 to 0.5
- w_project: bfloat16 [2, 1056, 176], P('pipe'), may hold values from -0.052978516 to 0.052978516
- w_head: bfloat16 [2, 176, 5504], P('pipe'), may hold values from -0.12988281 to 0.12988281
- w_class: bfloat16 [2, 5504, 500], P('pipe'), may hold values from -0.22949219 to 0.22949219
Outputs:
- g_expand: float32 [2, 176, 1056], P('pipe')
- g_depth: float32 [2, 5, 5, 1056], P('pipe')
- g_reduce: float32 [2, 1056, 44], P('pipe')
- g_excite: float32 [2, 44, 1056], P('pipe')
- g_project: float32 [2, 1056, 176], P('pipe')
All inputs are finite; a program needn't handle non-finite values.
Results may differ from a plain program's by a relative error of at most 0.0065.
Values may be sent and summed in bfloat16 or wider, within the bound.
No kernel may reach another device: no remote copies, remote signals or barrier semaphores. Data moves between devices by JAX's collectives and lax.ppermute only.
A program may use at most 128 MiB of HBM per device.

v0:
```python
from functools import reduce

import jax
import jax.numpy as jnp
from jax import lax
from jax.sharding import PartitionSpec as P

loss_scale = 256.0
highest = lax.Precision.HIGHEST


def with_halo(array, sides, width):
    for axis, dim in sides:
        size, length = (lax.axis_size(axis), array.shape[dim])
        up = [(i, (i + 1) % size) for i in range(size - 1)]
        down = [(j, i) for i, j in up]
        last = lax.slice_in_dim(array, length - width, length, axis=dim)
        first = lax.slice_in_dim(array, 0, width, axis=dim)
        before = lax.ppermute(last, axis, up)
        after = lax.ppermute(first, axis, down)
        array = jnp.concatenate([before, array, after], axis=dim)
    return array


def swapped(array, axis, stride):
    return lax.ppermute(array, axis, [(i, i ^ 1 << stride) for i in range(lax.axis_size(axis))])


def swish_act(value):
    return value * jax.nn.sigmoid(value)


def swish_slope(value):
    sigma = jax.nn.sigmoid(value)
    return sigma * (1.0 + value * (1.0 - sigma))


def depthwise(padded, kernel, height, breadth):
    extent = kernel.shape[0]
    pieces = [
        padded[..., step_y : step_y + height, step_x : step_x + breadth, :].astype(jnp.float32)
        * kernel[step_y, step_x].astype(jnp.float32)
        for step_y in range(extent)
        for step_x in range(extent)
    ]
    return reduce(lambda left, right: left + right, pieces)


def transposed(padded, kernel, height, breadth):
    extent = kernel.shape[0]
    pieces = [
        padded[
            ...,
            extent - 1 - step_y : extent - 1 - step_y + height,
            extent - 1 - step_x : extent - 1 - step_x + breadth,
            :,
        ].astype(jnp.float32)
        * kernel[step_y, step_x].astype(jnp.float32)
        for step_y in range(extent)
        for step_x in range(extent)
    ]
    return reduce(lambda left, right: left + right, pieces)


def kernel_grad(gradient, padded, height, breadth, extent):
    axes_all = tuple(range(gradient.ndim - 1))
    grad_wide = gradient.astype(jnp.float32)
    stacked = [
        jnp.stack(
            [
                jnp.sum(
                    grad_wide
                    * padded[..., step_y : step_y + height, step_x : step_x + breadth, :].astype(
                        jnp.float32
                    ),
                    axis=axes_all,
                )
                for step_x in range(extent)
            ]
        )
        for step_y in range(extent)
    ]
    return jnp.stack(stacked)


def shards(views, w_expand, w_depth, w_reduce, w_excite, w_project, w_head, w_class):
    own_view = views[0]
    expand_w = w_expand[0]
    depth_w = w_depth[0]
    reduce_w = w_reduce[0]
    excite_w = w_excite[0]
    project_w = w_project[0]
    head_w = w_head[0]
    class_w = w_class[0]
    images, row_count, col_count, channels = own_view.shape
    hidden = expand_w.shape[1]
    head_width = head_w.shape[1]
    extent = depth_w.shape[0]
    margin = extent // 2
    cell_total = row_count * lax.axis_size("space") * col_count
    flat_view = own_view.reshape(-1, channels)
    pre_expand = jnp.dot(flat_view, expand_w, preferred_element_type=jnp.float32).reshape(
        images, row_count, col_count, hidden
    )
    expanded = swish_act(pre_expand).astype(jnp.bfloat16)
    with_rim = with_halo(expanded, (("space", 1),), 2)
    padded_exp = jnp.pad(with_rim, ((0, 0), (0, 0), (margin, margin), (0, 0)))
    pre_depth = depthwise(padded_exp, depth_w, row_count, col_count)
    act_depth = swish_act(pre_depth)
    squeeze = lax.psum(jnp.sum(act_depth, axis=(1, 2)), "space") / cell_total
    reduced_in = jnp.dot(squeeze, reduce_w.astype(jnp.float32), precision=highest)
    reduced = swish_act(reduced_in)
    excite_gate = jax.nn.sigmoid(jnp.dot(reduced, excite_w.astype(jnp.float32), precision=highest))
    gated = (act_depth * excite_gate[:, None, None, :]).astype(jnp.bfloat16)
    flat_gated = gated.reshape(-1, hidden)
    block_out = (
        flat_view.astype(jnp.float32)
        + jnp.dot(flat_gated, project_w, preferred_element_type=jnp.float32)
    ).astype(jnp.bfloat16)
    pre_head = jnp.dot(block_out, head_w, preferred_element_type=jnp.float32)
    head_sum = jnp.sum(swish_act(pre_head).reshape(images, -1, head_width), axis=1)
    pooled = (lax.psum(head_sum, "space") / cell_total).astype(jnp.bfloat16)
    logits = jnp.dot(pooled, class_w, preferred_element_type=jnp.float32)
    partner = swapped(logits, "pipe", 0)
    teacher = lax.axis_index("pipe") == 0
    teacher_logits = jnp.where(teacher, logits, partner)
    student_logits = jnp.where(teacher, partner, logits)
    exp_teacher = jnp.exp(teacher_logits)
    teacher_prob = exp_teacher / jnp.sum(exp_teacher, axis=-1, keepdims=True)
    student_logprob = student_logits - jnp.log(
        jnp.sum(jnp.exp(student_logits), axis=-1, keepdims=True)
    )
    cross = jnp.sum(teacher_prob * student_logprob, axis=-1, keepdims=True)
    teacher_grad = loss_scale * teacher_prob * (cross - student_logprob)
    student_grad = loss_scale * (jnp.exp(student_logprob) - teacher_prob)
    grad_logits = jnp.where(teacher, teacher_grad, student_grad).astype(jnp.bfloat16)
    grad_pooled = jnp.einsum("ik,fk->if", grad_logits, class_w, preferred_element_type=jnp.float32)
    grad_head = (
        (
            grad_pooled[:, None, :]
            / cell_total
            * swish_slope(pre_head.reshape(images, -1, head_width))
        )
        .astype(jnp.bfloat16)
        .reshape(-1, head_width)
    )
    grad_block = jnp.einsum(
        "mf,cf->mc", grad_head, head_w, preferred_element_type=jnp.float32
    ).astype(jnp.bfloat16)
    g_project = jnp.einsum("me,mc->ec", flat_gated, grad_block, preferred_element_type=jnp.float32)
    grad_gated = jnp.einsum(
        "mc,ec->me", grad_block, project_w, preferred_element_type=jnp.float32
    ).reshape(images, row_count, col_count, hidden)
    grad_gate = lax.psum(jnp.sum(grad_gated * act_depth, axis=(1, 2)), "space")
    grad_excite = grad_gate * excite_gate * (1.0 - excite_gate)
    first_block = lax.axis_index("space") == 0
    g_excite = jnp.where(
        first_block, jnp.einsum("ir,ie->re", reduced, grad_excite, precision=highest), 0.0
    )
    grad_reduced = jnp.einsum(
        "ie,re->ir", grad_excite, excite_w.astype(jnp.float32), precision=highest
    ) * swish_slope(reduced_in)
    g_reduce = jnp.where(
        first_block, jnp.einsum("ie,ir->er", squeeze, grad_reduced, precision=highest), 0.0
    )
    back_pool = jnp.einsum(
        "ir,er->ie", grad_reduced, reduce_w.astype(jnp.float32), precision=highest
    )
    grad_act = (
        grad_gated * excite_gate[:, None, None, :] + (back_pool / cell_total)[:, None, None, :]
    )
    grad_depth = (grad_act * swish_slope(pre_depth)).astype(jnp.bfloat16)
    grad_rim = with_halo(grad_depth, (("space", 1),), 2)
    padded_grad = jnp.pad(grad_rim, ((0, 0), (0, 0), (margin, margin), (0, 0)))
    g_depth = kernel_grad(grad_depth, padded_exp, row_count, col_count, extent)
    grad_expanded = transposed(padded_grad, depth_w, row_count, col_count)
    grad_expand = (grad_expanded * swish_slope(pre_expand)).astype(jnp.bfloat16)
    g_expand = jnp.einsum(
        "mc,me->ce", flat_view, grad_expand.reshape(-1, hidden), preferred_element_type=jnp.float32
    )
    g_expand, g_depth, g_reduce, g_excite, g_project = lax.psum(
        (g_expand, g_depth, g_reduce, g_excite, g_project), ("replica", "space")
    )
    return (g_expand[None], g_depth[None], g_reduce[None], g_excite[None], g_project[None])


def solution(mesh):
    in_specs = (
        P("pipe", "replica", "space", None, None),
        P("pipe", None, None),
        P("pipe", None, None, None),
        P("pipe", None, None),
        P("pipe", None, None),
        P("pipe", None, None),
        P("pipe", None, None),
        P("pipe", None, None),
    )
    out_specs = (
        P("pipe", None, None),
        P("pipe", None, None, None),
        P("pipe", None, None),
        P("pipe", None, None),
        P("pipe", None, None),
    )
    return jax.shard_map(shards, mesh=mesh, in_specs=in_specs, out_specs=out_specs, check_vma=False)
```

profile of v0, /device:TPU:1, one launch (start us, length us, event | category | flops | bytes accessed | tf_op | source)
XLA Modules:
  0.0 1567.2 jit_solution(12515516414099899443)
XLA Ops:
  7.2 1.2 copy.14
  8.7 3.6 fusion.94
  12.3 3.5 reshape.439
  15.8 4.4 multiply_convert_fusion.4
  20.2 2.2 fusion.160
  22.4 1.3 collective-permute-start.1
  23.7 7.2 collective-permute-start
  31.4 17.2 %collective-permute-done.1 = bf16[1,2,100,1056]{3,2,1,0:T(8,128)(2,1)S(1)} collective-permute-done((bf16[1,2,100,1056]{3,2,1,0:T(8,128)(2,1)}, bf16[1,2,100,1056]{3,2,1,0:T(8,128)(2,1)S(1)}, u32[]{:S(2)}, u32[]{:S(2)}) %collective-permute-start.1) | collective-permute-done | bytes 422432 | tf_op jit(solution)/shard_map/ppermute | solution.py:20
  48.6 4.0 fusion.75
  52.7 17.1 %fusion.156 = (f32[1056]{0:T(1024)S(1)}, f32[1,8,100,1056]{3,2,1,0:T(8,128)}) fusion(f32[1056]{0:T(1024)S(1)} %get-tuple-element.35, bf16[1,12,104,1056]{3,2,1,0:T(8,128)(2,1)S(1)} %fusion.75, f32[1056]{0:T(1024)S(1)} %get-tuple-element.36, f32[1056]{0:T(1024)S(1)} %get-tuple-element.37, bf16[1,2,100,1056]{3,2,1,0:T(8,128)(2,1)S(1)} %collective-permute-done.1, ...), kind=kLoop, calls=%fused_computation.278 | loop fusion | flops 70117344 | bytes 39815424 | tf_op jit(solution)/shard_map/reduce_sum | solution.py:110
  70.0 13.4 psum.56
  85.0 4.5 multiply_convert_fusion.3
  89.5 2.9 reshape.441
  92.4 2.3 fusion.83
  94.7 8.8 multiply_reduce_fusion
  103.5 16.2 %psum.57 = f32[1,5504]{1,0:T(1,128)S(1)} all-reduce(f32[1,5504]{1,0:T(1,128)S(1)} %reduce_sum.288), channel_id=1, replica_groups=mesh['pipe'=2,'replica'=32,'space'=4] {'space'}, use_global_device_ids=true, to_apply=%region_3.4 | all-reduce | flops 5504 | bytes 44032 | tf_op jit(solution)/shard_map/psum | solution.py:122
  119.8 4.1 fusion.4
  124.5 2.1 collective-permute-done.2
  127.9 1.3 multiply_reduce_fusion.3
  129.2 4.1 fusion.87
  133.3 10.4 fusion.84
  143.7 2.6 fusion.91
  146.3 3.5 reshape.444
  149.8 4.5 multiply_reduce_fusion.1
  154.8 7.7 psum.58
  162.5 1.3 fusion.157
  163.9 1.0 fusion.90
  164.9 1.1 convolution_reduce_fusion
  166.1 15.4 fusion.68
  181.5 1.1 fusion.159
  182.6 5.0 collective-permute-start.3
  187.6 1.6 collective-permute-start.4
  189.3 8.1 fusion.66
  197.5 0.8 stack.115
  211.1 0.8 multiply_select_fusion.1
  213.5 0.8 broadcast_in_dim.19
  214.3 0.8 broadcast_in_dim.21
  215.3 3.2 convolution_bitcast_fusion
  218.5 3.6 select_maximum_fusion
  222.3 15.8 %fusion.70 = bf16[1,8,100,1056]{3,2,1,0:T(8,128)(2,1)} fusion(f32[1,8,100,1056]{3,2,1,0:T(8,128)S(1)} %copy-done.6, bf16[1,8,100,1056]{3,2,1,0:T(8,128)(2,1)S(1)} %copy-done.5, bf16[1,2,100,1056]{3,2,1,0:T(8,128)(2,1)} %collective-permute-done.3, bf16[1,2,100,1056]{3,2,1,0:T(8,128)(2,1)} %collective-permute-done.4, ...), kind=kLoop, calls=%fused_computation.132 | loop fusion | flops 73497600 | bytes 41500800 | tf_op jit(solution)/shard_map/convert_element_type | solution.py:177
  238.1 2.9 reshape.446
  241.0 3.2 convolution_bitcast_fusion.1
  244.2 1307.1 %all-reduce.5.cloned.1.call-done = (f32[1,176,1056]{2,1,0:T(8,128)}, f32[1,5,5,1056]{3,0,2,1:T(1,128)}, f32[1,1056,44]{1,0,2:T(1,128)}, f32[1,44,1056]{2,0,1:T(1,128)}, f32[1,1056,176]{1,2,0:T(8,128)}) async-done(((f32[1,176,1056]{2,1,0:T(8,128)}, f32[1,5,5,1056]{3,0,2,1:T(1,128)}, f32[1,1056,44]{1,0,2:T(1,128)}, f32[1,44,1056]{2,0,1:T(1,128)}, f32[1,1056,176]{1,2,0:T(8,128)}), (f32[1,176,1056]{2,1,0:T(8,128)}, ...) | async-done | bytes 1964176 | tf_op jit(solution)/shard_map/psum | solution.py:181
  1551.4 2.1 copy.24
  1553.4 1.6 copy.25
  1555.0 1.6 copy.26
  1556.6 1.6 copy.27
  1558.3 2.1 copy.28
  (167 shorter events, 18.7 us)
Async XLA Ops:
  7.2 87.5 %copy-start = (bf16[1,176,5504]{2,1,0:T(8,128)(2,1)S(1)}, bf16[1,176,5504]{2,1,0:T(8,128)(2,1)}, u32[]{:S(2)}) copy-start(bf16[1,176,5504]{2,1,0:T(8,128)(2,1)} %param.14) | copy-start | bytes 5812228
  7.2 1544.2 %all-reduce.5.cloned.1.call-start = ((), (), s32[]{:S(2)}) async-start(), calls=%async_computation | async-start | bytes 4285440 | tf_op jit(solution)/shard_map/psum | solution.py:181
  15.8 15.1 copy-start.10
  22.4 26.2 %collective-permute-start.1 = (bf16[1,2,100,1056]{3,2,1,0:T(8,128)(2,1)}, bf16[1,2,100,1056]{3,2,1,0:T(8,128)(2,1)S(1)}, u32[]{:S(2)}, u32[]{:S(2)}) collective-permute-start(bf16[1,2,100,1056]{3,2,1,0:T(8,128)(2,1)} %get-tuple-element.76), channel_id=1, source_target_pairs={{1,0},{2,1},{3,2},{5,4},{6,5},{7,6},{9,8},{10,9},{11,10},{13,12},{... | collective-permute-start | bytes 1267208 | tf_op jit(solution)/shard_map/ppermute | solution.py:20
  23.7 24.9 %collective-permute-start = (bf16[1,2,100,1056]{3,2,1,0:T(8,128)(2,1)}, bf16[1,2,100,1056]{3,2,1,0:T(8,128)(2,1)}, u32[]{:S(2)}, u32[]{:S(2)}) collective-permute-start(bf16[1,2,100,1056]{3,2,1,0:T(8,128)(2,1)} %get-tuple-element.75), channel_id=1, source_target_pairs={{0,1},{1,2},{2,3},{4,5},{5,6},{6,7},{8,9},{9,10},{10,11},{12,13},{... | collective-permute-start | bytes 1267208 | tf_op jit(solution)/shard_map/ppermute | solution.py:19
  30.9 38.8 %copy-start.13 = (f32[1056]{0:T(1024)}, f32[1056]{0:T(1024)S(1)}, u32[]{:S(2)}) copy-start(f32[1056]{0:T(1024)S(1)} %get-tuple-element.58) | copy-start | bytes 12676
  31.2 38.6 %copy-start.15 = (f32[1056]{0:T(1024)}, f32[1056]{0:T(1024)S(1)}, u32[]{:S(2)}) copy-start(f32[1056]{0:T(1024)S(1)} %get-tuple-element.34) | copy-start | bytes 12676
  31.2 38.6 %copy-start.17 = (f32[1056]{0:T(1024)}, f32[1056]{0:T(1024)S(1)}, u32[]{:S(2)}) copy-start(f32[1056]{0:T(1024)S(1)} %get-tuple-element.35) | copy-start | bytes 12676
  31.2 38.6 %copy-start.19 = (f32[1056]{0:T(1024)}, f32[1056]{0:T(1024)S(1)}, u32[]{:S(2)}) copy-start(f32[1056]{0:T(1024)S(1)} %get-tuple-element.36) | copy-start | bytes 12676
  31.2 38.6 %copy-start.21 = (f32[1056]{0:T(1024)}, f32[1056]{0:T(1024)S(1)}, u32[]{:S(2)}) copy-start(f32[1056]{0:T(1024)S(1)} %get-tuple-element.37) | copy-start | bytes 12676
  31.2 38.6 %copy-start.23 = (f32[1056]{0:T(1024)}, f32[1056]{0:T(1024)S(1)}, u32[]{:S(2)}) copy-start(f32[1056]{0:T(1024)S(1)} %get-tuple-element.38) | copy-start | bytes 12676
  31.2 38.6 %copy-start.25 = (f32[1056]{0:T(1024)}, f32[1056]{0:T(1024)S(1)}, u32[]{:S(2)}) copy-start(f32[1056]{0:T(1024)S(1)} %get-tuple-element.39) | copy-start | bytes 12676
  31.3 38.6 %copy-start.27 = (f32[1056]{0:T(1024)}, f32[1056]{0:T(1024)S(1)}, u32[]{:S(2)}) copy-start(f32[1056]{0:T(1024)S(1)} %get-tuple-element.40) | copy-start | bytes 12676
  31.3 38.6 %copy-start.29 = (f32[1056]{0:T(1024)}, f32[1056]{0:T(1024)S(1)}, u32[]{:S(2)}) copy-start(f32[1056]{0:T(1024)S(1)} %get-tuple-element.41) | copy-start | bytes 12676
  31.3 38.6 %copy-start.31 = (f32[1056]{0:T(1024)}, f32[1056]{0:T(1024)S(1)}, u32[]{:S(2)}) copy-start(f32[1056]{0:T(1024)S(1)} %get-tuple-element.42) | copy-start | bytes 12676
  31.3 38.6 %copy-start.33 = (f32[1056]{0:T(1024)}, f32[1056]{0:T(1024)S(1)}, u32[]{:S(2)}) copy-start(f32[1056]{0:T(1024)S(1)} %get-tuple-element.43) | copy-start | bytes 12676
  31.3 38.6 %copy-start.35 = (f32[1056]{0:T(1024)}, f32[1056]{0:T(1024)S(1)}, u32[]{:S(2)}) copy-start(f32[1056]{0:T(1024)S(1)} %get-tuple-element.44) | copy-start | bytes 12676
  31.3 38.6 %copy-start.37 = (f32[1056]{0:T(1024)}, f32[1056]{0:T(1024)S(1)}, u32[]{:S(2)}) copy-start(f32[1056]{0:T(1024)S(1)} %get-tuple-element.45) | copy-start | bytes 12676
  31.3 38.6 %copy-start.39 = (f32[1056]{0:T(1024)}, f32[1056]{0:T(1024)S(1)}, u32[]{:S(2)}) copy-start(f32[1056]{0:T(1024)S(1)} %get-tuple-element.46) | copy-start | bytes 12676
  31.3 38.6 %copy-start.41 = (f32[1056]{0:T(1024)}, f32[1056]{0:T(1024)S(1)}, u32[]{:S(2)}) copy-start(f32[1056]{0:T(1024)S(1)} %get-tuple-element.47) | copy-start | bytes 12676
  31.3 38.6 %copy-start.43 = (f32[1056]{0:T(1024)}, f32[1056]{0:T(1024)S(1)}, u32[]{:S(2)}) copy-start(f32[1056]{0:T(1024)S(1)} %get-tuple-element.48) | copy-start | bytes 12676
  31.3 38.6 %copy-start.45 = (f32[1056]{0:T(1024)}, f32[1056]{0:T(1024)S(1)}, u32[]{:S(2)}) copy-start(f32[1056]{0:T(1024)S(1)} %get-tuple-element.49) | copy-start | bytes 12676
  31.4 38.6 %copy-start.47 = (f32[1056]{0:T(1024)}, f32[1056]{0:T(1024)S(1)}, u32[]{:S(2)}) copy-start(f32[1056]{0:T(1024)S(1)} %get-tuple-element.50) | copy-start | bytes 12676
  31.4 38.6 %copy-start.49 = (f32[1056]{0:T(1024)}, f32[1056]{0:T(1024)S(1)}, u32[]{:S(2)}) copy-start(f32[1056]{0:T(1024)S(1)} %get-tuple-element.51) | copy-start | bytes 12676
  31.4 38.6 %copy-start.51 = (f32[1056]{0:T(1024)}, f32[1056]{0:T(1024)S(1)}, u32[]{:S(2)}) copy-start(f32[1056]{0:T(1024)S(1)} %get-tuple-element.52) | copy-start | bytes 12676
  48.6 21.4 %copy-start.7 = (bf16[1,2,100,1056]{3,2,1,0:T(8,128)(2,1)}, bf16[1,2,100,1056]{3,2,1,0:T(8,128)(2,1)S(1)}, u32[]{:S(2)}) copy-start(bf16[1,2,100,1056]{3,2,1,0:T(8,128)(2,1)S(1)} %collective-permute-done.1) | copy-start | bytes 1267204
  52.7 17.3 %copy-start.2 = (bf16[1,12,104,1056]{3,2,1,0:T(8,128)(2,1)}, bf16[1,12,104,1056]{3,2,1,0:T(8,128)(2,1)S(1)}, u32[]{:S(2)}) copy-start(bf16[1,12,104,1056]{3,2,1,0:T(8,128)(2,1)S(1)} %fusion.75) | copy-start | bytes 7907332
  52.7 30.8 %copy-start.12 = (bf16[1,1056,44]{1,2,0:T(8,128)(2,1)S(1)}, bf16[1,1056,44]{1,2,0:T(8,128)(2,1)}, u32[]{:S(2)}) copy-start(bf16[1,1056,44]{1,2,0:T(8,128)(2,1)} %param.11) | copy-start | bytes 278788
  52.7 31.5 %copy-start.11 = (bf16[1,44,1056]{2,1,0:T(8,128)(2,1)S(1)}, bf16[1,44,1056]{2,1,0:T(8,128)(2,1)}, u32[]{:S(2)}) copy-start(bf16[1,44,1056]{2,1,0:T(8,128)(2,1)} %param.12) | copy-start | bytes 278788
  84.2 8.2 copy-start.55
  85.0 7.4 copy-start.9
  123.9 2.7 collective-permute-start.2
  149.8 16.3 %copy-start.3 = (bf16[1,12,104,1056]{3,2,1,0:T(8,128)(2,1)S(1)}, bf16[1,12,104,1056]{3,2,1,0:T(8,128)(2,1)}, u32[]{:S(2)}) copy-start(bf16[1,12,104,1056]{3,2,1,0:T(8,128)(2,1)} %copy-done.2) | copy-start | bytes 7907332
  164.9 16.6 %copy-start.54 = (f32[44]{0:T(128)}, f32[44]{0:T(128)S(1)}, u32[]{:S(2)}) copy-start(f32[44]{0:T(128)S(1)} %fusion.90) | copy-start | bytes 532
  166.1 23.2 %copy-start.8 = (bf16[1,2,100,1056]{3,2,1,0:T(8,128)(2,1)S(1)}, bf16[1,2,100,1056]{3,2,1,0:T(8,128)(2,1)}, u32[]{:S(2)}) copy-start(bf16[1,2,100,1056]{3,2,1,0:T(8,128)(2,1)} %copy-done.7) | copy-start | bytes 1267204
  181.5 15.9 %copy-start.4 = (bf16[1,8,100,1056]{3,2,1,0:T(8,128)(2,1)}, bf16[1,8,100,1056]{3,2,1,0:T(8,128)(2,1)S(1)}, u32[]{:S(2)}) copy-start(bf16[1,8,100,1056]{3,2,1,0:T(8,128)(2,1)S(1)} %get-tuple-element.66) | copy-start | bytes 5068804
  182.6 35.9 %collective-permute-start.3 = (bf16[1,2,100,1056]{3,2,1,0:T(8,128)(2,1)}, bf16[1,2,100,1056]{3,2,1,0:T(8,128)(2,1)}, u32[]{:S(2)}, u32[]{:S(2)}) collective-permute-start(bf16[1,2,100,1056]{3,2,1,0:T(8,128)(2,1)} %get-tuple-element.74), channel_id=1, source_target_pairs={{0,1},{1,2},{2,3},{4,5},{5,6},{6,7},{8,9},{9,10},{10,11},{12,13},{... | collective-permute-start | bytes 1267208 | tf_op jit(solution)/shard_map/ppermute | solution.py:19
  187.6 23.3 %copy-start.53 = (f32[1056]{0:T(1024)S(1)}, f32[1056]{0:T(1024)}, u32[]{:S(2)}) copy-start(f32[1056]{0:T(1024)} %get-tuple-element.5) | copy-start | bytes 12676
  187.6 30.9 %collective-permute-start.4 = (bf16[1,2,100,1056]{3,2,1,0:T(8,128)(2,1)}, bf16[1,2,100,1056]{3,2,1,0:T(8,128)(2,1)}, u32[]{:S(2)}, u32[]{:S(2)}) collective-permute-start(bf16[1,2,100,1056]{3,2,1,0:T(8,128)(2,1)} %get-tuple-element.73), channel_id=1, source_target_pairs={{1,0},{2,1},{3,2},{5,4},{6,5},{7,6},{9,8},{10,9},{11,10},{13,12},{... | collective-permute-start | bytes 1267208 | tf_op jit(solution)/shard_map/ppermute | solution.py:20
  197.4 21.1 %copy-start.5 = (bf16[1,8,100,1056]{3,2,1,0:T(8,128)(2,1)S(1)}, bf16[1,8,100,1056]{3,2,1,0:T(8,128)(2,1)}, u32[]{:S(2)}) copy-start(bf16[1,8,100,1056]{3,2,1,0:T(8,128)(2,1)} %copy-done.4) | copy-start | bytes 5068804
  215.1 7.0 copy-start.20
  215.2 7.0 copy-start.22
  215.2 7.0 copy-start.24
  215.2 7.0 copy-start.26
  215.2 7.0 copy-start.28
  215.2 7.0 copy-start.30
  215.2 7.0 copy-start.32
  241.0 1319.3 %copy-start.1 = (bf16[1,176,5504]{2,1,0:T(8,128)(2,1)S(1)}, bf16[1,176,5504]{2,1,0:T(8,128)(2,1)}, u32[]{:S(2)}) copy-start(bf16[1,176,5504]{2,1,0:T(8,128)(2,1)} %param.14) | copy-start | bytes 5812228
  (14 other events, 98.1 us)
Sparse Core Ops, SparseCore 0:
  244.4 1306.9 all-reduce.4
where the time goes:
time: 1570 us
  waiting for transfers between devices  1330 us (85%)
  other arithmetic  83.8 us (5%)
  matrix products  45.3 us (3%)
  local copies, waits for them, and re-layouts  43.5 us (3%)
  blocking collectives  37.3 us (2%)
    psum x1, waiting for transfers between devices, shards(): lax.psum((g_expand, g_depth, g_reduce, g_excite, g_project), ('replica',...  1310 us
  transfers between devices with their start and end apart: 6, of which 3 were waited for; matrix products, arithmetic and copies ran while one was open for 2% of the time, Pallas kernels for 0%

commit v1 on v0

--- a/solution.py
+++ b/solution.py
@@ -3,6 +3,7 @@
 import jax
 import jax.numpy as jnp
 from jax import lax
+from jax.sharding import Mesh
 from jax.sharding import PartitionSpec as P
 
 loss_scale = 256.0
@@ -24,6 +25,31 @@
 
 def swapped(array, axis, stride):
     return lax.ppermute(array, axis, [(i, i ^ 1 << stride) for i in range(lax.axis_size(axis))])
+
+
+def summed(packed):
+    rows, breadth = packed.shape
+    peers = lax.axis_size("x") * lax.axis_size("y")
+    share = -(-rows // (2 * peers * 8)) * 8
+    padded = jnp.pad(packed, ((0, 2 * peers * share - rows), (0, 0)))
+    halves = padded.reshape(2, peers, share, breadth)
+    core = lax.axis_index("core")
+    swap = [(0, 1), (1, 0)]
+    mine = lax.dynamic_index_in_dim(halves, core, 0, False)
+    other = lax.dynamic_index_in_dim(halves, 1 - core, 0, False)
+    half = mine + lax.ppermute(other, "core", swap)
+    pieces = lax.all_to_all(half, ("x", "y"), 0, 0, tiled=True)
+    piece = jnp.sum(pieces, axis=0)
+    for step in (1, 2):
+        piece = piece + lax.ppermute(
+            piece, "space", [(i, i ^ step) for i in range(lax.axis_size("space"))]
+        )
+    copies = jnp.broadcast_to(piece[None], pieces.shape)
+    gathered = lax.all_to_all(copies, ("x", "y"), 0, 0, tiled=True)
+    remote = lax.ppermute(gathered, "core", swap)
+    first = jnp.where(core == 0, gathered, remote)
+    second = jnp.where(core == 0, remote, gathered)
+    return jnp.concatenate([first, second]).reshape(2 * peers * share, breadth)[:rows]
 
 
 def swish_act(value):
@@ -178,15 +204,40 @@
     g_expand = jnp.einsum(
         "mc,me->ce", flat_view, grad_expand.reshape(-1, hidden), preferred_element_type=jnp.float32
     )
-    g_expand, g_depth, g_reduce, g_excite, g_project = lax.psum(
-        (g_expand, g_depth, g_reduce, g_excite, g_project), ("replica", "space")
-    )
-    return (g_expand[None], g_depth[None], g_reduce[None], g_excite[None], g_project[None])
+    packed = jnp.concatenate(
+        [
+            g_expand,
+            g_depth.reshape(extent * extent, hidden),
+            g_reduce.T,
+            g_excite,
+            g_project.T,
+        ]
+    )
+    marks = [0]
+    for rows in (channels, extent * extent, reduce_w.shape[1], reduce_w.shape[1], channels):
+        marks.append(marks[-1] + rows)
+    total = summed(packed)
+    parts = [total[start:stop] for start, stop in zip(marks, marks[1:])]
+    return (
+        parts[0][None],
+        parts[1].reshape(1, extent, extent, hidden),
+        parts[2].T[None],
+        parts[3][None],
+        parts[4].T[None],
+    )
 
 
 def solution(mesh):
+    pipe, replica, space = (mesh.shape[name] for name in ("pipe", "replica", "space"))
+    side = 1
+    while 2 * side * side < replica:
+        side *= 2
+    fine = Mesh(
+        mesh.devices.reshape(pipe, replica // (2 * side), side, 2, space),
+        ("pipe", "x", "y", "core", "space"),
+    )
     in_specs = (
-        P("pipe", "replica", "space", None, None),
+        P("pipe", ("x", "y", "core"), "space", None, None),
         P("pipe", None, None),
         P("pipe", None, None, None),
         P("pipe", None, None),
@@ -202,4 +253,4 @@
         P("pipe", None, None),
         P("pipe", None, None),
     )
-    return jax.shard_map(shards, mesh=mesh, in_specs=in_specs, out_specs=out_specs, check_vma=False)
+    return jax.shard_map(shards, mesh=fine, in_specs=in_specs, out_specs=out_specs, check_vma=False)

time: 1570 us -> 316 us (0.20)
  waiting for transfers between devices: 1330 us -> 37.5 us
  blocking collectives: 37.3 us -> 78.9 us
  starting transfers between devices: 15.1 us -> 35 us
    psum x1 -> x0, waiting for transfers between devices: 1310 us -> none  [shards(): lax.psum((g_expand, g_depth, g_reduce, g_excite, g_project), ('replica',...]
    all_to_all x0 -> x2, blocking collectives: none -> 41.6 us  [the longest x1 24.1 us: summed(): pieces = lax.all_to_all(half, ('x', 'y'), 0, 0, tiled=True)]
    ppermute x0 -> x4, starting transfers between devices: none -> 20 us  [the longest x1 11.6 us: summed(): half = mine + lax.ppermute(other, 'core', swap)]
  transfers between devices with their start and end apart: 6 -> 9, of which waited for: 3 -> 7; matrix products, arithmetic and copies ran while one was open for 2% -> 3% of each run, Pallas kernels for 0% -> 0%
where the time goes in v1:
time: 316 us; the launch traced here: 315 us
  other arithmetic  84.1 us (27%)
  blocking collectives  78.9 us (25%)
  matrix products  40.9 us (13%)
  waiting for transfers between devices  37.5 us (12%)
  local copies, waits for them, and re-layouts  36.2 us (11%)
  starting transfers between devices  35 us (11%)
    all_to_all x1, blocking collectives, summed(): pieces = lax.all_to_all(half, ('x', 'y'), 0, 0, tiled=True)  24.1 us
    reduce_sum x2, other arithmetic, kernel_grad(): jnp.sum(grad_wide * padded[..., step_y:step_y + height, step_x:step_x + b...  22.3 us
    ppermute x2, waiting for transfers between devices, with_halo(): after = lax.ppermute(first, axis, down)  21.1 us
    all_to_all x1, blocking collectives, summed(): gathered = lax.all_to_all(copies, ('x', 'y'), 0, 0, tiled=True)  17.4 us
    reduce_sum x1, other arithmetic, shards(): squeeze = lax.psum(jnp.sum(act_depth, axis=(1, 2)), 'space') / cell_total  17.1 us
    psum x1, blocking collectives, shards(): pooled = (lax.psum(head_sum, 'space') / cell_total).astype(jnp.bfloat16)  16.2 us
    convert_element_type x1, other arithmetic, shards(): grad_expand = (grad_expanded * swish_slope(pre_expand)).astype(jnp.bfloat16)  15.8 us
    psum x1, blocking collectives, shards(): squeeze = lax.psum(jnp.sum(act_depth, axis=(1, 2)), 'space') / cell_total  13.4 us
  transfers between devices with their start and end apart: 9, of which 7 were waited for; matrix products, arithmetic and copies ran while one was open for 3% of the time, Pallas kernels for 0%

profile of v1, /device:TPU:1, one launch (start us, length us, event | category | flops | bytes accessed | tf_op | source)
XLA Modules:
  0.0 314.8 jit_solution(9992613754461332582)
XLA Ops:
  2.2 3.6 %fusion.94 = f32[800,1056]{1,0:T(8,128)} fusion(bf16[800,176]{0,1:T(8,128)(2,1)S(1)} %reshape_squeeze.3, bf16[1,176,1056]{2,1,0:T(8,128)(2,1)} %param.9), kind=kOutput, calls=%fused_computation.178 | convolution fusion | flops 297369600 | bytes 4032512 | tf_op jit(solution)/shard_map/dot_general | solution.py:128
  5.7 3.5 %reshape.454 = f32[1,8,100,1056]{3,2,1,0:T(8,128)} reshape(f32[800,1056]{1,0:T(8,128)} %fusion.94) | data formatting | bytes 6758400 | tf_op jit(solution)/shard_map/reshape | solution.py:128
  9.2 4.4 %multiply_convert_fusion.4 = bf16[1,8,100,1056]{3,2,1,0:T(8,128)(2,1)} fusion(f32[1,8,100,1056]{3,2,1,0:T(8,128)} %reshape.454), kind=kLoop, calls=%fused_computation.130 | loop fusion | flops 4224000 | bytes 5068800 | tf_op jit(solution)/shard_map/convert_element_type | solution.py:131
  13.7 2.2 fusion.161
  15.8 1.3 collective-permute-start.1
  17.1 7.1 %collective-permute-start = (bf16[1,2,100,1056]{3,2,1,0:T(8,128)(2,1)}, bf16[1,2,100,1056]{3,2,1,0:T(8,128)(2,1)}, u32[]{:S(2)}, u32[]{:S(2)}) collective-permute-start(bf16[1,2,100,1056]{3,2,1,0:T(8,128)(2,1)} %get-tuple-element.74), channel_id=1, source_target_pairs={{0,1},{1,2},{2,3},{4,5},{5,6},{6,7},{8,9},{9,10},{10,11},{12,13},{... | collective-permute-start | bytes 1267208 | tf_op jit(solution)/shard_map/ppermute | solution.py:20
  24.7 17.3 %collective-permute-done.1 = bf16[1,2,100,1056]{3,2,1,0:T(8,128)(2,1)S(1)} collective-permute-done((bf16[1,2,100,1056]{3,2,1,0:T(8,128)(2,1)}, bf16[1,2,100,1056]{3,2,1,0:T(8,128)(2,1)S(1)}, u32[]{:S(2)}, u32[]{:S(2)}) %collective-permute-start.1) | collective-permute-done | bytes 422432 | tf_op jit(solution)/shard_map/ppermute | solution.py:21
  42.0 4.0 %fusion.75 = bf16[1,12,104,1056]{3,2,1,0:T(8,128)(2,1)S(1)} fusion(bf16[1,2,100,1056]{3,2,1,0:T(8,128)(2,1)S(1)} %collective-permute-done.1, bf16[1,8,100,1056]{3,2,1,0:T(8,128)(2,1)} %multiply_convert_fusion.4, bf16[1,2,100,1056]{3,2,1,0:T(8,128)(2,1)} %collective-permute-done), kind=kLoop, calls=%fused_computation.139 | loop fusion | flops 15814656 | bytes 5170176 | tf_op jit(solution)/shard_map/concatenate | solution.py:22
  46.1 17.1 %fusion.156 = (f32[1056]{0:T(1024)S(1)}, f32[1,8,100,1056]{3,2,1,0:T(8,128)}) fusion(f32[1056]{0:T(1024)S(1)} %get-tuple-element.35, bf16[1,12,104,1056]{3,2,1,0:T(8,128)(2,1)S(1)} %fusion.75, f32[1056]{0:T(1024)S(1)} %get-tuple-element.36, f32[1056]{0:T(1024)S(1)} %get-tuple-element.37, bf16[1,2,100,1056]{3,2,1,0:T(8,128)(2,1)S(1)} %collective-permute-done.1, ...), kind=kLoop, calls=%fused_computation.284 | loop fusion | flops 70117344 | bytes 39815424 | tf_op jit(solution)/shard_map/reduce_sum | solution.py:136
  63.4 13.4 %psum.21 = f32[1,1056]{1,0:T(1,128)S(1)} all-reduce(f32[1,1056]{1,0:T(1,128)S(1)} %reduce_sum.295), channel_id=1, replica_groups=mesh['pipe'=2,'x'=4,'y'=4,'core'=2,'space'=4] {'space'}, use_global_device_ids=true, to_apply=%region_1.2 | all-reduce | flops 1056 | bytes 8448 | tf_op jit(solution)/shard_map/psum | solution.py:136
  78.9 4.5 %multiply_convert_fusion.3 = bf16[1,8,100,1056]{3,2,1,0:T(8,128)(2,1)} fusion(f32[1056]{0:T(1024)S(1)} %get-tuple-element.76, f32[1,8,100,1056]{3,2,1,0:T(8,128)} %get-tuple-element.67), kind=kLoop, calls=%fused_computation.127 | loop fusion | flops 5068800 | bytes 5073024 | tf_op jit(solution)/shard_map/convert_element_type | solution.py:140
  83.3 2.9 reshape.456
  86.2 2.3 fusion.83
  88.5 8.8 %multiply_reduce_fusion = (f32[5504]{0:T(1024)S(1)}, f32[800,5504]{1,0:T(8,128)}) fusion(bf16[800,176]{0,1:T(8,128)(2,1)S(1)} %fusion.83, bf16[1,176,5504]{2,1,0:T(8,128)(2,1)S(1)} %copy-done), kind=kOutput, calls=%fused_computation.27 | convolution fusion | flops 1571936896 | bytes 19853824 | tf_op jit(solution)/shard_map/dot_general | solution.py:146
  97.4 16.2 %psum.22 = f32[1,5504]{1,0:T(1,128)S(1)} all-reduce(f32[1,5504]{1,0:T(1,128)S(1)} %reduce_sum.297), channel_id=1, replica_groups=mesh['pipe'=2,'x'=4,'y'=4,'core'=2,'space'=4] {'space'}, use_global_device_ids=true, to_apply=%region_3.4 | all-reduce | flops 5504 | bytes 44032 | tf_op jit(solution)/shard_map/psum | solution.py:148
  113.7 4.1 %fusion.4 = f32[1,500]{1,0:T(1,128)S(1)} fusion(bf16[1,5504,500]{1,2,0:T(8,128)(2,1)} %param.15, f32[1,5504]{1,0:T(1,128)S(1)} %psum.22), kind=kOutput, calls=%fused_computation.35 | convolution fusion | flops 5515008 | bytes 5528016 | tf_op jit(solution)/shard_map/dot_general | solution.py:149
  118.4 2.1 collective-permute-done.2
  121.8 1.3 multiply_reduce_fusion.3
  123.1 4.1 %fusion.87 = f32[5504]{0:T(1024)S(1)} fusion(bf16[1,5504,500]{1,2,0:T(8,128)(2,1)} %param.15, pred[]{:T(512)S(6)} %eq.11, f32[1,500]{1,0:T(1,128)S(1)} %get-tuple-element.63, f32[1,500]{1,0:T(1,128)S(1)} %get-tuple-element.65, f32[]{:T(128)} %get-tuple-element.62, f32[]{:T(128)S(6)} %log.4), kind=kOutput, calls=%fused_computation.166 | convolution fusion | flops 5508000 | bytes 5530025 | tf_op jit(solution)/shard_map/ik,fk->if/dot_general | solution.py:163
  127.2 10.4 %fusion.84 = bf16[800,176]{0,1:T(8,128)(2,1)S(1)} fusion(bf16[1,176,5504]{2,1,0:T(8,128)(2,1)S(1)} %copy-done, f32[800,5504]{1,0:T(8,128)} %get-tuple-element.80, f32[5504]{0:T(1024)S(1)} %broadcast_multiply_fusion), kind=kOutput, calls=%fused_computation.163 | convolution fusion | flops 1589696000 | bytes 19853824 | tf_op jit(solution)/shard_map/mf,cf->mc/dot_general | solution.py:173
  137.6 2.6 fusion.91
  140.2 1.5 fusion.162
  141.7 3.5 %reshape.459 = f32[1,8,100,1056]{3,2,1,0:T(8,128)} reshape(f32[800,1056]{1,0:T(8,128)} %fusion.91) | data formatting | bytes 6758400 | tf_op jit(solution)/shard_map/reshape | solution.py:179
  145.2 4.5 %multiply_reduce_fusion.1 = f32[1056]{0:T(1024)S(1)} fusion(f32[1,8,100,1056]{3,2,1,0:T(8,128)} %reshape.459, f32[1,8,100,1056]{3,2,1,0:T(8,128)} %get-tuple-element.67), kind=kLoop, calls=%fused_computation.126 | loop fusion | flops 5067744 | bytes 6762624 | tf_op jit(solution)/shard_map/reduce_sum | solution.py:180
  150.3 7.7 %psum.23 = f32[1,1056]{1,0:T(1,128)} all-reduce(f32[1,1056]{1,0:T(1,128)} %reduce_sum.302), channel_id=1, replica_groups=mesh['pipe'=2,'x'=4,'y'=4,'core'=2,'space'=4] {'space'}, use_global_device_ids=true, to_apply=%region_8.9 | all-reduce | flops 1056 | bytes 8448 | tf_op jit(solution)/shard_map/psum | solution.py:180
  157.9 1.3 fusion.157
  160.4 14.8 %fusion.68 = (f32[1056]{0:T(1024)S(1)}, f32[1056]{0:T(1024)S(1)}, f32[1056]{0:T(1024)S(1)}, f32[1056]{0:T(1024)S(1)}, f32[1056]{0:T(1024)S(1)}, /*index=5*/f32[1...) fusion(bf16[1,12,104,1056]{3,2,1,0:T(8,128)(2,1)S(1)} %copy-don, ...), kind=kLoop, calls=%fused_computation.124 | loop fusion | flops 55737792 | bytes 38945280 | tf_op jit(solution)/shard_map/reduce_sum | solution.py:97
  176.3 5.0 %collective-permute-start.3 = (bf16[1,2,100,1056]{3,2,1,0:T(8,128)(2,1)}, bf16[1,2,100,1056]{3,2,1,0:T(8,128)(2,1)}, u32[]{:S(2)}, u32[]{:S(2)}) collective-permute-start(bf16[1,2,100,1056]{3,2,1,0:T(8,128)(2,1)} %get-tuple-element.73), channel_id=1, source_target_pairs={{0,1},{1,2},{2,3},{4,5},{5,6},{6,7},{8,9},{9,10},{10,11},{12,13},{... | collective-permute-start | bytes 1267208 | tf_op jit(solution)/shard_map/ppermute | solution.py:20
  181.4 1.5 collective-permute-start.4
  182.9 7.5 %fusion.66 = (f32[1056]{0:T(1024)S(1)}, f32[1056]{0:T(1024)S(1)}, f32[1056]{0:T(1024)S(1)}, f32[1056]{0:T(1024)S(1)}, f32[1056]{0:T(1024)S(1)}, /*index=5*/f32[1056]{0:T(1024)S(1)}, f32[1056]{0:T(1024)S(1)}) fusion(bf16[1,8,100,1056]{3,2,1,0:T(8,128)(2,1)S(1)} %get-tuple-element.61, bf16[1,2,100,1056]{3,2,1,0:T(8,128)(2,1)S(1)} %copy-done.9, ...), kind=kLoop, calls=%fused_computation.122 | loop fusion | flops 21957408 | bytes 7632768 | tf_op jit(solution)/shard_map/reduce_sum | solution.py:97
  192.8 3.8 %collective-permute-done.4 = bf16[1,2,100,1056]{3,2,1,0:T(8,128)(2,1)} collective-permute-done((bf16[1,2,100,1056]{3,2,1,0:T(8,128)(2,1)}, bf16[1,2,100,1056]{3,2,1,0:T(8,128)(2,1)}, u32[]{:S(2)}, u32[]{:S(2)}) %collective-permute-start.4) | collective-permute-done | bytes 422432 | tf_op jit(solution)/shard_map/ppermute | solution.py:21
  196.6 3.9 %select_maximum_fusion = bf16[1,12,104,1056]{3,2,1,0:T(8,128)(2,1)S(1)} fusion(bf16[1,2,100,1056]{3,2,1,0:T(8,128)(2,1)} %collective-permute-done.4, bf16[1,8,100,1056]{3,2,1,0:T(8,128)(2,1)} %copy-done.4, bf16[1,2,100,1056]{3,2,1,0:T(8,128)(2,1)} %collective-permute-done.3), kind=kLoop, calls=%fused_computation.133 | loop fusion | flops 15814656 | bytes 5170176 | tf_op jit(solution)/shard_map/concatenate | solution.py:22
  200.6 15.8 %fusion.70 = bf16[1,8,100,1056]{3,2,1,0:T(8,128)(2,1)} fusion(f32[1,8,100,1056]{3,2,1,0:T(8,128)S(1)} %copy-done.6, bf16[1,8,100,1056]{3,2,1,0:T(8,128)(2,1)S(1)} %copy-done.5, bf16[1,2,100,1056]{3,2,1,0:T(8,128)(2,1)} %collective-permute-done.3, bf16[1,2,100,1056]{3,2,1,0:T(8,128)(2,1)} %collective-permute-done.4, ...), kind=kLoop, calls=%fused_computation.132 | loop fusion | flops 73497600 | bytes 41500800 | tf_op jit(solution)/shard_map/convert_element_type | solution.py:203
  216.4 2.0 reshape.461
  218.5 1.5 convolution_bitcast_fusion
  220.0 10.8 %concatenate.34 = f32[465,1056]{1,0:T(8,128)} concatenate(f32[176,1056]{1,0:T(8,128)} %convolution_bitcast_fusion, f32[25,1056]{1,0:T(8,128)} %reshape.462, f32[44,1056]{1,0:T(8,128)S(1)} %get-tuple-element.84, f32[44,1056]{1,0:T(8,128)S(1)} %get-tuple-element.83, f32[176,1056]{1,0:T(8,128)S(1)} %copy-done.10), dimensions={0} | concatenate | bytes 3928320 | tf_op jit(solution)/shard_map/concatenate | solution.py:207
  230.9 1.8 pad.13
  232.7 11.6 %collective-permute-start.5 = (f32[16,16,1056]{2,1,0:T(8,128)S(1)}, f32[16,16,1056]{2,1,0:T(8,128)}, u32[]{:S(2)}, u32[]{:S(2)}) collective-permute-start(f32[16,16,1056]{2,1,0:T(8,128)S(1)} %dynamic-slice_bitcast_fusion), channel_id=1, source_target_pairs={{0,4},{4,0},{1,5},{5,1},{2,6},{6,2},{3,7},{7,3},{8,12},{12,8},{9,1... | collective-permute-start | bytes 3244040 | tf_op jit(solution)/shard_map/ppermute | solution.py:40
  244.4 2.6 collective-permute-done.5
  247.0 1.4 bitcast_add_fusion
  248.4 24.1 %all_to_all.10 = f32[16,16,1056]{2,1,0:T(8,128)S(1)} all-to-all(f32[16,16,1056]{2,1,0:T(8,128)S(1)} %bitcast_add_fusion), channel_id=1, replica_groups=mesh['pipe'=2,'x'=4,'y'=4,'core'=2,'space'=4] {'x','y'}, dimensions={0} | all-to-all | bytes 2162688 | tf_op jit(solution)/shard_map/all_to_all | solution.py:41
  272.6 1.6 collective-permute-start.6
  274.1 3.4 %collective-permute-done.6 = f32[16,1056]{1,0:T(8,128)S(1)} collective-permute-done((f32[16,1056]{1,0:T(8,128)S(1)}, f32[16,1056]{1,0:T(8,128)S(1)}, u32[]{:S(2)}, u32[]{:S(2)}) %collective-permute-start.6) | collective-permute-done | bytes 67616 | tf_op jit(solution)/shard_map/ppermute | solution.py:44
  277.6 1.5 collective-permute-start.7
  279.1 5.8 %collective-permute-done.7 = f32[16,1056]{1,0:T(8,128)S(1)} collective-permute-done((f32[16,1056]{1,0:T(8,128)S(1)}, f32[16,1056]{1,0:T(8,128)S(1)}, u32[]{:S(2)}, u32[]{:S(2)}) %collective-permute-start.7) | collective-permute-done | bytes 67616 | tf_op jit(solution)/shard_map/ppermute | solution.py:44
  285.0 17.4 %all_to_all.11 = f32[16,16,1056]{2,1,0:T(8,128)S(1)} all-to-all(f32[16,16,1056]{2,1,0:T(8,128)S(1)} %broadcast_in_dim.15), channel_id=1, replica_groups=mesh['pipe'=2,'x'=4,'y'=4,'core'=2,'space'=4] {'x','y'}, dimensions={0} | all-to-all | bytes 2162688 | tf_op jit(solution)/shard_map/all_to_all | solution.py:48
  302.4 5.3 %collective-permute-start.8 = (f32[16,16,1056]{2,1,0:T(8,128)S(1)}, f32[16,16,1056]{2,1,0:T(8,128)S(1)}, u32[]{:S(2)}, u32[]{:S(2)}) collective-permute-start(f32[16,16,1056]{2,1,0:T(8,128)S(1)} %all_to_all.11), channel_id=1, source_target_pairs={{0,4},{4,0},{1,5},{5,1},{2,6},{6,2},{3,7},{7,3},{8,12},{12,8},{9,1... | collective-permute-start | bytes 3244040 | tf_op jit(solution)/shard_map/ppermute | solution.py:49
  307.7 2.5 collective-permute-done.8
  (139 shorter events, 15.0 us)
Async XLA Ops:
  0.6 87.9 %copy-start = (bf16[1,176,5504]{2,1,0:T(8,128)(2,1)S(1)}, bf16[1,176,5504]{2,1,0:T(8,128)(2,1)}, u32[]{:S(2)}) copy-start(bf16[1,176,5504]{2,1,0:T(8,128)(2,1)} %param.14) | copy-start | bytes 5812228
  9.2 15.1 %copy-start.12 = (bf16[1,5,5,1056]{3,2,1,0:T(8,128)(2,1)S(1)}, bf16[1,5,5,1056]{3,2,1,0:T(8,128)(2,1)}, u32[]{:S(2)}) copy-start(bf16[1,5,5,1056]{3,2,1,0:T(8,128)(2,1)} %param.10) | copy-start | bytes 158404
  15.8 26.2 %collective-permute-start.1 = (bf16[1,2,100,1056]{3,2,1,0:T(8,128)(2,1)}, bf16[1,2,100,1056]{3,2,1,0:T(8,128)(2,1)S(1)}, u32[]{:S(2)}, u32[]{:S(2)}) collective-permute-start(bf16[1,2,100,1056]{3,2,1,0:T(8,128)(2,1)} %get-tuple-element.75), channel_id=1, source_target_pairs={{1,0},{2,1},{3,2},{5,4},{6,5},{7,6},{9,8},{10,9},{11,10},{13,12},{... | collective-permute-start | bytes 1267208 | tf_op jit(solution)/shard_map/ppermute | solution.py:21
  17.1 24.9 %collective-permute-start = (bf16[1,2,100,1056]{3,2,1,0:T(8,128)(2,1)}, bf16[1,2,100,1056]{3,2,1,0:T(8,128)(2,1)}, u32[]{:S(2)}, u32[]{:S(2)}) collective-permute-start(bf16[1,2,100,1056]{3,2,1,0:T(8,128)(2,1)} %get-tuple-element.74), channel_id=1, source_target_pairs={{0,1},{1,2},{2,3},{4,5},{5,6},{6,7},{8,9},{9,10},{10,11},{12,13},{... | collective-permute-start | bytes 1267208 | tf_op jit(solution)/shard_map/ppermute | solution.py:20
  24.6 38.6 %copy-start.15 = (f32[1056]{0:T(1024)}, f32[1056]{0:T(1024)S(1)}, u32[]{:S(2)}) copy-start(f32[1056]{0:T(1024)S(1)} %get-tuple-element.44) | copy-start | bytes 12676
  24.6 38.6 %copy-start.17 = (f32[1056]{0:T(1024)}, f32[1056]{0:T(1024)S(1)}, u32[]{:S(2)}) copy-start(f32[1056]{0:T(1024)S(1)} %get-tuple-element.45) | copy-start | bytes 12676
  24.6 38.6 %copy-start.19 = (f32[1056]{0:T(1024)}, f32[1056]{0:T(1024)S(1)}, u32[]{:S(2)}) copy-start(f32[1056]{0:T(1024)S(1)} %get-tuple-element.46) | copy-start | bytes 12676
  24.6 38.6 %copy-start.21 = (f32[1056]{0:T(1024)}, f32[1056]{0:T(1024)S(1)}, u32[]{:S(2)}) copy-start(f32[1056]{0:T(1024)S(1)} %get-tuple-element.47) | copy-start | bytes 12676
  24.7 38.6 %copy-start.23 = (f32[1056]{0:T(1024)}, f32[1056]{0:T(1024)S(1)}, u32[]{:S(2)}) copy-start(f32[1056]{0:T(1024)S(1)} %get-tuple-element.48) | copy-start | bytes 12676
  24.7 38.6 %copy-start.25 = (f32[1056]{0:T(1024)}, f32[1056]{0:T(1024)S(1)}, u32[]{:S(2)}) copy-start(f32[1056]{0:T(1024)S(1)} %get-tuple-element.49) | copy-start | bytes 12676
  24.7 38.6 %copy-start.27 = (f32[1056]{0:T(1024)}, f32[1056]{0:T(1024)S(1)}, u32[]{:S(2)}) copy-start(f32[1056]{0:T(1024)S(1)} %get-tuple-element.50) | copy-start | bytes 12676
  24.7 38.6 %copy-start.29 = (f32[1056]{0:T(1024)}, f32[1056]{0:T(1024)S(1)}, u32[]{:S(2)}) copy-start(f32[1056]{0:T(1024)S(1)} %get-tuple-element.51) | copy-start | bytes 12676
  24.7 38.6 %copy-start.31 = (f32[1056]{0:T(1024)}, f32[1056]{0:T(1024)S(1)}, u32[]{:S(2)}) copy-start(f32[1056]{0:T(1024)S(1)} %get-tuple-element.52) | copy-start | bytes 12676
  42.0 21.3 %copy-start.8 = (bf16[1,2,100,1056]{3,2,1,0:T(8,128)(2,1)}, bf16[1,2,100,1056]{3,2,1,0:T(8,128)(2,1)S(1)}, u32[]{:S(2)}) copy-start(bf16[1,2,100,1056]{3,2,1,0:T(8,128)(2,1)S(1)} %collective-permute-done.1) | copy-start | bytes 1267204
  46.1 17.2 %copy-start.2 = (bf16[1,12,104,1056]{3,2,1,0:T(8,128)(2,1)}, bf16[1,12,104,1056]{3,2,1,0:T(8,128)(2,1)S(1)}, u32[]{:S(2)}) copy-start(bf16[1,12,104,1056]{3,2,1,0:T(8,128)(2,1)S(1)} %fusion.75) | copy-start | bytes 7907332
  46.1 30.7 %copy-start.14 = (bf16[1,1056,44]{1,2,0:T(8,128)(2,1)S(1)}, bf16[1,1056,44]{1,2,0:T(8,128)(2,1)}, u32[]{:S(2)}) copy-start(bf16[1,1056,44]{1,2,0:T(8,128)(2,1)} %param.11) | copy-start | bytes 278788
  46.1 31.9 %copy-start.13 = (bf16[1,44,1056]{2,1,0:T(8,128)(2,1)S(1)}, bf16[1,44,1056]{2,1,0:T(8,128)(2,1)}, u32[]{:S(2)}) copy-start(bf16[1,44,1056]{2,1,0:T(8,128)(2,1)} %param.12) | copy-start | bytes 278788
  77.5 0.5 copy-start.33
  78.9 7.4 %copy-start.11 = (bf16[1,1056,176]{1,2,0:T(8,128)(2,1)S(1)}, bf16[1,1056,176]{1,2,0:T(8,128)(2,1)}, u32[]{:S(2)}) copy-start(bf16[1,1056,176]{1,2,0:T(8,128)(2,1)} %param.13) | copy-start | bytes 1115140
  117.8 2.7 collective-permute-start.2
  137.6 2.6 copy-start.7
  145.2 15.1 %copy-start.3 = (bf16[1,12,104,1056]{3,2,1,0:T(8,128)(2,1)S(1)}, bf16[1,12,104,1056]{3,2,1,0:T(8,128)(2,1)}, u32[]{:S(2)}) copy-start(bf16[1,12,104,1056]{3,2,1,0:T(8,128)(2,1)} %copy-done.2) | copy-start | bytes 7907332
  160.3 22.5 %copy-start.9 = (bf16[1,2,100,1056]{3,2,1,0:T(8,128)(2,1)S(1)}, bf16[1,2,100,1056]{3,2,1,0:T(8,128)(2,1)}, u32[]{:S(2)}) copy-start(bf16[1,2,100,1056]{3,2,1,0:T(8,128)(2,1)} %copy-done.8) | copy-start | bytes 1267204
  175.2 15.2 %copy-start.4 = (bf16[1,8,100,1056]{3,2,1,0:T(8,128)(2,1)}, bf16[1,8,100,1056]{3,2,1,0:T(8,128)(2,1)S(1)}, u32[]{:S(2)}) copy-start(bf16[1,8,100,1056]{3,2,1,0:T(8,128)(2,1)S(1)} %get-tuple-element.61) | copy-start | bytes 5068804
  176.3 16.5 %collective-permute-start.3 = (bf16[1,2,100,1056]{3,2,1,0:T(8,128)(2,1)}, bf16[1,2,100,1056]{3,2,1,0:T(8,128)(2,1)}, u32[]{:S(2)}, u32[]{:S(2)}) collective-permute-start(bf16[1,2,100,1056]{3,2,1,0:T(8,128)(2,1)} %get-tuple-element.73), channel_id=1, source_target_pairs={{0,1},{1,2},{2,3},{4,5},{5,6},{6,7},{8,9},{9,10},{10,11},{12,13},{... | collective-permute-start | bytes 1267208 | tf_op jit(solution)/shard_map/ppermute | solution.py:20
  181.4 15.2 %collective-permute-start.4 = (bf16[1,2,100,1056]{3,2,1,0:T(8,128)(2,1)}, bf16[1,2,100,1056]{3,2,1,0:T(8,128)(2,1)}, u32[]{:S(2)}, u32[]{:S(2)}) collective-permute-start(bf16[1,2,100,1056]{3,2,1,0:T(8,128)(2,1)} %get-tuple-element.72), channel_id=1, source_target_pairs={{1,0},{2,1},{3,2},{5,4},{6,5},{7,6},{9,8},{10,9},{11,10},{13,12},{... | collective-permute-start | bytes 1267208 | tf_op jit(solution)/shard_map/ppermute | solution.py:21
  190.4 10.1 %copy-start.16 = (f32[1056]{0:T(1024)S(1)}, f32[1056]{0:T(1024)}, u32[]{:S(2)}) copy-start(f32[1056]{0:T(1024)} %copy-done.15) | copy-start | bytes 12676
  190.4 10.1 %copy-start.18 = (f32[1056]{0:T(1024)S(1)}, f32[1056]{0:T(1024)}, u32[]{:S(2)}) copy-start(f32[1056]{0:T(1024)} %copy-done.17) | copy-start | bytes 12676
  190.4 10.1 %copy-start.20 = (f32[1056]{0:T(1024)S(1)}, f32[1056]{0:T(1024)}, u32[]{:S(2)}) copy-start(f32[1056]{0:T(1024)} %copy-done.19) | copy-start | bytes 12676
  190.4 10.1 %copy-start.22 = (f32[1056]{0:T(1024)S(1)}, f32[1056]{0:T(1024)}, u32[]{:S(2)}) copy-start(f32[1056]{0:T(1024)} %copy-done.21) | copy-start | bytes 12676
  190.4 10.1 %copy-start.24 = (f32[1056]{0:T(1024)S(1)}, f32[1056]{0:T(1024)}, u32[]{:S(2)}) copy-start(f32[1056]{0:T(1024)} %copy-done.23) | copy-start | bytes 12676
  190.4 10.1 %copy-start.26 = (f32[1056]{0:T(1024)S(1)}, f32[1056]{0:T(1024)}, u32[]{:S(2)}) copy-start(f32[1056]{0:T(1024)} %copy-done.25) | copy-start | bytes 12676
  190.4 10.1 %copy-start.28 = (f32[1056]{0:T(1024)S(1)}, f32[1056]{0:T(1024)}, u32[]{:S(2)}) copy-start(f32[1056]{0:T(1024)} %copy-done.27) | copy-start | bytes 12676
  190.4 10.1 %copy-start.30 = (f32[1056]{0:T(1024)S(1)}, f32[1056]{0:T(1024)}, u32[]{:S(2)}) copy-start(f32[1056]{0:T(1024)} %copy-done.29) | copy-start | bytes 12676
  190.5 10.1 %copy-start.32 = (f32[1056]{0:T(1024)S(1)}, f32[1056]{0:T(1024)}, u32[]{:S(2)}) copy-start(f32[1056]{0:T(1024)} %copy-done.31) | copy-start | bytes 12676
  190.5 10.1 %copy-start.5 = (bf16[1,8,100,1056]{3,2,1,0:T(8,128)(2,1)S(1)}, bf16[1,8,100,1056]{3,2,1,0:T(8,128)(2,1)}, u32[]{:S(2)}) copy-start(bf16[1,8,100,1056]{3,2,1,0:T(8,128)(2,1)} %copy-done.4) | copy-start | bytes 5068804
  191.8 8.8 %copy-start.6 = (f32[1,8,100,1056]{3,2,1,0:T(8,128)S(1)}, f32[1,8,100,1056]{3,2,1,0:T(8,128)}, u32[]{:S(2)}) copy-start(f32[1,8,100,1056]{3,2,1,0:T(8,128)} %reshape.454) | copy-start | bytes 10137604
  216.4 3.6 %copy-start.10 = (f32[176,1056]{1,0:T(8,128)S(1)}, f32[176,1056]{1,0:T(8,128)}, u32[]{:S(2)}) copy-start(f32[176,1056]{1,0:T(8,128)} %fusion.162) | copy-start | bytes 2230276
  232.7 14.2 %collective-permute-start.5 = (f32[16,16,1056]{2,1,0:T(8,128)S(1)}, f32[16,16,1056]{2,1,0:T(8,128)}, u32[]{:S(2)}, u32[]{:S(2)}) collective-permute-start(f32[16,16,1056]{2,1,0:T(8,128)S(1)} %dynamic-slice_bitcast_fusion), channel_id=1, source_target_pairs={{0,4},{4,0},{1,5},{5,1},{2,6},{6,2},{3,7},{7,3},{8,12},{12,8},{9,1... | collective-permute-start | bytes 3244040 | tf_op jit(solution)/shard_map/ppermute | solution.py:40
  272.6 5.0 %collective-permute-start.6 = (f32[16,1056]{1,0:T(8,128)S(1)}, f32[16,1056]{1,0:T(8,128)S(1)}, u32[]{:S(2)}, u32[]{:S(2)}) collective-permute-start(f32[16,1056]{1,0:T(8,128)S(1)} %reduce_sum.328), channel_id=1, source_target_pairs={{0,1},{1,0},{2,3},{3,2},{4,5},{5,4},{6,7},{7,6},{8,9},{9,8},{10,11... | collective-permute-start | bytes 202760 | tf_op jit(solution)/shard_map/ppermute | solution.py:44
  277.6 7.3 %collective-permute-start.7 = (f32[16,1056]{1,0:T(8,128)S(1)}, f32[16,1056]{1,0:T(8,128)S(1)}, u32[]{:S(2)}, u32[]{:S(2)}) collective-permute-start(f32[16,1056]{1,0:T(8,128)S(1)} %add.317), channel_id=1, source_target_pairs={{0,2},{1,3},{2,0},{3,1},{4,6},{5,7},{6,4},{7,5},{8,10},{9,11},{10,... | collective-permute-start | bytes 202760 | tf_op jit(solution)/shard_map/ppermute | solution.py:44
  302.4 7.8 %collective-permute-start.8 = (f32[16,16,1056]{2,1,0:T(8,128)S(1)}, f32[16,16,1056]{2,1,0:T(8,128)S(1)}, u32[]{:S(2)}, u32[]{:S(2)}) collective-permute-start(f32[16,16,1056]{2,1,0:T(8,128)S(1)} %all_to_all.11), channel_id=1, source_target_pairs={{0,4},{4,0},{1,5},{5,1},{2,6},{6,2},{3,7},{7,3},{8,12},{12,8},{9,1... | collective-permute-start | bytes 3244040 | tf_op jit(solution)/shard_map/ppermute | solution.py:49
  311.3 3.6 %copy-start.1 = (bf16[1,176,5504]{2,1,0:T(8,128)(2,1)S(1)}, bf16[1,176,5504]{2,1,0:T(8,128)(2,1)}, u32[]{:S(2)}) copy-start(bf16[1,176,5504]{2,1,0:T(8,128)(2,1)} %param.14) | copy-start | bytes 5812228

commit v2 on v0

v2 whole, which is shorter than its diff:
```python
import jax
import jax.numpy as jnp
from jax import lax
from jax.experimental import pallas as pl
from jax.experimental.pallas import tpu as pltpu
from jax.sharding import Mesh
from jax.sharding import PartitionSpec as P

loss_scale = 256.0
f32 = jnp.float32
bf16 = jnp.bfloat16
LANES = 128
BAND = 384
HEAD_CHUNK = 512
STRIP = 20
VMEM = pl.BlockSpec(memory_space=pltpu.VMEM)
SMEM = pl.BlockSpec(memory_space=pltpu.SMEM)
ANY = pl.BlockSpec(memory_space=pl.ANY)


def up_to(size, multiple):
    return -(-size // multiple) * multiple


def params(**extra):
    return pltpu.CompilerParams(vmem_limit_bytes=50 * 1024 * 1024, **extra)


def contract(left, right, left_dim, right_dim):
    return lax.dot_general(
        left, right, (((left_dim,), (right_dim,)), ((), ())), preferred_element_type=f32
    )


def row_window(own, rim, extent, place):
    margin = extent // 2
    window = []
    for i in range(extent):
        d = i - margin
        if d == 0:
            window.append(own)
        elif d > 0:
            window.append(pltpu.roll(jnp.where(place < d, rim, own), 8 - d, 0))
        else:
            window.append(pltpu.roll(jnp.where(place >= 8 + d, rim, own), -d, 0))
    return window


def forward_kernel(
    own_ref, before_ref, after_ref, expand_ref, depth_ref,
    cells_ref, cells_t_ref, mine_ref, half_ref, squeeze_ref,
    left, right, expanded,
):
    columns, channels = own_ref.shape[1:]
    extent, margin = 5, 2

    @pl.when(pl.program_id(0) == 0)
    def lay_out():
        left[...] = jnp.zeros_like(left)
        right[...] = jnp.zeros_like(right)
        rest = channels - LANES
        for ref, first, base in ((own_ref, 0, 0), (after_ref, 0, 8), (before_ref, 0, 14)):
            for y in range(ref.shape[0]):
                row = ref[y].astype(f32)
                left[pl.ds(base + y, columns, stride=16), :] = row[:, :LANES]
                right[pl.ds(base + y, columns, stride=16), :] = jnp.concatenate(
                    [row[:, LANES:], jnp.zeros((columns, LANES - rest), f32)], axis=1
                )
        low, high = left[...], right[...]
        cells_ref[:, :LANES] = low.astype(bf16)
        cells_ref[:, LANES:] = high[:, :rest].astype(bf16)
        for start in range(0, 16 * columns, 320):
            cells_t_ref[:LANES, start : start + 320] = left[start : start + 320, :].T.astype(bf16)
            cells_t_ref[LANES:, start : start + 320] = right[start : start + 320, :].T[
                :rest
            ].astype(bf16)
        mine_ref[:, :LANES] = (
            low.reshape(columns, 16, LANES)[:, :8].reshape(8 * columns, LANES).astype(bf16)
        )
        mine_ref[:, LANES:] = (
            high.reshape(columns, 16, LANES)[:, :8]
            .reshape(8 * columns, LANES)[:, :rest]
            .astype(bf16)
        )
        edge = jnp.zeros((margin, 16, BAND), f32)
        expanded[:margin] = edge
        expanded[margin + columns :] = edge

    @pl.loop(0, columns // 10)
    def expand(part):
        cells = cells_ref[pl.ds(pl.multiple_of(part * 160, 160), 160), :]
        half = jnp.dot(cells, expand_ref[...], preferred_element_type=f32)
        value = half + half * jnp.tanh(half)
        expanded[pl.ds(margin + part * 10, 10)] = value.reshape(10, 16, BAND)

    place = lax.broadcasted_iota(jnp.int32, (8, LANES), 0)

    @pl.loop(0, BAND // LANES)
    def convolve(tile):
        lanes = pl.ds(pl.multiple_of(tile * LANES, LANES), LANES)
        weight = [
            [depth_ref[i * extent + j : i * extent + j + 1, lanes] for j in range(extent)]
            for i in range(extent)
        ]

        def strip(number, total):
            x0 = number * STRIP
            sums = {}
            for k in range(STRIP + extent - 1):
                window = row_window(
                    expanded[x0 + k, :8, lanes], expanded[x0 + k, 8:, lanes], extent, place
                )
                for j in range(extent):
                    x = k - j
                    if 0 <= x < STRIP:
                        term = window[0] * weight[0][j]
                        for i in range(1, extent):
                            term = term + window[i] * weight[i][j]
                        sums[x] = term if x not in sums else sums[x] + term
                x = k - extent + 1
                if x >= 0:
                    half = 0.5 * sums.pop(x)
                    half_ref[pl.ds(pl.multiple_of((x0 + x) * 8, 8), 8), lanes] = half
                    total = total + (half + half * jnp.tanh(half))
            return total

        total = lax.fori_loop(0, columns // STRIP, strip, jnp.zeros((8, LANES), f32))
        squeeze_ref[:, lanes] = jnp.sum(total, axis=0, keepdims=True)


def gate_of(squeeze, reduce_t, excite):
    reduced_in = jnp.sum(reduce_t * squeeze, axis=1, keepdims=True)
    reduced = reduced_in * jax.nn.sigmoid(reduced_in)
    gate = jax.nn.sigmoid(jnp.sum(excite * reduced, axis=0, keepdims=True))
    return reduced_in, reduced, gate


def head_kernel(
    half_ref, squeeze_ref, reduce_ref, excite_ref, project_ref, mine_ref, head_ref, class_ref,
    logits_ref, gated_ref, block_ref,
    gate_row, head_w, class_w, sums, sems,
):
    cells = half_ref.shape[0]
    width = head_ref.shape[1]
    classes = class_ref.shape[1]
    head_copy = pltpu.make_async_copy(head_ref, head_w.at[:, :width], sems.at[0])
    class_copy = pltpu.make_async_copy(class_ref, class_w, sems.at[1])
    head_copy.start()
    class_copy.start()
    head_w[:, width:] = jnp.zeros((head_w.shape[0], head_w.shape[1] - width), bf16)
    cell_total = 4 * cells
    gate_row[...] = gate_of(squeeze_ref[...] / cell_total, reduce_ref[...], excite_ref[...])[2]

    @pl.loop(0, cells // 80)
    def gating(part):
        rows = pl.ds(pl.multiple_of(part * 80, 80), 80)
        half = half_ref[rows, :]
        gated_ref[rows, :] = ((half + half * jnp.tanh(half)) * gate_row[...]).astype(bf16)

    residual = contract(gated_ref[...], project_ref[...], 1, 1)
    block = (mine_ref[...].astype(f32) + residual).astype(bf16)
    block_ref[...] = (0.5 * block.astype(f32)).astype(bf16)
    head_copy.wait()

    @pl.loop(0, head_w.shape[1] // HEAD_CHUNK)
    def head(part):
        lanes = pl.ds(pl.multiple_of(part * HEAD_CHUNK, HEAD_CHUNK), HEAD_CHUNK)
        half = jnp.dot(block_ref[...], head_w[:, lanes], preferred_element_type=f32)
        act = half + half * jnp.tanh(half)
        sums[:, lanes] = jnp.sum(act.reshape(cells // 8, 8, HEAD_CHUNK), axis=0)

    class_copy.wait()
    pooled = sums[:, :width]
    high = pooled.astype(bf16).astype(f32)
    both = jnp.concatenate([high, pooled - high], axis=0).astype(bf16)
    partial = jnp.sum(
        jnp.dot(both, class_w[...], preferred_element_type=f32), axis=0, keepdims=True
    )
    logits_ref[...] = jnp.zeros_like(logits_ref)
    logits_ref[:, :classes] = jnp.broadcast_to(
        partial / cell_total, (logits_ref.shape[0], classes)
    )


def head_grad_kernel(
    which_ref, logits_ref, block_ref, gated_ref, project_ref, head_ref, class_ref,
    grad_ref, project_grad_ref, gate_grad_ref,
    head_w, class_w, pooled, total, sems,
):
    cells = block_ref.shape[0]
    width = head_ref.shape[1]
    classes = class_ref.shape[1]
    head_copy = pltpu.make_async_copy(head_ref, head_w.at[:, :width], sems.at[0])
    class_copy = pltpu.make_async_copy(class_ref, class_w, sems.at[1])
    class_copy.start()
    head_copy.start()
    head_w[:, width:] = jnp.zeros((head_w.shape[0], head_w.shape[1] - width), bf16)
    total[...] = jnp.zeros_like(total)

    rows = logits_ref[...]
    network = lax.broadcasted_iota(jnp.int32, rows.shape, 0) % 2
    valid = lax.broadcasted_iota(jnp.int32, (1, rows.shape[1]), 1) < classes
    teacher = jnp.sum(jnp.where(network == 0, rows, 0.0), axis=0, keepdims=True)
    student = jnp.sum(jnp.where(network == 1, rows, 0.0), axis=0, keepdims=True)
    exp_teacher = jnp.where(valid, jnp.exp(teacher), 0.0)
    prob = exp_teacher / jnp.sum(exp_teacher, axis=1, keepdims=True)
    log_sum = jnp.log(
        jnp.sum(jnp.where(valid, jnp.exp(student), 0.0), axis=1, keepdims=True)
    )
    logprob = student - log_sum
    cross = jnp.sum(prob * logprob, axis=1, keepdims=True)
    teacher_grad = loss_scale * prob * (cross - logprob)
    student_grad = loss_scale * (jnp.exp(logprob) - prob)
    grad = jnp.where(which_ref[0] == 0, teacher_grad, student_grad)
    grad = jnp.where(valid, grad, 0.0)
    grad = jnp.broadcast_to(grad, (16, rows.shape[1])).astype(bf16)[:, :classes]
    class_copy.wait()
    pooled[:, :width] = contract(grad, class_w[...], 1, 1)[:1] * (0.5 / (4 * cells))
    pooled[:, width:] = jnp.zeros((1, pooled.shape[1] - width), f32)
    head_copy.wait()

    @pl.loop(0, head_w.shape[1] // HEAD_CHUNK)
    def head(part):
        lanes = pl.ds(pl.multiple_of(part * HEAD_CHUNK, HEAD_CHUNK), HEAD_CHUNK)
        weight = head_w[:, lanes]
        half = jnp.dot(block_ref[...], weight, preferred_element_type=f32)
        t = jnp.tanh(half)
        slope = (1.0 + t) * (1.0 + (half - half * t))
        grad_head = (slope * pooled[:, lanes]).astype(bf16)
        total[...] += contract(grad_head, weight, 1, 1)

    grad_block = total[...]
    grad_ref[...] = grad_block.astype(bf16)
    project_grad = jnp.dot(grad_block.T.astype(bf16), gated_ref[...], preferred_element_type=f32)
    project_grad_ref[...] = project_grad
    gate_grad_ref[...] = jnp.sum(
        project_ref[...].astype(f32) * project_grad, axis=0, keepdims=True
    )


def backward_kernel(
    space_ref, gate_grad_ref, squeeze_ref, reduce_ref, excite_ref, cells_ref, cells_t_ref,
    expand_ref, depth_ref, half_ref, grad_ref, project_ref, project_grad_ref,
    out_ref,
    gate_row, pool_row, excite_grad, reduce_grad, expanded, slope, grad_depth, grad_expand,
):
    step = pl.program_id(0)
    cells = half_ref.shape[0]
    columns = cells // 8
    channels = grad_ref.shape[1]
    reduced_rows = reduce_ref.shape[0]
    extent, margin = 5, 2
    cell_total = 4 * cells

    @pl.when(step == 0)
    def gates():
        squeeze = squeeze_ref[...] / cell_total
        reduced_in, reduced, gate = gate_of(squeeze, reduce_ref[...], excite_ref[...])
        grad_excite = (1.0 - gate) * gate_grad_ref[...]
        sigma = jax.nn.sigmoid(reduced_in)
        grad_reduced = jnp.sum(excite_ref[...] * grad_excite, axis=1, keepdims=True) * (
            sigma * (1.0 + reduced_in * (1.0 - sigma))
        )
        back_pool = jnp.sum(reduce_ref[...] * grad_reduced, axis=0, keepdims=True)
        gate_row[...] = 0.5 * gate
        pool_row[...] = back_pool * (0.5 / cell_total)
        once = jnp.where(space_ref[0] == 0, 1.0, 0.0)
        excite_grad[...] = reduced * (grad_excite * once)
        reduce_grad[...] = grad_reduced * (squeeze * once)
        edge = jnp.zeros((margin, 16, BAND), f32)
        expanded[:margin] = edge
        expanded[margin + columns :] = edge
        grad_depth[:margin] = edge[:, :8]
        grad_depth[margin + columns :] = edge[:, :8]

    band = pl.ds(pl.multiple_of(step * BAND, LANES), BAND)
    gate = gate_row[:, band]
    back_pool = pool_row[:, band]

    @pl.loop(0, columns // 10)
    def elements(part):
        rows = pl.ds(pl.multiple_of(part * 160, 160), 160)
        half = jnp.dot(cells_ref[rows, :], expand_ref[...], preferred_element_type=f32)
        t = jnp.tanh(half)
        turn = half * t
        expanded[pl.ds(margin + part * 10, 10)] = (half + turn).reshape(10, 16, BAND)
        slope[pl.ds(part * 10, 10)] = ((1.0 + t) * (1.0 + (half - turn))).reshape(10, 16, BAND)
        rows = pl.ds(pl.multiple_of(part * 80, 80), 80)
        grad_gated = jnp.dot(grad_ref[rows, :], project_ref[...], preferred_element_type=f32)
        half = half_ref[rows, :]
        t = jnp.tanh(half)
        value = (grad_gated * gate + back_pool) * ((1.0 + t) * (1.0 + (half - half * t)))
        grad_depth[pl.ds(margin + part * 10, 10)] = value.reshape(10, 8, BAND)

    place = lax.broadcasted_iota(jnp.int32, (8, LANES), 0)

    depth_base = 2 * channels
    excite_base = depth_base + up_to(extent * extent, 8)
    reduce_base = excite_base + reduced_rows
    out_ref[excite_base:reduce_base, :] = excite_grad[:, band]
    out_ref[reduce_base : reduce_base + reduced_rows, :] = reduce_grad[:, band]
    out_ref[channels:depth_base, :] = project_grad_ref[...]
    spare = out_ref.shape[0] - reduce_base - reduced_rows
    out_ref[reduce_base + reduced_rows :, :] = jnp.zeros((spare, BAND), f32)

    @pl.loop(0, BAND // LANES)
    def convolve(tile):
        lanes = pl.ds(pl.multiple_of(tile * LANES, LANES), LANES)

        def taps(number, sums):
            sums = [list(line) for line in sums]
            base = margin + number * 10
            grads = {}
            for k in range(10):
                window = row_window(
                    expanded[base + k, :8, lanes], expanded[base + k, 8:, lanes], extent, place
                )
                for j in range(extent):
                    place_x = k - j
                    if place_x not in grads:
                        grads[place_x] = grad_depth[base + place_x + margin, :, lanes]
                    for i in range(extent):
                        sums[i][j] = sums[i][j] + window[i] * grads[place_x]
            return tuple(tuple(line) for line in sums)

        zero = jnp.zeros((8, LANES), f32)
        sums = lax.fori_loop(0, columns // 10, taps, ((zero,) * extent,) * extent)
        for i in range(extent):
            for j in range(extent):
                row = depth_base + i * extent + j
                out_ref[row : row + 1, lanes] = jnp.sum(sums[i][j], axis=0, keepdims=True)
        for row in range(depth_base + extent * extent, excite_base):
            out_ref[row : row + 1, lanes] = jnp.zeros((1, LANES), f32)

        weight = [
            [0.5 * depth_ref[i * extent + j : i * extent + j + 1, lanes] for j in range(extent)]
            for i in range(extent)
        ]

        @pl.loop(0, columns // STRIP)
        def spread(number):
            x0 = number * STRIP
            grads = [grad_depth[x0 + k, :, lanes] for k in range(extent - 1)]
            for x in range(STRIP):
                grads.append(grad_depth[x0 + x + extent - 1, :, lanes])
                near, far = None, None
                for i in range(extent):
                    term = grads[x + extent - 1] * weight[i][0]
                    for j in range(1, extent):
                        term = term + grads[x + extent - 1 - j] * weight[i][j]
                    d = i - margin
                    if d == 0:
                        near = term if near is None else near + term
                        continue
                    rolled = pltpu.roll(term, d % 8, 0)
                    inside = place >= d if d > 0 else place < 8 + d
                    stay = jnp.where(inside, rolled, 0.0)
                    leave = jnp.where(inside, 0.0, rolled)
                    near = stay if near is None else near + stay
                    far = leave if far is None else far + leave
                near = near * slope[x0 + x, :8, lanes]
                far = far * slope[x0 + x, 8:, lanes]
                rows = pl.ds(pl.multiple_of((x0 + x) * 16, 16), 16)
                grad_expand[rows, lanes] = jnp.concatenate([near, far], axis=0).astype(bf16)

    out_ref[:channels, :] = jnp.dot(
        cells_t_ref[...], grad_expand[...], preferred_element_type=f32
    )


def unpack_kernel(
    core_ref, own_ref, other_ref, expand_ref, depth_ref, reduce_ref, excite_ref, project_ref
):
    channels, hidden = expand_ref.shape[1:]
    extent = depth_ref.shape[1]
    reduced = excite_ref.shape[1]
    depth_base = 2 * channels
    excite_base = depth_base + up_to(extent * extent, 8)
    reduce_base = excite_base + up_to(reduced, 8)
    half_rows = own_ref.shape[0]

    def rows(start, stop):
        pieces = []
        if start < half_rows:
            end = min(stop, half_rows)
            pieces.append(
                jnp.where(core_ref[0] == 0, own_ref[start:end, :], other_ref[start:end, :])
            )
        if stop > half_rows:
            begin = max(start, half_rows)
            pieces.append(
                jnp.where(
                    core_ref[0] == 0,
                    other_ref[begin - half_rows : stop - half_rows, :],
                    own_ref[begin - half_rows : stop - half_rows, :],
                )
            )
        return pieces[0] if len(pieces) == 1 else jnp.concatenate(pieces, axis=0)

    expand_ref[0] = rows(0, channels)[:, :hidden]
    project_ref[0] = rows(channels, depth_base).T[:hidden]
    depth = rows(depth_base, excite_base)
    for i in range(extent):
        depth_ref[0, i] = depth[i * extent : (i + 1) * extent, :hidden]
    excite_ref[0] = rows(excite_base, reduce_base)[:reduced, :hidden]
    reduce_ref[0] = rows(reduce_base, reduce_base + up_to(reduced, 8)).T[:hidden, :reduced]


def shards(views, w_expand, w_depth, w_reduce, w_excite, w_project, w_head, w_class):
    own = views[0, 0]
    height, columns, channels = own.shape
    hidden = w_expand.shape[2]
    reduced = w_reduce.shape[2]
    extent = w_depth.shape[1]
    width = w_head.shape[2]
    classes = w_class.shape[2]
    cells = height * columns
    space = lax.axis_size("space")
    broad = up_to(hidden, BAND)
    bands = broad // BAND
    tall = up_to(reduced, 8)

    up = [(i, i + 1) for i in range(space - 1)]
    down = [(i + 1, i) for i in range(space - 1)]
    before = lax.ppermute(own[height - 2 :], "space", up)
    after = lax.ppermute(own[:2], "space", down)

    fill = broad - hidden
    expand_w = jnp.pad(w_expand[0] * bf16(0.5), ((0, 0), (0, fill)))
    depth_w = jnp.pad(
        w_depth[0].reshape(extent * extent, hidden).astype(f32),
        ((0, up_to(extent * extent, 8) - extent * extent), (0, fill)),
    )
    reduce_t = jnp.pad(w_reduce[0].T.astype(f32), ((0, tall - reduced), (0, fill)))
    excite_w = jnp.pad(w_excite[0].astype(f32), ((0, tall - reduced), (0, fill)))
    project_t = jnp.pad(w_project[0].T, ((0, 0), (0, fill)))

    def whole(*shape):
        return pl.BlockSpec(shape, lambda e: (0,) * len(shape))

    def banded(rows):
        return pl.BlockSpec((rows, BAND), lambda e: (0, e))

    depth_rows = depth_w.shape[0]
    cell_rows, cells_t, mine, half, squeeze = pl.pallas_call(
        forward_kernel,
        grid=(bands,),
        in_specs=[
            whole(height, columns, channels),
            whole(2, columns, channels),
            whole(2, columns, channels),
            banded(channels),
            banded(depth_rows),
        ],
        out_specs=[
            whole(16 * columns, channels),
            whole(channels, 16 * columns),
            whole(cells, channels),
            banded(cells),
            banded(1),
        ],
        out_shape=[
            jax.ShapeDtypeStruct((16 * columns, channels), bf16),
            jax.ShapeDtypeStruct((channels, 16 * columns), bf16),
            jax.ShapeDtypeStruct((cells, channels), bf16),
            jax.ShapeDtypeStruct((cells, broad), f32),
            jax.ShapeDtypeStruct((1, broad), f32),
        ],
        scratch_shapes=[
            pltpu.VMEM((16 * columns, LANES), f32),
            pltpu.VMEM((16 * columns, LANES), f32),
            pltpu.VMEM((columns + 4, 16, BAND), f32),
        ],
        compiler_params=params(),
        name="expand_depthwise",
    )(own, before, after, expand_w, depth_w)
    squeeze = lax.psum(squeeze, "space")

    head_wide = up_to(width, HEAD_CHUNK)
    ranks = 2 * space
    logits, gated, block = pl.pallas_call(
        head_kernel,
        in_specs=[VMEM] * 6 + [ANY] * 2,
        out_specs=[VMEM] * 3,
        out_shape=[
            jax.ShapeDtypeStruct((ranks, up_to(classes, LANES)), f32),
            jax.ShapeDtypeStruct((cells, broad), bf16),
            jax.ShapeDtypeStruct((cells, channels), bf16),
        ],
        scratch_shapes=[
            pltpu.VMEM((1, broad), f32),
            pltpu.VMEM((channels, head_wide), bf16),
            pltpu.VMEM((width, classes), bf16),
            pltpu.VMEM((8, head_wide), f32),
            pltpu.SemaphoreType.DMA((2,)),
        ],
        compiler_params=params(),
        name="project_head",
    )(half, squeeze, reduce_t, excite_w, project_t, mine, w_head[0], w_class[0])
    logits = lax.all_to_all(logits, ("space", "pipe"), 0, 0, tiled=True)

    def index(name):
        return lax.axis_index(name).astype(jnp.int32).reshape(1)

    grad_block, project_grad, gate_grad = pl.pallas_call(
        head_grad_kernel,
        in_specs=[SMEM] + [VMEM] * 4 + [ANY] * 2,
        out_specs=[VMEM] * 3,
        out_shape=[
            jax.ShapeDtypeStruct((cells, channels), bf16),
            jax.ShapeDtypeStruct((channels, broad), f32),
            jax.ShapeDtypeStruct((1, broad), f32),
        ],
        scratch_shapes=[
            pltpu.VMEM((channels, head_wide), bf16),
            pltpu.VMEM((width, classes), bf16),
            pltpu.VMEM((1, head_wide), f32),
            pltpu.VMEM((cells, channels), f32),
            pltpu.SemaphoreType.DMA((2,)),
        ],
        compiler_params=params(),
        name="head_grad",
    )(index("pipe"), logits, block, gated, project_t, w_head[0], w_class[0])
    gate_grad = lax.psum(gate_grad, "space")

    peers = lax.axis_size("x") * lax.axis_size("y")
    used = 2 * channels + depth_rows + 2 * tall
    share = up_to(-(-used // (2 * peers)), 8)
    rows = 2 * peers * share
    packed = pl.pallas_call(
        backward_kernel,
        grid=(bands,),
        in_specs=[
            SMEM,
            whole(1, broad),
            whole(1, broad),
            whole(tall, broad),
            whole(tall, broad),
            whole(16 * columns, channels),
            whole(channels, 16 * columns),
            banded(channels),
            banded(depth_rows),
            banded(cells),
            whole(cells, channels),
            banded(channels),
            banded(channels),
        ],
        out_specs=banded(rows),
        out_shape=jax.ShapeDtypeStruct((rows, broad), f32),
        scratch_shapes=[
            pltpu.VMEM((1, broad), f32),
            pltpu.VMEM((1, broad), f32),
            pltpu.VMEM((tall, broad), f32),
            pltpu.VMEM((tall, broad), f32),
            pltpu.VMEM((columns + 4, 16, BAND), f32),
            pltpu.VMEM((columns, 16, BAND), f32),
            pltpu.VMEM((columns + 4, 8, BAND), f32),
            pltpu.VMEM((16 * columns, BAND), bf16),
        ],
        compiler_params=params(),
        name="depthwise_grad",
    )(
        index("space"), gate_grad, squeeze, reduce_t, excite_w, cell_rows, cells_t,
        expand_w, depth_w, half, grad_block, project_t, project_grad,
    )

    halves = packed.reshape(2, peers, share, broad)
    core = lax.axis_index("core")
    swap = [(0, 1), (1, 0)]
    keep = lax.dynamic_index_in_dim(halves, core, 0, False)
    send = lax.dynamic_index_in_dim(halves, 1 - core, 0, False)
    pieces = lax.all_to_all(
        keep + lax.ppermute(send, "core", swap), ("x", "y"), 0, 0, tiled=True
    )
    piece = jnp.sum(pieces, axis=0)
    for step in (1, 2):
        piece = piece + lax.ppermute(piece, "space", [(i, i ^ step) for i in range(space)])
    copies = jnp.broadcast_to(piece[None], pieces.shape)
    gathered = lax.all_to_all(copies, ("x", "y"), 0, 0, tiled=True)
    remote = lax.ppermute(gathered, "core", swap)
    return pl.pallas_call(
        unpack_kernel,
        in_specs=[SMEM] + [VMEM] * 2,
        out_specs=[VMEM] * 5,
        out_shape=[
            jax.ShapeDtypeStruct((1, channels, hidden), f32),
            jax.ShapeDtypeStruct((1, extent, extent, hidden), f32),
            jax.ShapeDtypeStruct((1, hidden, reduced), f32),
            jax.ShapeDtypeStruct((1, reduced, hidden), f32),
            jax.ShapeDtypeStruct((1, hidden, channels), f32),
        ],
        compiler_params=params(),
        name="unpack",
    )(index("core"), gathered.reshape(peers * share, broad), remote.reshape(peers * share, broad))


def solution(mesh):
    pipe, replica, space = (mesh.shape[name] for name in ("pipe", "replica", "space"))
    side = 1
    while 2 * side * side < replica:
        side *= 2
    fine = Mesh(
        mesh.devices.reshape(pipe, replica // (2 * side), side, 2, space),
        ("pipe", "x", "y", "core", "space"),
    )
    in_specs = (P("pipe", ("x", "y", "core"), "space"),) + (P("pipe"),) * 7
    return jax.shard_map(
        shards, mesh=fine, in_specs=in_specs, out_specs=(P("pipe"),) * 5, check_vma=False
    )
```

time: 1570 us -> 212 us (0.14)
  waiting for transfers between devices: 1330 us -> 18.4 us
  other arithmetic: 83.8 us -> 1.56 us
  Pallas kernels: 0 us -> 72.9 us
  matrix products: 45.3 us -> 0 us
  blocking collectives: 37.3 us -> 60.5 us
    psum x1 -> x0, waiting for transfers between devices: 1310 us -> none  [shards(): lax.psum((g_expand, g_depth, g_reduce, g_excite, g_project), ('replica',...]
    pallas_call x0 -> x5, Pallas kernels: none -> 72.9 us  [the longest x1 31.3 us: shards(): pl.pallas_call(backward_kernel, grid=(bands,), in_specs=[SMEM, whole(1, b...]
    reduce_sum x6 -> x1, other arithmetic: 46.9 us -> 0.06 us  [shards(): piece = jnp.sum(pieces, axis=0)]
    dot_general x13 -> x0, matrix products: 45.3 us -> none  [the longest x1 10.4 us: shards(): jnp.einsum('mf,cf->mc', grad_head, head_w, preferred_element_type=jnp.flo...]
    all_to_all x0 -> x2, blocking collectives: none -> 41.4 us  [the longest x1 24.2 us: shards(): lax.all_to_all(keep + lax.ppermute(send, 'core', swap), ('x', 'y'), 0, 0,...]
    convert_element_type x5 -> x0, other arithmetic: 25.1 us -> none  [the longest x1 15.8 us: shards(): grad_expand = (grad_expanded * swish_slope(pre_expand)).astype(jnp.bfloat16)]
    psum x3 -> x2, blocking collectives: 37.3 us -> 19 us  [the longest x1 11.7 us: shards(): squeeze = lax.psum(squeeze, 'space')]
  transfers between devices with their start and end apart: 6 -> 7, of which waited for: 3 -> 6; matrix products, arithmetic and copies ran while one was open for 2% -> 4% of each run, Pallas kernels for 0% -> 0%
where the time goes in v2:
time: 212 us; the launch traced here: 211 us
  Pallas kernels  72.9 us (34%)
  blocking collectives  60.5 us (29%)
  starting transfers between devices  29.1 us (14%)
  local copies, waits for them, and re-layouts  28.1 us (13%)
  waiting for transfers between devices  18.4 us (9%)
    pallas_call x1, Pallas kernels, shards(): pl.pallas_call(backward_kernel, grid=(bands,), in_specs=[SMEM, whole(1, b...  31.3 us
    all_to_all x1, blocking collectives, shards(): lax.all_to_all(keep + lax.ppermute(send, 'core', swap), ('x', 'y'), 0, 0,...  24.2 us
    unnamed x45, local copies, waits for them, and re-layouts  22 us
    all_to_all x1, blocking collectives, shards(): gathered = lax.all_to_all(copies, ('x', 'y'), 0, 0, tiled=True)  17.3 us
    pallas_call x1, Pallas kernels, shards(): pl.pallas_call(forward_kernel, grid=(bands,), in_specs=[whole(height, col...  16.8 us
    pallas_call x1, Pallas kernels, shards(): pl.pallas_call(head_grad_kernel, in_specs=[SMEM] + [VMEM] * 4 + [ANY] * 2...  13.5 us
    psum x1, blocking collectives, shards(): squeeze = lax.psum(squeeze, 'space')  11.7 us
    pallas_call x1, Pallas kernels, shards(): pl.pallas_call(head_kernel, in_specs=[VMEM] * 6 + [ANY] * 2, out_specs=[V...  8.61 us
  transfers between devices with their start and end apart: 7, of which 6 were waited for; matrix products, arithmetic and copies ran while one was open for 4% of the time, Pallas kernels for 0%

profile of v2, /device:TPU:1, one launch (start us, length us, event | category | flops | bytes accessed | tf_op | source)
XLA Modules:
  0.0 211.5 jit_solution(13048385223821175537)
XLA Ops:
  0.7 1.3 copy.21
  2.0 5.7 %collective-permute-start = (bf16[2,100,176]{2,1,0:T(8,128)(2,1)S(1)}, bf16[2,100,176]{2,1,0:T(8,128)(2,1)S(1)}, u32[]{:S(2)}, u32[]{:S(2)}) collective-permute-start(bf16[2,100,176]{2,1,0:T(8,128)(2,1)S(1)} %get-tuple-element.38), channel_id=1, source_target_pairs={{0,1},{1,2},{2,3},{4,5},{5,6},{6,7},{8,9},{9,10},{10,11},{12,13},{... | collective-permute-start | bytes 211208 | tf_op jit(solution)/shard_map/ppermute | solution.py:425
  7.7 1.4 collective-permute-start.1
  9.2 0.1 convert_element_type.23
  9.5 8.4 %copy.24 = bf16[1,5504,500]{2,1,0:T(8,128)(2,1)} copy(bf16[1,5504,500]{1,2,0:T(8,128)(2,1)} %param.15) | data formatting | bytes 11008000 | tf_op args[7]
  17.9 1.3 collective-permute-done.1.after_ref
  19.2 16.8 %expand_depthwise.1 = (bf16[1600,176]{1,0:T(8,128)(2,1)S(1)}, bf16[176,1600]{1,0:T(8,128)(2,1)S(1)}, bf16[800,176]{1,0:T(8,128)(2,1)S(1)}, f32[800,1152]{1,0:T(8,128)}, f32[1,1152]{1,0:T(1,128)S(1)}) custom-call(bf16[8,100,176]{2,1,0:T(8,128)(2,1)S(1)} %bitcast.31, bf16[2,100,176]{2,1,0:T(8,128)(2,1)S(1)} %collective-permute-done.before_ref, ...), custom_call_target="tpu_custom_call" | custom-call | tf_op jit(solution)/shard_map/expand_depthwise/pallas_call | solution.py:445
  36.1 0.9 copy-done.2
  37.0 0.8 copy-done.6
  37.8 0.7 copy-done.12
  38.5 11.7 %psum.14.squeeze_ref = f32[1,1152]{1,0:T(1,128)S(1)} all-reduce(f32[1,1152]{1,0:T(1,128)S(1)} %get-tuple-element.17), channel_id=1, replica_groups=mesh['pipe'=2,'x'=4,'y'=4,'core'=2,'space'=4] {'space'}, use_global_device_ids=true, to_apply=%region_0.1 | all-reduce | flops 1152 | bytes 9216 | tf_op jit(solution)/shard_map/psum | solution.py:477
  50.2 0.0 copy-start.13
  50.2 1.0 copy-done.13
  51.2 8.6 %project_head.1 = (f32[8,512]{1,0:T(8,128)S(1)}, bf16[800,1152]{1,0:T(8,128)(2,1)S(1)}, bf16[800,176]{1,0:T(8,128)(2,1)S(1)}) custom-call(f32[800,1152]{1,0:T(8,128)} %get-tuple-element.16.half_ref, f32[1,1152]{1,0:T(1,128)S(1)} %psum.14.squeeze_ref, f32[48,1152]{1,0:T(8,128)S(1)} %get-tuple-element.40.reduce_ref, ...), custom_call_target="tpu_custom_call" | custom-call | tf_op jit(solution)/shard_map/project_head/pallas_call | solution.py:481
  59.8 0.7 copy-done.8
  60.6 0.6 copy.25
  61.2 3.7 %all-to-all-start = ((f32[8,1,512]{2,1,0:T(1,128)}), f32[8,1,512]{2,1,0:T(1,128)S(1)}, u32[]{:S(2)}, u32[]{:S(2)}) async-start(f32[8,1,512]{2,1,0:T(1,128)} %copy.25), calls=%async_computation | async-start | bytes 32768 | tf_op jit(solution)/shard_map/all_to_all | solution.py:500
  64.9 6.6 %all-to-all-done = f32[8,1,512]{2,1,0:T(1,128)S(1)} async-done(((f32[8,1,512]{2,1,0:T(1,128)}), f32[8,1,512]{2,1,0:T(1,128)S(1)}, u32[]{:S(2)}, u32[]{:S(2)}) %all-to-all-start) | async-done | bytes 16416 | tf_op jit(solution)/shard_map/all_to_all | solution.py:500
  71.5 1.0 copy-done.9
  72.5 13.5 %head_grad.1 = (bf16[800,176]{1,0:T(8,128)(2,1)S(1)}, f32[176,1152]{1,0:T(8,128)S(1)}, f32[1,1152]{1,0:T(1,128)S(1)}) custom-call(s32[1]{0:T(128)} %bitcast.2.which_ref, f32[8,512]{1,0:T(8,128)S(1)} %bitcast.32, bf16[800,176]{1,0:T(8,128)(2,1)S(1)} %copy-done.9, bf16[800,1152]{1,0:T(8,128)(2,1)S(1)} %get-tuple-element.21.gated_ref, ...), custom_call_target="tpu_custom_call" | custom-call | tf_op jit(solution)/shard_map/head_grad/pallas_call | solution.py:505
  86.0 0.9 copy-done.4
  86.9 0.7 copy-done.10
  87.6 7.4 %psum.15.gate_grad_ref = f32[1,1152]{1,0:T(1,128)S(1)} all-reduce(f32[1,1152]{1,0:T(1,128)S(1)} %get-tuple-element.22), channel_id=1, replica_groups=mesh['pipe'=2,'x'=4,'y'=4,'core'=2,'space'=4] {'space'}, use_global_device_ids=true, to_apply=%region_1.2 | all-reduce | flops 1152 | bytes 9216 | tf_op jit(solution)/shard_map/psum | solution.py:524
  95.0 1.1 copy-done.3
  96.2 1.1 copy-done.5
  97.3 1.1 copy-done.7
  98.4 1.0 copy-done.11
  99.4 31.3 %depthwise_grad.1 = f32[512,1152]{1,0:T(8,128)} custom-call(s32[1]{0:T(128)} %bitcast.1.space_ref, f32[1,1152]{1,0:T(1,128)S(1)} %psum.15.gate_grad_ref, f32[1,1152]{1,0:T(1,128)S(1)} %psum.14.squeeze_ref, f32[48,1152]{1,0:T(8,128)S(1)} %get-tuple-element.40.reduce_ref, f32[48,1152]{1,0:T(8,128)S(1)} %get-tuple-element.39.excite_ref, ...), custom_call_target="tpu_custom_call" | custom-call | tf_op jit(solution)/shard_map/depthwise_grad/pallas_call | solution.py:530
  130.6 1.5 dynamic-slice_bitcast_fusion
  132.1 6.8 %collective-permute-start.2 = (f32[16,16,1152]{2,1,0:T(8,128)S(1)}, f32[16,16,1152]{2,1,0:T(8,128)}, u32[]{:S(2)}, u32[]{:S(2)}) collective-permute-start(f32[16,16,1152]{2,1,0:T(8,128)S(1)} %dynamic-slice_bitcast_fusion), channel_id=1, source_target_pairs={{0,4},{4,0},{1,5},{5,1},{2,6},{6,2},{3,7},{7,3},{8,12},{12,8},{9,1... | collective-permute-start | bytes 3538952 | tf_op jit(solution)/shard_map/ppermute | solution.py:573
  138.9 2.6 %collective-permute-done.2 = f32[16,16,1152]{2,1,0:T(8,128)} collective-permute-done((f32[16,16,1152]{2,1,0:T(8,128)S(1)}, f32[16,16,1152]{2,1,0:T(8,128)}, u32[]{:S(2)}, u32[]{:S(2)}) %collective-permute-start.2) | collective-permute-done | bytes 1179680 | tf_op jit(solution)/shard_map/ppermute | solution.py:573
  141.6 1.4 bitcast_add_fusion
  142.9 24.2 %all_to_all.21 = f32[16,16,1152]{2,1,0:T(8,128)S(1)} all-to-all(f32[16,16,1152]{2,1,0:T(8,128)S(1)} %bitcast_add_fusion), channel_id=1, replica_groups=mesh['pipe'=2,'x'=4,'y'=4,'core'=2,'space'=4] {'x','y'}, dimensions={0} | all-to-all | bytes 2359296 | tf_op jit(solution)/shard_map/all_to_all | solution.py:572
  167.1 0.1 reduce_sum.9
  167.2 2.1 collective-permute-start.3
  169.3 2.1 collective-permute-done.3
  171.4 4.0 %collective-permute-start.4 = (f32[16,1152]{1,0:T(8,128)S(1)}, f32[16,1152]{1,0:T(8,128)S(1)}, u32[]{:S(2)}, u32[]{:S(2)}) collective-permute-start(f32[16,1152]{1,0:T(8,128)S(1)} %add.34), channel_id=1, source_target_pairs={{0,2},{1,3},{2,0},{3,1},{4,6},{5,7},{6,4},{7,5},{8,10},{9,11},{10,... | collective-permute-start | bytes 221192 | tf_op jit(solution)/shard_map/ppermute | solution.py:577
  175.4 3.3 %collective-permute-done.4 = f32[16,1152]{1,0:T(8,128)S(1)} collective-permute-done((f32[16,1152]{1,0:T(8,128)S(1)}, f32[16,1152]{1,0:T(8,128)S(1)}, u32[]{:S(2)}, u32[]{:S(2)}) %collective-permute-start.4) | collective-permute-done | bytes 73760 | tf_op jit(solution)/shard_map/ppermute | solution.py:577
  178.7 0.1 broadcast_in_dim.2
  178.8 17.3 %all_to_all.22 = f32[16,16,1152]{2,1,0:T(8,128)S(1)} all-to-all(f32[16,16,1152]{2,1,0:T(8,128)S(1)} %broadcast_in_dim.2), channel_id=1, replica_groups=mesh['pipe'=2,'x'=4,'y'=4,'core'=2,'space'=4] {'x','y'}, dimensions={0} | all-to-all | bytes 2359296 | tf_op jit(solution)/shard_map/all_to_all | solution.py:579
  196.0 5.4 %collective-permute-start.5 = (f32[16,16,1152]{2,1,0:T(8,128)S(1)}, f32[16,16,1152]{2,1,0:T(8,128)S(1)}, u32[]{:S(2)}, u32[]{:S(2)}) collective-permute-start(f32[16,16,1152]{2,1,0:T(8,128)S(1)} %all_to_all.22), channel_id=1, source_target_pairs={{0,4},{4,0},{1,5},{5,1},{2,6},{6,2},{3,7},{7,3},{8,12},{12,8},{9,1... | collective-permute-start | bytes 3538952 | tf_op jit(solution)/shard_map/ppermute | solution.py:580
  201.4 2.5 %collective-permute-done.5 = f32[16,16,1152]{2,1,0:T(8,128)S(1)} collective-permute-done((f32[16,16,1152]{2,1,0:T(8,128)S(1)}, f32[16,16,1152]{2,1,0:T(8,128)S(1)}, u32[]{:S(2)}, u32[]{:S(2)}) %collective-permute-start.5) | collective-permute-done | bytes 1179680 | tf_op jit(solution)/shard_map/ppermute | solution.py:580
  203.9 1.1 copy-done.15
  204.9 2.7 %unpack.1 = (f32[1,176,1056]{2,1,0:T(8,128)}, f32[1,5,5,1056]{3,2,1,0:T(8,128)S(1)}, f32[1,1056,44]{2,1,0:T(8,128)S(1)}, f32[1,44,1056]{2,1,0:T(8,128)S(1)}, f32[1,1056,176]{2,1,0:T(8,128)S(1)}) custom-call(s32[1]{0:T(128)} %bitcast.core_ref, f32[256,1152]{1,0:T(8,128)S(1)} %bitcast.30, f32[256,1152]{1,0:T(8,128)} %bitcast.40), custom_call_target="tpu_custom_call" | custom-call | tf_op jit(solution)/shard_map/unpack/pallas_call | solution.py:581
  207.7 1.2 copy.29
  208.9 0.9 copy.27
  209.8 0.9 copy.28
  210.7 0.8 copy.26
  (38 shorter events, 0.3 us)
Async XLA Ops:
  0.6 8.5 %copy-start.16 = (bf16[1,176,1056]{2,1,0:T(8,128)(2,1)S(1)}, bf16[1,176,1056]{2,1,0:T(8,128)(2,1)}, u32[]{:S(2)}) copy-start(bf16[1,176,1056]{2,1,0:T(8,128)(2,1)} %param.9) | copy-start | bytes 1115140
  0.6 8.6 %copy-start.20 = (bf16[1,5,5,1056]{3,2,1,0:T(8,128)(2,1)S(1)}, bf16[1,5,5,1056]{3,2,1,0:T(8,128)(2,1)}, u32[]{:S(2)}) copy-start(bf16[1,5,5,1056]{3,2,1,0:T(8,128)(2,1)} %param.10) | copy-start | bytes 158404
  0.7 8.6 %copy-start.19 = (bf16[1,1056,44]{1,2,0:T(8,128)(2,1)S(1)}, bf16[1,1056,44]{1,2,0:T(8,128)(2,1)}, u32[]{:S(2)}) copy-start(bf16[1,1056,44]{1,2,0:T(8,128)(2,1)} %param.11) | copy-start | bytes 278788
  0.7 8.6 %copy-start.18 = (bf16[1,44,1056]{2,1,0:T(8,128)(2,1)S(1)}, bf16[1,44,1056]{2,1,0:T(8,128)(2,1)}, u32[]{:S(2)}) copy-start(bf16[1,44,1056]{2,1,0:T(8,128)(2,1)} %param.12) | copy-start | bytes 278788
  2.0 15.9 %collective-permute-start = (bf16[2,100,176]{2,1,0:T(8,128)(2,1)S(1)}, bf16[2,100,176]{2,1,0:T(8,128)(2,1)S(1)}, u32[]{:S(2)}, u32[]{:S(2)}) collective-permute-start(bf16[2,100,176]{2,1,0:T(8,128)(2,1)S(1)} %get-tuple-element.38), channel_id=1, source_target_pairs={{0,1},{1,2},{2,3},{4,5},{5,6},{6,7},{8,9},{9,10},{10,11},{12,13},{... | collective-permute-start | bytes 211208 | tf_op jit(solution)/shard_map/ppermute | solution.py:425
  7.7 1.7 copy-start.17
  7.7 11.5 %collective-permute-start.1 = (bf16[2,100,176]{2,1,0:T(8,128)(2,1)S(1)}, bf16[2,100,176]{2,1,0:T(8,128)(2,1)S(1)}, u32[]{:S(2)}, u32[]{:S(2)}) collective-permute-start(bf16[2,100,176]{2,1,0:T(8,128)(2,1)S(1)} %get-tuple-element.37), channel_id=1, source_target_pairs={{1,0},{2,1},{3,2},{5,4},{6,5},{7,6},{9,8},{10,9},{11,10},{13,12},{... | collective-permute-start | bytes 211208 | tf_op jit(solution)/shard_map/ppermute | solution.py:426
  9.4 9.8 %copy-start = (f32[32,1152]{1,0:T(8,128)}, f32[32,1152]{1,0:T(8,128)S(1)}, u32[]{:S(2)}) copy-start(f32[32,1152]{1,0:T(8,128)S(1)} %pad_convert_fusion.2.depth_ref) | copy-start | bytes 442372
  36.1 0.9 copy-start.2
  37.0 0.8 copy-start.6
  37.8 0.8 copy-start.12
  50.2 1.0 copy-start.13
  59.8 0.8 copy-start.8
  61.2 10.3 %all-to-all-start = ((f32[8,1,512]{2,1,0:T(1,128)}), f32[8,1,512]{2,1,0:T(1,128)S(1)}, u32[]{:S(2)}, u32[]{:S(2)}) async-start(f32[8,1,512]{2,1,0:T(1,128)} %copy.25), calls=%async_computation | async-start | bytes 32768 | tf_op jit(solution)/shard_map/all_to_all | solution.py:500
  71.5 1.0 copy-start.9
  72.5 22.5 %copy-start.1 = (f32[32,1152]{1,0:T(8,128)S(1)}, f32[32,1152]{1,0:T(8,128)}, u32[]{:S(2)}) copy-start(f32[32,1152]{1,0:T(8,128)} %copy-done) | copy-start | bytes 442372
  86.0 0.9 copy-start.4
  86.9 0.8 copy-start.10
  95.0 1.1 copy-start.3
  96.2 1.1 copy-start.5
  97.3 1.1 copy-start.7
  98.4 1.0 copy-start.11
  130.6 10.9 %copy-start.14 = (f32[512,1152]{1,0:T(8,128)S(1)}, f32[512,1152]{1,0:T(8,128)}, u32[]{:S(2)}) copy-start(f32[512,1152]{1,0:T(8,128)} %depthwise_grad.1) | copy-start | bytes 7077892
  132.1 9.4 %collective-permute-start.2 = (f32[16,16,1152]{2,1,0:T(8,128)S(1)}, f32[16,16,1152]{2,1,0:T(8,128)}, u32[]{:S(2)}, u32[]{:S(2)}) collective-permute-start(f32[16,16,1152]{2,1,0:T(8,128)S(1)} %dynamic-slice_bitcast_fusion), channel_id=1, source_target_pairs={{0,4},{4,0},{1,5},{5,1},{2,6},{6,2},{3,7},{7,3},{8,12},{12,8},{9,1... | collective-permute-start | bytes 3538952 | tf_op jit(solution)/shard_map/ppermute | solution.py:573
  167.2 4.2 %collective-permute-start.3 = (f32[16,1152]{1,0:T(8,128)S(1)}, f32[16,1152]{1,0:T(8,128)S(1)}, u32[]{:S(2)}, u32[]{:S(2)}) collective-permute-start(f32[16,1152]{1,0:T(8,128)S(1)} %reduce_sum.9), channel_id=1, source_target_pairs={{0,1},{1,0},{2,3},{3,2},{4,5},{5,4},{6,7},{7,6},{8,9},{9,8},{10,11... | collective-permute-start | bytes 221192 | tf_op jit(solution)/shard_map/ppermute | solution.py:577
  171.4 7.3 %collective-permute-start.4 = (f32[16,1152]{1,0:T(8,128)S(1)}, f32[16,1152]{1,0:T(8,128)S(1)}, u32[]{:S(2)}, u32[]{:S(2)}) collective-permute-start(f32[16,1152]{1,0:T(8,128)S(1)} %add.34), channel_id=1, source_target_pairs={{0,2},{1,3},{2,0},{3,1},{4,6},{5,7},{6,4},{7,5},{8,10},{9,11},{10,... | collective-permute-start | bytes 221192 | tf_op jit(solution)/shard_map/ppermute | solution.py:577
  196.0 7.9 %collective-permute-start.5 = (f32[16,16,1152]{2,1,0:T(8,128)S(1)}, f32[16,16,1152]{2,1,0:T(8,128)S(1)}, u32[]{:S(2)}, u32[]{:S(2)}) collective-permute-start(f32[16,16,1152]{2,1,0:T(8,128)S(1)} %all_to_all.22), channel_id=1, source_target_pairs={{0,4},{4,0},{1,5},{5,1},{2,6},{6,2},{3,7},{7,3},{8,12},{12,8},{9,1... | collective-permute-start | bytes 3538952 | tf_op jit(solution)/shard_map/ppermute | solution.py:580
  203.9 1.1 copy-start.15

commit v3 on v2

v3 whole, which is shorter than its diff:
```python
import jax
import jax.numpy as jnp
from jax import lax
from jax.experimental import pallas as pl
from jax.experimental.pallas import tpu as pltpu
from jax.sharding import Mesh
from jax.sharding import PartitionSpec as P

loss_scale = 256.0
f32 = jnp.float32
bf16 = jnp.bfloat16
LANES = 128
BAND = 384
HEAD_CHUNK = 512
UNROLL = 2
STRIP = 50
WIDE = 100
TAPS = 50
VMEM = pl.BlockSpec(memory_space=pltpu.VMEM)
SMEM = pl.BlockSpec(memory_space=pltpu.SMEM)
ANY = pl.BlockSpec(memory_space=pl.ANY)
PARAMS = pltpu.CompilerParams(vmem_limit_bytes=60 * 1024 * 1024)


def up_to(size, multiple):
    return -(-size // multiple) * multiple


def started(*copies):
    made = [pltpu.make_async_copy(*copy) for copy in copies]
    for copy in made:
        copy.start()
    return made


def chunks(width, chunk, work):
    whole = width // chunk

    @pl.loop(0, whole, unroll=UNROLL)
    def each(part):
        work(pl.multiple_of(part * chunk, chunk), chunk)

    if width > whole * chunk:
        work(whole * chunk, width - whole * chunk)


def contract(left, right, left_dim, right_dim):
    return lax.dot_general(
        left, right, (((left_dim,), (right_dim,)), ((), ())), preferred_element_type=f32
    )


def row_window(own, rim, extent, place):
    margin = extent // 2
    window = []
    for i in range(extent):
        d = i - margin
        if d == 0:
            window.append(own)
        elif d > 0:
            window.append(pltpu.roll(jnp.where(place < d, rim, own), 8 - d, 0))
        else:
            window.append(pltpu.roll(jnp.where(place >= 8 + d, rim, own), -d, 0))
    return window


def forward_kernel(
    own_ref, before_ref, after_ref, expand_ref, depth_ref,
    cells_out, cells_t_out, mine_out, half_out, squeeze_ref,
    cells_ref, cells_t_ref, mine_ref, half_ref, left, right, expanded, sems,
):
    columns, channels = own_ref.shape[1:]
    extent, margin = 5, 2

    left[...] = jnp.zeros_like(left)
    right[...] = jnp.zeros_like(right)
    rest = channels - LANES
    for ref, base in ((own_ref, 0), (after_ref, 8), (before_ref, 14)):
        for y in range(ref.shape[0]):
            row = ref[y].astype(f32)
            left[pl.ds(base + y, columns, stride=16), :] = row[:, :LANES]
            right[pl.ds(base + y, columns, stride=16), :] = jnp.concatenate(
                [row[:, LANES:], jnp.zeros((columns, LANES - rest), f32)], axis=1
            )
    low, high = left[...], right[...]
    cells_ref[:, :LANES] = low.astype(bf16)
    cells_ref[:, LANES:] = high[:, :rest].astype(bf16)
    for start in range(0, 16 * columns, 320):
        cells_t_ref[:LANES, start : start + 320] = left[start : start + 320, :].T.astype(bf16)
        cells_t_ref[LANES:, start : start + 320] = right[start : start + 320, :].T[:rest].astype(
            bf16
        )
    mine_ref[:, :LANES] = (
        low.reshape(columns, 16, LANES)[:, :8].reshape(8 * columns, LANES).astype(bf16)
    )
    mine_ref[:, LANES:] = (
        high.reshape(columns, 16, LANES)[:, :8]
        .reshape(8 * columns, LANES)[:, :rest]
        .astype(bf16)
    )
    sends = started(
        (cells_ref, cells_out, sems.at[0]),
        (cells_t_ref, cells_t_out, sems.at[1]),
        (mine_ref, mine_out, sems.at[2]),
    )
    edge = jnp.zeros((margin, 16, expanded.shape[2]), f32)
    expanded[:margin] = edge
    expanded[margin + columns :] = edge

    @pl.loop(0, columns // WIDE)
    def expand(part):
        rows = pl.ds(pl.multiple_of(part * 16 * WIDE, 16 * WIDE), 16 * WIDE)
        half = jnp.dot(cells_ref[rows, :], expand_ref[...], preferred_element_type=f32)
        value = half + half * jnp.tanh(half)
        expanded[pl.ds(margin + part * WIDE, WIDE)] = value.reshape(WIDE, 16, half.shape[1])

    place = lax.broadcasted_iota(jnp.int32, (8, LANES), 0)

    @pl.loop(0, expanded.shape[2] // LANES)
    def convolve(tile):
        lanes = pl.ds(pl.multiple_of(tile * LANES, LANES), LANES)
        weight = [
            [depth_ref[i * extent + j : i * extent + j + 1, lanes] for j in range(extent)]
            for i in range(extent)
        ]

        def strip(number, total):
            x0 = number * STRIP
            sums = {}
            for k in range(STRIP + extent - 1):
                window = row_window(
                    expanded[x0 + k, :8, lanes], expanded[x0 + k, 8:, lanes], extent, place
                )
                for j in range(extent):
                    x = k - j
                    if 0 <= x < STRIP:
                        term = window[0] * weight[0][j]
                        for i in range(1, extent):
                            term = term + window[i] * weight[i][j]
                        sums[x] = term if x not in sums else sums[x] + term
                x = k - extent + 1
                if x >= 0:
                    half = 0.5 * sums.pop(x)
                    half_ref[pl.ds(pl.multiple_of((x0 + x) * 8, 8), 8), lanes] = half
                    total = total + (half + half * jnp.tanh(half))
            return total

        total = lax.fori_loop(0, columns // STRIP, strip, jnp.zeros((8, LANES), f32))
        squeeze_ref[:, lanes] = jnp.sum(total, axis=0, keepdims=True)
        pltpu.make_async_copy(
            half_ref.at[:, lanes], half_out.at[:, lanes], sems.at[3 + tile]
        ).start()

    for tile in range(half_ref.shape[1] // LANES):
        lanes = slice(tile * LANES, (tile + 1) * LANES)
        pltpu.make_async_copy(
            half_ref.at[:, lanes], half_out.at[:, lanes], sems.at[3 + tile]
        ).wait()
    for send in sends:
        send.wait()


def gate_of(squeeze, reduce_t, excite):
    reduced_in = jnp.sum(reduce_t * squeeze, axis=1, keepdims=True)
    reduced = reduced_in * jax.nn.sigmoid(reduced_in)
    gate = jax.nn.sigmoid(jnp.sum(excite * reduced, axis=0, keepdims=True))
    return reduced_in, reduced, gate


def head_kernel(
    half_in, squeeze_ref, reduce_ref, excite_ref, project_in, mine_in, head_in, class_in,
    logits_ref, gated_out, block_ref,
    half_ref, gated_ref, project_ref, mine_ref, head_ref, class_ref, gate_row, sums,
    sems, part_sems,
):
    cells = half_ref.shape[0]
    classes = class_ref.shape[0]

    def piece(part):
        rows = pl.ds(pl.multiple_of(part * 80, 80), 80)
        return half_in.at[rows, :], half_ref.at[rows, :], part_sems.at[part]

    for part in range(cells // 80):
        started(piece(part))
    project_copy, mine_copy, head_copy, class_copy = started(
        (project_in, project_ref, sems.at[3]),
        (mine_in, mine_ref, sems.at[4]),
        (head_in, head_ref, sems.at[0]),
        (class_in, class_ref, sems.at[1]),
    )
    cell_total = 4 * cells
    gate_row[...] = gate_of(squeeze_ref[...] / cell_total, reduce_ref[...], excite_ref[...])[2]

    @pl.loop(0, cells // 80)
    def gating(part):
        pltpu.make_async_copy(*piece(part)).wait()
        rows = pl.ds(pl.multiple_of(part * 80, 80), 80)
        half = half_ref[rows, :]
        gated_ref[rows, :] = ((half + half * jnp.tanh(half)) * gate_row[...]).astype(bf16)

    (send,) = started((gated_ref, gated_out, sems.at[2]))
    project_copy.wait()
    mine_copy.wait()
    residual = contract(gated_ref[...], project_ref[...], 1, 1)
    block = (mine_ref[...].astype(f32) + residual).astype(bf16)
    block_ref[...] = (0.5 * block.astype(f32)).astype(bf16)

    def head(first, count):
        lanes = pl.ds(first, count)
        half = jnp.dot(block_ref[...], head_ref[:, lanes], preferred_element_type=f32)
        act = half + half * jnp.tanh(half)
        sums[:, lanes] = jnp.sum(act.reshape(cells // 8, 8, count), axis=0)

    head_copy.wait()
    chunks(head_ref.shape[1], HEAD_CHUNK, head)
    class_copy.wait()
    pooled = sums[...]
    high = pooled.astype(bf16).astype(f32)
    both = jnp.concatenate([high, pooled - high], axis=0).astype(bf16)
    partial = jnp.sum(contract(both, class_ref[...], 1, 1), axis=0, keepdims=True)
    logits_ref[...] = jnp.zeros_like(logits_ref)
    logits_ref[:, :classes] = jnp.broadcast_to(
        partial / cell_total, (logits_ref.shape[0], classes)
    )
    send.wait()


def head_grad_kernel(
    which_ref, logits_ref, block_in, gated_in, project_in, head_in, class_in,
    grad_ref, project_grad_ref, gate_grad_ref,
    block_ref, gated_ref, project_ref, head_ref, class_ref, pooled, total, sems,
):
    class_copy, block_copy, head_copy, gated_copy, project_copy = started(
        (class_in, class_ref, sems.at[0]),
        (block_in, block_ref, sems.at[1]),
        (head_in, head_ref, sems.at[2]),
        (gated_in, gated_ref, sems.at[3]),
        (project_in, project_ref, sems.at[4]),
    )
    cells = block_ref.shape[0]
    classes = class_ref.shape[0]
    total[...] = jnp.zeros_like(total)

    rows = logits_ref[...]
    network = lax.broadcasted_iota(jnp.int32, rows.shape, 0) % 2
    valid = lax.broadcasted_iota(jnp.int32, (1, rows.shape[1]), 1) < classes
    teacher = jnp.sum(jnp.where(network == 0, rows, 0.0), axis=0, keepdims=True)
    student = jnp.sum(jnp.where(network == 1, rows, 0.0), axis=0, keepdims=True)
    exp_teacher = jnp.where(valid, jnp.exp(teacher), 0.0)
    prob = exp_teacher / jnp.sum(exp_teacher, axis=1, keepdims=True)
    log_sum = jnp.log(
        jnp.sum(jnp.where(valid, jnp.exp(student), 0.0), axis=1, keepdims=True)
    )
    logprob = student - log_sum
    cross = jnp.sum(prob * logprob, axis=1, keepdims=True)
    teacher_grad = loss_scale * prob * (cross - logprob)
    student_grad = loss_scale * (jnp.exp(logprob) - prob)
    grad = jnp.where(which_ref[0] == 0, teacher_grad, student_grad)
    grad = jnp.where(valid, grad, 0.0)
    grad = jnp.broadcast_to(grad, (16, rows.shape[1])).astype(bf16)[:, :classes]
    class_copy.wait()
    pooled[...] = contract(grad, class_ref[...], 1, 0)[:1] * (0.5 / (4 * cells))

    def head(first, count):
        lanes = pl.ds(first, count)
        weight = head_ref[:, lanes]
        half = jnp.dot(block_ref[...], weight, preferred_element_type=f32)
        t = jnp.tanh(half)
        slope = (1.0 + t) * (1.0 + (half - half * t))
        grad_head = (slope * pooled[:, lanes]).astype(bf16)
        total[...] += contract(grad_head, weight, 1, 1)

    block_copy.wait()
    head_copy.wait()
    chunks(head_ref.shape[1], HEAD_CHUNK, head)
    grad_block = total[...]
    grad_ref[...] = grad_block.astype(bf16)
    gated_copy.wait()
    project_copy.wait()
    project_grad = jnp.dot(grad_block.T.astype(bf16), gated_ref[...], preferred_element_type=f32)
    project_grad_ref[...] = project_grad
    gate_grad_ref[...] = jnp.sum(
        project_ref[...].astype(f32) * project_grad, axis=0, keepdims=True
    )


def backward_kernel(
    space_ref, gate_grad_ref, squeeze_ref, reduce_ref, excite_ref, cells_in, cells_t_in,
    expand_in, depth_ref, half_in, grad_in, project_in, project_grad_in,
    out_ref,
    cells_ref, cells_t_ref, expand_ref, half_ref, grad_ref, project_ref, gate_row, pool_row,
    expanded, slope, grad_depth, grad_expand, sems,
):
    channels = grad_in.shape[1]
    depth_base = 2 * channels
    arriving = started(
        (cells_in, cells_ref, sems.at[0]),
        (expand_in, expand_ref, sems.at[1]),
        (grad_in, grad_ref, sems.at[2]),
        (project_in, project_ref, sems.at[3]),
        (half_in, half_ref, sems.at[4]),
        (cells_t_in, cells_t_ref, sems.at[5]),
        (project_grad_in, out_ref.at[channels:depth_base, :], sems.at[6]),
    )
    cells = half_ref.shape[0]
    columns = cells // 8
    reduced_rows = reduce_ref.shape[0]
    extent, margin = 5, 2
    cell_total = 4 * cells
    excite_base = depth_base + up_to(extent * extent, 8)
    reduce_base = excite_base + reduced_rows
    end = reduce_base + reduced_rows

    squeeze = squeeze_ref[...] / cell_total
    reduced_in, reduced, gate = gate_of(squeeze, reduce_ref[...], excite_ref[...])
    grad_excite = (1.0 - gate) * gate_grad_ref[...]
    sigma = jax.nn.sigmoid(reduced_in)
    grad_reduced = jnp.sum(excite_ref[...] * grad_excite, axis=1, keepdims=True) * (
        sigma * (1.0 + reduced_in * (1.0 - sigma))
    )
    back_pool = jnp.sum(reduce_ref[...] * grad_reduced, axis=0, keepdims=True)
    gate_row[...] = 0.25 * gate
    pool_row[...] = back_pool * (0.25 / cell_total)
    once = jnp.where(space_ref[0] == 0, 1.0, 0.0)
    out_ref[excite_base:reduce_base, :] = reduced * (grad_excite * once)
    out_ref[reduce_base:end, :] = grad_reduced * (squeeze * once)
    if end < out_ref.shape[0]:
        out_ref[end:, :] = jnp.zeros((out_ref.shape[0] - end, out_ref.shape[1]), f32)
    edge = jnp.zeros((margin, 16, BAND), f32)
    expanded[:margin] = edge
    expanded[margin + columns :] = edge
    grad_depth[:margin] = edge[:, :8]
    grad_depth[margin + columns :] = edge[:, :8]

    for copy in arriving[:2]:
        copy.wait()

    @pl.loop(0, out_ref.shape[1] // BAND)
    def each(step):
        backward_band(
            step, arriving[2:], depth_base, excite_base,
            cells_ref, cells_t_ref, expand_ref, depth_ref, half_ref, grad_ref, project_ref,
            out_ref, gate_row, pool_row, expanded, slope, grad_depth, grad_expand,
        )


def backward_band(
    step, arriving, depth_base, excite_base,
    cells_ref, cells_t_ref, expand_ref, depth_ref, half_ref, grad_ref, project_ref,
    out_ref, gate_row, pool_row, expanded, slope, grad_depth, grad_expand,
):
    columns = half_ref.shape[0] // 8
    channels = grad_ref.shape[1]
    extent, margin = 5, 2
    start = pl.multiple_of(step * BAND, BAND)
    band = pl.ds(start, BAND)
    gate = gate_row[:, band]
    back_pool = pool_row[:, band]

    @pl.loop(0, columns // WIDE)
    def elements(part):
        rows = pl.ds(pl.multiple_of(part * 16 * WIDE, 16 * WIDE), 16 * WIDE)
        half = jnp.dot(cells_ref[rows, :], expand_ref[:, band], preferred_element_type=f32)
        t = jnp.tanh(half)
        turn = half * t
        expanded[pl.ds(margin + part * WIDE, WIDE)] = (half + turn).reshape(WIDE, 16, BAND)
        value = (1.0 + t) * (1.0 + (half - turn))
        slope[pl.ds(part * WIDE, WIDE)] = value.reshape(WIDE, 16, BAND)

    @pl.when(step == 0)
    def arrive():
        for copy in arriving:
            copy.wait()

    @pl.loop(0, columns // WIDE)
    def gradients(part):
        rows = pl.ds(pl.multiple_of(part * 8 * WIDE, 8 * WIDE), 8 * WIDE)
        grad_gated = jnp.dot(
            grad_ref[rows, :], project_ref[:, band], preferred_element_type=f32
        )
        half = half_ref[rows, band]
        t = jnp.tanh(half)
        value = (grad_gated * gate + back_pool) * ((1.0 + t) * (1.0 + (half - half * t)))
        grad_depth[pl.ds(margin + part * WIDE, WIDE)] = value.reshape(WIDE, 8, BAND)

    place = lax.broadcasted_iota(jnp.int32, (8, LANES), 0)

    @pl.loop(0, BAND // LANES)
    def convolve(tile):
        lanes = pl.ds(pl.multiple_of(tile * LANES, LANES), LANES)
        out_lanes = pl.ds(pl.multiple_of(start + tile * LANES, LANES), LANES)

        def taps(number, sums):
            sums = [list(line) for line in sums]
            base = margin + number * TAPS
            grads = {}
            for k in range(TAPS):
                window = row_window(
                    expanded[base + k, :8, lanes], expanded[base + k, 8:, lanes], extent, place
                )
                for j in range(extent):
                    place_x = k - j
                    if place_x not in grads:
                        grads[place_x] = grad_depth[base + place_x + margin, :, lanes]
                    for i in range(extent):
                        sums[i][j] = sums[i][j] + window[i] * grads[place_x]
            return tuple(tuple(line) for line in sums)

        zero = jnp.zeros((8, LANES), f32)
        sums = lax.fori_loop(0, columns // TAPS, taps, ((zero,) * extent,) * extent)
        for i in range(extent):
            for j in range(extent):
                row = depth_base + i * extent + j
                out_ref[row : row + 1, out_lanes] = 2.0 * jnp.sum(sums[i][j], axis=0, keepdims=True)
        for row in range(depth_base + extent * extent, excite_base):
            out_ref[row : row + 1, out_lanes] = jnp.zeros((1, LANES), f32)

        weight = [
            [depth_ref[i * extent + j : i * extent + j + 1, out_lanes] for j in range(extent)]
            for i in range(extent)
        ]

        @pl.loop(0, columns // STRIP)
        def spread(number):
            x0 = number * STRIP
            grads = [grad_depth[x0 + k, :, lanes] for k in range(extent - 1)]
            for x in range(STRIP):
                grads.append(grad_depth[x0 + x + extent - 1, :, lanes])
                whole, far = None, None
                for i in range(extent):
                    term = grads[x + extent - 1] * weight[i][0]
                    for j in range(1, extent):
                        term = term + grads[x + extent - 1 - j] * weight[i][j]
                    d = i - margin
                    if d != 0:
                        term = pltpu.roll(term, d % 8, 0)
                        inside = place >= d if d > 0 else place < 8 + d
                        leave = jnp.where(inside, 0.0, term)
                        far = leave if far is None else far + leave
                    whole = term if whole is None else whole + term
                near = whole - far
                near = near * slope[x0 + x, :8, lanes]
                far = far * slope[x0 + x, 8:, lanes]
                rows = pl.ds(pl.multiple_of((x0 + x) * 16, 16), 16)
                grad_expand[rows, lanes] = jnp.concatenate([near, far], axis=0).astype(bf16)

    out_ref[:channels, band] = jnp.dot(
        cells_t_ref[...], grad_expand[...], preferred_element_type=f32
    )


def unpack_kernel(
    core_ref, own_ref, other_ref, expand_ref, depth_ref, reduce_ref, excite_ref, project_ref
):
    channels, hidden = expand_ref.shape[1:]
    extent = depth_ref.shape[0]
    reduced = excite_ref.shape[0]
    depth_base = 2 * channels
    excite_base = depth_base + up_to(extent * extent, 8)
    reduce_base = excite_base + up_to(reduced, 8)
    half_rows = own_ref.shape[0]

    def rows(start, stop):
        pieces = []
        if start < half_rows:
            end = min(stop, half_rows)
            pieces.append(
                jnp.where(core_ref[0] == 0, own_ref[start:end, :], other_ref[start:end, :])
            )
        if stop > half_rows:
            begin = max(start, half_rows)
            pieces.append(
                jnp.where(
                    core_ref[0] == 0,
                    other_ref[begin - half_rows : stop - half_rows, :],
                    own_ref[begin - half_rows : stop - half_rows, :],
                )
            )
        return pieces[0] if len(pieces) == 1 else jnp.concatenate(pieces, axis=0)

    expand_ref[0] = rows(0, channels)[:, :hidden]
    project_ref[0] = rows(channels, depth_base)[:, :hidden]
    depth = rows(depth_base, excite_base)[:, :hidden]
    for i in range(extent):
        for j in range(extent):
            depth_ref[i, j] = depth[i * extent + j : i * extent + j + 1]
    excite = rows(excite_base, reduce_base)[:, :hidden]
    reduce = rows(reduce_base, reduce_base + up_to(reduced, 8))[:, :hidden]
    for row in range(reduced):
        excite_ref[row] = excite[row : row + 1]
        reduce_ref[row] = reduce[row : row + 1]


def shards(views, w_expand, w_depth, w_reduce, w_excite, w_project, w_head, w_class):
    own = views[0, 0]
    height, columns, channels = own.shape
    hidden = w_expand.shape[2]
    reduced = w_reduce.shape[2]
    extent = w_depth.shape[1]
    width = w_head.shape[2]
    classes = w_class.shape[2]
    cells = height * columns
    space = lax.axis_size("space")
    broad = up_to(hidden, BAND)
    tall = up_to(reduced, 8)

    up = [(i, i + 1) for i in range(space - 1)]
    down = [(i + 1, i) for i in range(space - 1)]
    before = lax.ppermute(own[height - 2 :], "space", up)
    after = lax.ppermute(own[:2], "space", down)

    fill = broad - hidden
    expand_w = jnp.pad(w_expand[0] * bf16(0.5), ((0, 0), (0, fill)))
    depth_w = jnp.pad(
        w_depth[0].reshape(extent * extent, hidden).astype(f32),
        ((0, up_to(extent * extent, 8) - extent * extent), (0, fill)),
    )
    reduce_t = jnp.pad(w_reduce[0].T.astype(f32), ((0, tall - reduced), (0, fill)))
    excite_w = jnp.pad(w_excite[0].astype(f32), ((0, tall - reduced), (0, fill)))
    class_t = w_class[0].T
    project_t = jnp.pad(w_project[0].T, ((0, 0), (0, fill)))

    depth_rows = depth_w.shape[0]
    cell_rows, cells_t, mine, half, squeeze = pl.pallas_call(
        forward_kernel,
        in_specs=[VMEM] * 5,
        out_specs=[ANY] * 4 + [VMEM],
        out_shape=[
            jax.ShapeDtypeStruct((16 * columns, channels), bf16),
            jax.ShapeDtypeStruct((channels, 16 * columns), bf16),
            jax.ShapeDtypeStruct((cells, channels), bf16),
            jax.ShapeDtypeStruct((cells, broad), f32),
            jax.ShapeDtypeStruct((1, broad), f32),
        ],
        scratch_shapes=[
            pltpu.VMEM((16 * columns, channels), bf16),
            pltpu.VMEM((channels, 16 * columns), bf16),
            pltpu.VMEM((cells, channels), bf16),
            pltpu.VMEM((cells, broad), f32),
            pltpu.VMEM((16 * columns, LANES), f32),
            pltpu.VMEM((16 * columns, LANES), f32),
            pltpu.VMEM((columns + 4, 16, broad), f32),
            pltpu.SemaphoreType.DMA((3 + broad // LANES,)),
        ],
        compiler_params=PARAMS,
        name="expand_depthwise",
    )(own, before, after, expand_w, depth_w)
    squeeze = lax.psum(squeeze, "space")

    ranks = 2 * space
    logits, gated, block = pl.pallas_call(
        head_kernel,
        in_specs=[ANY] + [VMEM] * 3 + [ANY] * 4,
        out_specs=[VMEM, ANY, VMEM],
        out_shape=[
            jax.ShapeDtypeStruct((ranks, up_to(classes, LANES)), f32),
            jax.ShapeDtypeStruct((cells, broad), bf16),
            jax.ShapeDtypeStruct((cells, channels), bf16),
        ],
        scratch_shapes=[
            pltpu.VMEM((cells, broad), f32),
            pltpu.VMEM((cells, broad), bf16),
            pltpu.VMEM((channels, broad), bf16),
            pltpu.VMEM((cells, channels), bf16),
            pltpu.VMEM((channels, width), bf16),
            pltpu.VMEM((classes, width), bf16),
            pltpu.VMEM((1, broad), f32),
            pltpu.VMEM((8, width), f32),
            pltpu.SemaphoreType.DMA((5,)),
            pltpu.SemaphoreType.DMA((cells // 80,)),
        ],
        compiler_params=PARAMS,
        name="project_head",
    )(half, squeeze, reduce_t, excite_w, project_t, mine, w_head[0], class_t)
    logits = lax.all_to_all(logits, ("space", "pipe"), 0, 0, tiled=True)

    def index(name):
        return lax.axis_index(name).astype(jnp.int32).reshape(1)

    grad_block, project_grad, gate_grad = pl.pallas_call(
        head_grad_kernel,
        in_specs=[SMEM, VMEM] + [ANY] * 5,
        out_specs=[VMEM] * 3,
        out_shape=[
            jax.ShapeDtypeStruct((cells, channels), bf16),
            jax.ShapeDtypeStruct((channels, broad), f32),
            jax.ShapeDtypeStruct((1, broad), f32),
        ],
        scratch_shapes=[
            pltpu.VMEM((cells, channels), bf16),
            pltpu.VMEM((cells, broad), bf16),
            pltpu.VMEM((channels, broad), bf16),
            pltpu.VMEM((channels, width), bf16),
            pltpu.VMEM((classes, width), bf16),
            pltpu.VMEM((1, width), f32),
            pltpu.VMEM((cells, channels), f32),
            pltpu.SemaphoreType.DMA((5,)),
        ],
        compiler_params=PARAMS,
        name="head_grad",
    )(index("pipe"), logits, block, gated, project_t, w_head[0], class_t)
    gate_grad = lax.psum(gate_grad, "space")

    peers = lax.axis_size("x") * lax.axis_size("y")
    used = 2 * channels + depth_rows + 2 * tall
    share = up_to(-(-used // (2 * peers)), 8)
    rows = 2 * peers * share
    packed = pl.pallas_call(
        backward_kernel,
        in_specs=[SMEM] + [VMEM] * 4 + [ANY] * 3 + [VMEM] + [ANY] * 4,
        out_specs=VMEM,
        out_shape=jax.ShapeDtypeStruct((rows, broad), f32),
        scratch_shapes=[
            pltpu.VMEM((16 * columns, channels), bf16),
            pltpu.VMEM((channels, 16 * columns), bf16),
            pltpu.VMEM((channels, broad), bf16),
            pltpu.VMEM((cells, broad), f32),
            pltpu.VMEM((cells, channels), bf16),
            pltpu.VMEM((channels, broad), bf16),
            pltpu.VMEM((1, broad), f32),
            pltpu.VMEM((1, broad), f32),
            pltpu.VMEM((columns + 4, 16, BAND), f32),
            pltpu.VMEM((columns, 16, BAND), f32),
            pltpu.VMEM((columns + 4, 8, BAND), f32),
            pltpu.VMEM((16 * columns, BAND), bf16),
            pltpu.SemaphoreType.DMA((7,)),
        ],
        compiler_params=PARAMS,
        name="depthwise_grad",
    )(
        index("space"), gate_grad, squeeze, reduce_t, excite_w, cell_rows, cells_t,
        expand_w, depth_w, half, grad_block, project_t, project_grad,
    )

    halves = packed.reshape(2, peers, share, broad)
    core = lax.axis_index("core")
    swap = [(0, 1), (1, 0)]
    keep = lax.dynamic_index_in_dim(halves, core, 0, False)
    send = lax.dynamic_index_in_dim(halves, 1 - core, 0, False)
    pieces = lax.all_to_all(
        keep + lax.ppermute(send, "core", swap), ("x", "y"), 0, 0, tiled=True
    )
    piece = jnp.sum(pieces, axis=0)
    for step in (1, 2):
        piece = piece + lax.ppermute(piece, "space", [(i, i ^ step) for i in range(space)])
    copies = jnp.broadcast_to(piece[None], pieces.shape)
    gathered = lax.all_to_all(copies, ("x", "y"), 0, 0, tiled=True)
    remote = lax.ppermute(gathered, "core", swap)
    g_expand, g_depth, g_reduce, g_excite, g_project = pl.pallas_call(
        unpack_kernel,
        in_specs=[SMEM] + [VMEM] * 2,
        out_specs=[VMEM] * 5,
        out_shape=[
            jax.ShapeDtypeStruct((1, channels, hidden), f32),
            jax.ShapeDtypeStruct((extent, extent, 1, hidden), f32),
            jax.ShapeDtypeStruct((reduced, 1, hidden), f32),
            jax.ShapeDtypeStruct((reduced, 1, hidden), f32),
            jax.ShapeDtypeStruct((1, channels, hidden), f32),
        ],
        compiler_params=PARAMS,
        name="unpack",
    )(index("core"), gathered.reshape(peers * share, broad), remote.reshape(peers * share, broad))
    return (
        g_expand,
        g_depth.transpose(2, 0, 1, 3),
        g_reduce.transpose(1, 2, 0),
        g_excite.transpose(1, 0, 2),
        g_project.transpose(0, 2, 1),
    )


def solution(mesh):
    pipe, replica, space = (mesh.shape[name] for name in ("pipe", "replica", "space"))
    side = 1
    while 2 * side * side < replica:
        side *= 2
    fine = Mesh(
        mesh.devices.reshape(pipe, replica // (2 * side), side, 2, space),
        ("pipe", "x", "y", "core", "space"),
    )
    in_specs = (P("pipe", ("x", "y", "core"), "space"),) + (P("pipe"),) * 7
    return jax.shard_map(
        shards, mesh=fine, in_specs=in_specs, out_specs=(P("pipe"),) * 5, check_vma=False
    )
```

time: 212 us -> 192 us (0.906)
  local copies, waits for them, and re-layouts: 28.1 us -> 8.16 us
  Pallas kernels: 72.9 us -> 65.3 us
  waiting for transfers between devices: 18.4 us -> 23.9 us
    unnamed x45 -> x24, local copies, waits for them, and re-layouts: 22 us -> 3.6 us
    pallas_call x4, Pallas kernels: 70.2 us -> 62.3 us  [the longest x1 25.7 us: shards(): pl.pallas_call(backward_kernel, in_specs=[SMEM] + [VMEM] * 4 + [ANY] * 3...]
    ppermute x1, waiting for transfers between devices: 1.32 us -> 6.83 us  [shards(): after = lax.ppermute(own[:2], 'space', down)]
    pallas_call x4 -> x0, local copies, waits for them, and re-layouts: 3.79 us -> none  [shards(): pl.pallas_call(unpack_kernel, in_specs=[SMEM] + [VMEM] * 2, out_specs=[VM...]
  transfers between devices with their start and end apart: 7 -> 7, of which waited for: 6 -> 6; matrix products, arithmetic and copies ran while one was open for 4% -> 2% of each run, Pallas kernels for 0% -> 0%
where the time goes in v3:
time: 192 us
  Pallas kernels  65.3 us (34%)
  blocking collectives  60.5 us (32%)
  starting transfers between devices  30 us (16%)
  waiting for transfers between devices  23.9 us (12%)
  local copies, waits for them, and re-layouts  8.16 us (4%)
  other arithmetic  3 us (2%)
    pallas_call x1, Pallas kernels, shards(): pl.pallas_call(backward_kernel, in_specs=[SMEM] + [VMEM] * 4 + [ANY] * 3...  25.7 us
    all_to_all x1, blocking collectives, shards(): lax.all_to_all(keep + lax.ppermute(send, 'core', swap), ('x', 'y'), 0, 0,...  24.1 us
    all_to_all x1, blocking collectives, shards(): gathered = lax.all_to_all(copies, ('x', 'y'), 0, 0, tiled=True)  17.3 us
    pallas_call x1, Pallas kernels, shards(): pl.pallas_call(head_grad_kernel, in_specs=[SMEM, VMEM] + [ANY] * 5, out_s...  13.5 us
    pallas_call x1, Pallas kernels, shards(): pl.pallas_call(forward_kernel, in_specs=[VMEM] * 5, out_specs=[ANY] * 4 +...  12.6 us
    psum x1, blocking collectives, shards(): squeeze = lax.psum(squeeze, 'space')  11 us
    pallas_call x1, Pallas kernels, shards(): pl.pallas_call(head_kernel, in_specs=[ANY] + [VMEM] * 3 + [ANY] * 4, out_...  10.5 us
    psum x1, blocking collectives, shards(): gate_grad = lax.psum(gate_grad, 'space')  8.11 us
  transfers between devices with their start and end apart: 7, of which 6 were waited for; matrix products, arithmetic and copies ran while one was open for 2% of the time, Pallas kernels for 0%

profile of v3, /device:TPU:1, one launch (start us, length us, event | category | flops | bytes accessed | tf_op | source)
XLA Modules:
  0.0 191.7 jit_solution(8873537702692343785)
XLA Ops:
  0.6 0.0 copy-start.4
  0.6 0.0 copy-start.10
  0.7 0.0 copy-start.7
  0.7 0.0 copy-start.6
  0.7 1.3 copy.16
  2.0 5.7 %collective-permute-start = (bf16[2,100,176]{2,1,0:T(8,128)(2,1)S(1)}, bf16[2,100,176]{2,1,0:T(8,128)(2,1)S(1)}, u32[]{:S(2)}, u32[]{:S(2)}) collective-permute-start(bf16[2,100,176]{2,1,0:T(8,128)(2,1)S(1)} %get-tuple-element.38), channel_id=1, source_target_pairs={{0,1},{1,2},{2,3},{4,5},{5,6},{6,7},{8,9},{9,10},{10,11},{12,13},{... | collective-permute-start | bytes 211208 | tf_op jit(solution)/shard_map/ppermute | solution.py:509
  7.7 0.0 copy-start.5
  7.7 1.4 collective-permute-start.1
  9.2 0.0 copy-done.4
  9.2 0.0 copy-done.10
  9.3 0.1 convert_element_type.23
  9.3 0.0 copy-done.7
  9.3 0.0 copy-done.6
  9.3 0.8 pad_convert_fusion
  10.1 0.7 pad_convert_fusion.2.depth_ref
  10.8 0.8 pad.24.expand_ref.expand_in
  11.6 0.0 copy-done.2
  11.6 0.0 copy-done.5
  11.6 0.8 pad.31.project_in
  12.4 0.0 collective-permute-done.before_ref
  12.4 6.8 %collective-permute-done.1.after_ref = bf16[2,100,176]{2,1,0:T(8,128)(2,1)S(1)} collective-permute-done((bf16[2,100,176]{2,1,0:T(8,128)(2,1)S(1)}, bf16[2,100,176]{2,1,0:T(8,128)(2,1)S(1)}, u32[]{:S(2)}, u32[]{:S(2)}) %collective-permute-start.1) | collective-permute-done | bytes 70432 | tf_op jit(solution)/shard_map/ppermute | solution.py:510
  19.2 0.6 copy-done.9
  19.9 12.6 %expand_depthwise.1 = (bf16[1600,176]{1,0:T(8,128)(2,1)}, bf16[176,1600]{1,0:T(8,128)(2,1)}, bf16[800,176]{1,0:T(8,128)(2,1)}, f32[800,1152]{1,0:T(8,128)}, f32[1,1152]{1,0:T(1,128)}) custom-call(bf16[8,100,176]{2,1,0:T(8,128)(2,1)} %bitcast.43, bf16[2,100,176]{2,1,0:T(8,128)(2,1)} %copy-done.8, bf16[2,100,176]{2,1,0:T(8,128)(2,1)} %copy-done.9, ...), custom_call_target="tpu_custom_call" | custom-call | tf_op jit(solution)/shard_map/expand_depthwise/pallas_call | solution.py:524
  32.5 11.0 %psum.14.squeeze_ref = f32[1,1152]{1,0:T(1,128)} all-reduce(f32[1,1152]{1,0:T(1,128)} %get-tuple-element.22), channel_id=1, replica_groups=mesh['pipe'=2,'x'=4,'y'=4,'core'=2,'space'=4] {'space'}, use_global_device_ids=true, to_apply=%region_0.1 | all-reduce | flops 1152 | bytes 9216 | tf_op jit(solution)/shard_map/psum | solution.py:548
  43.5 10.5 %project_head.1 = (f32[8,512]{1,0:T(8,128)}, bf16[800,1152]{1,0:T(8,128)(2,1)}, bf16[800,176]{1,0:T(8,128)(2,1)}) custom-call(f32[800,1152]{1,0:T(8,128)} %get-tuple-element.21.half_in, f32[1,1152]{1,0:T(1,128)} %psum.14.squeeze_ref, f32[48,1152]{1,0:T(8,128)} %get-tuple-element.40.reduce_ref, f32[48,1152]{1,0:T(8,128)} %get-tuple-element.39.excite_ref, ...), custom_call_target="tpu_custom_call" | custom-call | tf_op jit(solution)/shard_map/project_head/pallas_call | solution.py:551
  54.0 1.3 copy.19
  55.4 4.6 %all-to-all-start = ((f32[8,1,512]{2,1,0:T(1,128)}), f32[8,1,512]{2,1,0:T(1,128)S(1)}, u32[]{:S(2)}, u32[]{:S(2)}) async-start(f32[8,1,512]{2,1,0:T(1,128)} %copy.19), calls=%async_computation | async-start | bytes 32768 | tf_op jit(solution)/shard_map/all_to_all | solution.py:575
  59.9 6.6 %all-to-all-done = f32[8,1,512]{2,1,0:T(1,128)S(1)} async-done(((f32[8,1,512]{2,1,0:T(1,128)}), f32[8,1,512]{2,1,0:T(1,128)S(1)}, u32[]{:S(2)}, u32[]{:S(2)}) %all-to-all-start) | async-done | bytes 16416 | tf_op jit(solution)/shard_map/all_to_all | solution.py:575
  66.5 0.6 copy.22
  67.2 13.5 %head_grad.1 = (bf16[800,176]{1,0:T(8,128)(2,1)}, f32[176,1152]{1,0:T(8,128)}, f32[1,1152]{1,0:T(1,128)}) custom-call(s32[1]{0:T(128)} %bitcast.2.which_ref, f32[8,512]{1,0:T(8,128)} %bitcast.48, bf16[800,176]{1,0:T(8,128)(2,1)} %get-tuple-element.25.block_in, bf16[800,1152]{1,0:T(8,128)(2,1)} %get-tuple-element.26.gated_in, ...), custom_call_target="tpu_custom_call" | custom-call | tf_op jit(solution)/shard_map/head_grad/pallas_call | solution.py:580
  80.6 8.1 %psum.15.gate_grad_ref = f32[1,1152]{1,0:T(1,128)} all-reduce(f32[1,1152]{1,0:T(1,128)} %get-tuple-element.27), channel_id=1, replica_groups=mesh['pipe'=2,'x'=4,'y'=4,'core'=2,'space'=4] {'space'}, use_global_device_ids=true, to_apply=%region_1.2 | all-reduce | flops 1152 | bytes 9216 | tf_op jit(solution)/shard_map/psum | solution.py:602
  88.7 25.7 %depthwise_grad.1 = f32[512,1152]{1,0:T(8,128)} custom-call(s32[1]{0:T(128)} %bitcast.1.space_ref, f32[1,1152]{1,0:T(1,128)} %psum.15.gate_grad_ref, f32[1,1152]{1,0:T(1,128)} %psum.14.squeeze_ref, f32[48,1152]{1,0:T(8,128)} %get-tuple-element.40.reduce_ref, f32[48,1152]{1,0:T(8,128)} %get-tuple-element.39.excite_ref, ...), custom_call_target="tpu_custom_call" | custom-call | tf_op jit(solution)/shard_map/depthwise_grad/pallas_call | solution.py:608
  114.4 1.5 dynamic-slice_bitcast_fusion
  116.0 6.8 %collective-permute-start.2 = (f32[16,16,1152]{2,1,0:T(8,128)S(1)}, f32[16,16,1152]{2,1,0:T(8,128)}, u32[]{:S(2)}, u32[]{:S(2)}) collective-permute-start(f32[16,16,1152]{2,1,0:T(8,128)S(1)} %dynamic-slice_bitcast_fusion), channel_id=1, source_target_pairs={{0,4},{4,0},{1,5},{5,1},{2,6},{6,2},{3,7},{7,3},{8,12},{12,8},{9,1... | collective-permute-start | bytes 3538952 | tf_op jit(solution)/shard_map/ppermute | solution.py:641
  122.7 2.6 %collective-permute-done.2 = f32[16,16,1152]{2,1,0:T(8,128)} collective-permute-done((f32[16,16,1152]{2,1,0:T(8,128)S(1)}, f32[16,16,1152]{2,1,0:T(8,128)}, u32[]{:S(2)}, u32[]{:S(2)}) %collective-permute-start.2) | collective-permute-done | bytes 1179680 | tf_op jit(solution)/shard_map/ppermute | solution.py:641
  125.3 1.4 bitcast_add_fusion
  126.7 24.1 %all_to_all.21 = f32[16,16,1152]{2,1,0:T(8,128)S(1)} all-to-all(f32[16,16,1152]{2,1,0:T(8,128)S(1)} %bitcast_add_fusion), channel_id=1, replica_groups=mesh['pipe'=2,'x'=4,'y'=4,'core'=2,'space'=4] {'x','y'}, dimensions={0} | all-to-all | bytes 2359296 | tf_op jit(solution)/shard_map/all_to_all | solution.py:640
  150.9 0.1 reduce_sum.9
  150.9 2.1 %collective-permute-start.3 = (f32[16,1152]{1,0:T(8,128)S(1)}, f32[16,1152]{1,0:T(8,128)S(1)}, u32[]{:S(2)}, u32[]{:S(2)}) collective-permute-start(f32[16,1152]{1,0:T(8,128)S(1)} %reduce_sum.9), channel_id=1, source_target_pairs={{0,1},{1,0},{2,3},{3,2},{4,5},{5,4},{6,7},{7,6},{8,9},{9,8},{10,11... | collective-permute-start | bytes 221192 | tf_op jit(solution)/shard_map/ppermute | solution.py:645
  153.0 2.1 %collective-permute-done.3 = f32[16,1152]{1,0:T(8,128)S(1)} collective-permute-done((f32[16,1152]{1,0:T(8,128)S(1)}, f32[16,1152]{1,0:T(8,128)S(1)}, u32[]{:S(2)}, u32[]{:S(2)}) %collective-permute-start.3) | collective-permute-done | bytes 73760 | tf_op jit(solution)/shard_map/ppermute | solution.py:645
  155.1 4.1 %collective-permute-start.4 = (f32[16,1152]{1,0:T(8,128)S(1)}, f32[16,1152]{1,0:T(8,128)S(1)}, u32[]{:S(2)}, u32[]{:S(2)}) collective-permute-start(f32[16,1152]{1,0:T(8,128)S(1)} %add.34), channel_id=1, source_target_pairs={{0,2},{1,3},{2,0},{3,1},{4,6},{5,7},{6,4},{7,5},{8,10},{9,11},{10,... | collective-permute-start | bytes 221192 | tf_op jit(solution)/shard_map/ppermute | solution.py:645
  159.2 3.2 %collective-permute-done.4 = f32[16,1152]{1,0:T(8,128)S(1)} collective-permute-done((f32[16,1152]{1,0:T(8,128)S(1)}, f32[16,1152]{1,0:T(8,128)S(1)}, u32[]{:S(2)}, u32[]{:S(2)}) %collective-permute-start.4) | collective-permute-done | bytes 73760 | tf_op jit(solution)/shard_map/ppermute | solution.py:645
  162.5 0.1 broadcast_in_dim.2
  162.5 17.3 %all_to_all.22 = f32[16,16,1152]{2,1,0:T(8,128)S(1)} all-to-all(f32[16,16,1152]{2,1,0:T(8,128)S(1)} %broadcast_in_dim.2), channel_id=1, replica_groups=mesh['pipe'=2,'x'=4,'y'=4,'core'=2,'space'=4] {'x','y'}, dimensions={0} | all-to-all | bytes 2359296 | tf_op jit(solution)/shard_map/all_to_all | solution.py:647
  179.8 5.4 %collective-permute-start.5 = (f32[16,16,1152]{2,1,0:T(8,128)S(1)}, f32[16,16,1152]{2,1,0:T(8,128)S(1)}, u32[]{:S(2)}, u32[]{:S(2)}) collective-permute-start(f32[16,16,1152]{2,1,0:T(8,128)S(1)} %all_to_all.22), channel_id=1, source_target_pairs={{0,4},{4,0},{1,5},{5,1},{2,6},{6,2},{3,7},{7,3},{8,12},{12,8},{9,1... | collective-permute-start | bytes 3538952 | tf_op jit(solution)/shard_map/ppermute | solution.py:648
  185.2 2.5 %collective-permute-done.5 = f32[16,16,1152]{2,1,0:T(8,128)S(1)} collective-permute-done((f32[16,16,1152]{2,1,0:T(8,128)S(1)}, f32[16,16,1152]{2,1,0:T(8,128)S(1)}, u32[]{:S(2)}, u32[]{:S(2)}) %collective-permute-start.5) | collective-permute-done | bytes 1179680 | tf_op jit(solution)/shard_map/ppermute | solution.py:648
  187.7 1.0 copy-done.3
  188.7 3.0 %unpack.1 = (f32[1,176,1056]{2,1,0:T(8,128)}, f32[5,5,1,1056]{3,2,1,0:T(1,128)}, f32[44,1,1056]{2,1,0:T(1,128)}, f32[44,1,1056]{2,1,0:T(1,128)}, f32[1,176,1056]{2,1,0:T(8,128)}) custom-call(s32[1]{0:T(128)} %bitcast.core_ref, f32[256,1152]{1,0:T(8,128)} %bitcast.42, f32[256,1152]{1,0:T(8,128)} %bitcast.44), custom_call_target="tpu_custom_call" | custom-call | tf_op jit(solution)/shard_map/unpack/pallas_call | solution.py:649
  (13 shorter events, 0.1 us)
Async XLA Ops:
  0.6 8.5 %copy-start.4 = (bf16[1,176,1056]{2,1,0:T(8,128)(2,1)S(1)}, bf16[1,176,1056]{2,1,0:T(8,128)(2,1)}, u32[]{:S(2)}) copy-start(bf16[1,176,1056]{2,1,0:T(8,128)(2,1)} %param.9) | copy-start | bytes 1115140
  0.6 8.6 %copy-start.10 = (bf16[1,5,5,1056]{3,2,1,0:T(8,128)(2,1)S(1)}, bf16[1,5,5,1056]{3,2,1,0:T(8,128)(2,1)}, u32[]{:S(2)}) copy-start(bf16[1,5,5,1056]{3,2,1,0:T(8,128)(2,1)} %param.10) | copy-start | bytes 158404
  0.7 8.7 %copy-start.7 = (bf16[1,1056,44]{1,2,0:T(8,128)(2,1)S(1)}, bf16[1,1056,44]{1,2,0:T(8,128)(2,1)}, u32[]{:S(2)}) copy-start(bf16[1,1056,44]{1,2,0:T(8,128)(2,1)} %param.11) | copy-start | bytes 278788
  0.7 8.7 %copy-start.6 = (bf16[1,44,1056]{2,1,0:T(8,128)(2,1)S(1)}, bf16[1,44,1056]{2,1,0:T(8,128)(2,1)}, u32[]{:S(2)}) copy-start(bf16[1,44,1056]{2,1,0:T(8,128)(2,1)} %param.12) | copy-start | bytes 278788
  2.0 9.6 %copy-start.2 = (bf16[1,1,8,100,176]{4,3,2,1,0:T(8,128)(2,1)}, bf16[1,1,8,100,176]{4,3,2,1,0:T(8,128)(2,1)S(1)}, u32[]{:S(2)}) copy-start(bf16[1,1,8,100,176]{4,3,2,1,0:T(8,128)(2,1)S(1)} %copy.16) | copy-start | bytes 844804
  2.0 10.4 %collective-permute-start = (bf16[2,100,176]{2,1,0:T(8,128)(2,1)S(1)}, bf16[2,100,176]{2,1,0:T(8,128)(2,1)S(1)}, u32[]{:S(2)}, u32[]{:S(2)}) collective-permute-start(bf16[2,100,176]{2,1,0:T(8,128)(2,1)S(1)} %get-tuple-element.38), channel_id=1, source_target_pairs={{0,1},{1,2},{2,3},{4,5},{5,6},{6,7},{8,9},{9,10},{10,11},{12,13},{... | collective-permute-start | bytes 211208 | tf_op jit(solution)/shard_map/ppermute | solution.py:509
  7.7 3.9 %copy-start.5 = (bf16[1,1056,176]{1,2,0:T(8,128)(2,1)S(1)}, bf16[1,1056,176]{1,2,0:T(8,128)(2,1)}, u32[]{:S(2)}) copy-start(bf16[1,1056,176]{1,2,0:T(8,128)(2,1)} %param.13) | copy-start | bytes 1115140
  7.7 11.5 %collective-permute-start.1 = (bf16[2,100,176]{2,1,0:T(8,128)(2,1)S(1)}, bf16[2,100,176]{2,1,0:T(8,128)(2,1)S(1)}, u32[]{:S(2)}, u32[]{:S(2)}) collective-permute-start(bf16[2,100,176]{2,1,0:T(8,128)(2,1)S(1)} %get-tuple-element.37), channel_id=1, source_target_pairs={{1,0},{2,1},{3,2},{5,4},{6,5},{7,6},{9,8},{10,9},{11,10},{13,12},{... | collective-permute-start | bytes 211208 | tf_op jit(solution)/shard_map/ppermute | solution.py:510
  12.4 6.8 %copy-start.8 = (bf16[2,100,176]{2,1,0:T(8,128)(2,1)}, bf16[2,100,176]{2,1,0:T(8,128)(2,1)S(1)}, u32[]{:S(2)}) copy-start(bf16[2,100,176]{2,1,0:T(8,128)(2,1)S(1)} %collective-permute-done.before_ref) | copy-start | bytes 211204
  19.2 0.6 copy-start.9
  55.4 11.2 %all-to-all-start = ((f32[8,1,512]{2,1,0:T(1,128)}), f32[8,1,512]{2,1,0:T(1,128)S(1)}, u32[]{:S(2)}, u32[]{:S(2)}) async-start(f32[8,1,512]{2,1,0:T(1,128)} %copy.19), calls=%async_computation | async-start | bytes 32768 | tf_op jit(solution)/shard_map/all_to_all | solution.py:575
  114.4 10.9 %copy-start = (f32[512,1152]{1,0:T(8,128)S(1)}, f32[512,1152]{1,0:T(8,128)}, u32[]{:S(2)}) copy-start(f32[512,1152]{1,0:T(8,128)} %depthwise_grad.1) | copy-start | bytes 7077892
  116.0 9.4 %collective-permute-start.2 = (f32[16,16,1152]{2,1,0:T(8,128)S(1)}, f32[16,16,1152]{2,1,0:T(8,128)}, u32[]{:S(2)}, u32[]{:S(2)}) collective-permute-start(f32[16,16,1152]{2,1,0:T(8,128)S(1)} %dynamic-slice_bitcast_fusion), channel_id=1, source_target_pairs={{0,4},{4,0},{1,5},{5,1},{2,6},{6,2},{3,7},{7,3},{8,12},{12,8},{9,1... | collective-permute-start | bytes 3538952 | tf_op jit(solution)/shard_map/ppermute | solution.py:641
  150.9 4.2 %collective-permute-start.3 = (f32[16,1152]{1,0:T(8,128)S(1)}, f32[16,1152]{1,0:T(8,128)S(1)}, u32[]{:S(2)}, u32[]{:S(2)}) collective-permute-start(f32[16,1152]{1,0:T(8,128)S(1)} %reduce_sum.9), channel_id=1, source_target_pairs={{0,1},{1,0},{2,3},{3,2},{4,5},{5,4},{6,7},{7,6},{8,9},{9,8},{10,11... | collective-permute-start | bytes 221192 | tf_op jit(solution)/shard_map/ppermute | solution.py:645
  155.1 7.3 %collective-permute-start.4 = (f32[16,1152]{1,0:T(8,128)S(1)}, f32[16,1152]{1,0:T(8,128)S(1)}, u32[]{:S(2)}, u32[]{:S(2)}) collective-permute-start(f32[16,1152]{1,0:T(8,128)S(1)} %add.34), channel_id=1, source_target_pairs={{0,2},{1,3},{2,0},{3,1},{4,6},{5,7},{6,4},{7,5},{8,10},{9,11},{10,... | collective-permute-start | bytes 221192 | tf_op jit(solution)/shard_map/ppermute | solution.py:645
  179.8 7.9 %copy-start.1 = (f32[16,16,1152]{2,1,0:T(8,128)}, f32[16,16,1152]{2,1,0:T(8,128)S(1)}, u32[]{:S(2)}) copy-start(f32[16,16,1152]{2,1,0:T(8,128)S(1)} %all_to_all.22) | copy-start | bytes 3538948
  179.8 7.9 %collective-permute-start.5 = (f32[16,16,1152]{2,1,0:T(8,128)S(1)}, f32[16,16,1152]{2,1,0:T(8,128)S(1)}, u32[]{:S(2)}, u32[]{:S(2)}) collective-permute-start(f32[16,16,1152]{2,1,0:T(8,128)S(1)} %all_to_all.22), channel_id=1, source_target_pairs={{0,4},{4,0},{1,5},{5,1},{2,6},{6,2},{3,7},{7,3},{8,12},{12,8},{9,1... | collective-permute-start | bytes 3538952 | tf_op jit(solution)/shard_map/ppermute | solution.py:648
  187.7 1.0 copy-start.3

commit v4 on v3

--- a/solution.py
+++ b/solution.py
@@ -12,7 +12,6 @@
 LANES = 128
 BAND = 384
 HEAD_CHUNK = 512
-UNROLL = 2
 STRIP = 50
 WIDE = 100
 TAPS = 50
@@ -33,10 +32,10 @@
     return made
 
 
-def chunks(width, chunk, work):
+def chunks(width, chunk, unroll, work):
     whole = width // chunk
 
-    @pl.loop(0, whole, unroll=UNROLL)
+    @pl.loop(0, whole, unroll=unroll)
     def each(part):
         work(pl.multiple_of(part * chunk, chunk), chunk)
 
@@ -212,16 +211,15 @@
         sums[:, lanes] = jnp.sum(act.reshape(cells // 8, 8, count), axis=0)
 
     head_copy.wait()
-    chunks(head_ref.shape[1], HEAD_CHUNK, head)
+    chunks(head_ref.shape[1], HEAD_CHUNK, 5, head)
     class_copy.wait()
     pooled = sums[...]
     high = pooled.astype(bf16).astype(f32)
     both = jnp.concatenate([high, pooled - high], axis=0).astype(bf16)
     partial = jnp.sum(contract(both, class_ref[...], 1, 1), axis=0, keepdims=True)
     logits_ref[...] = jnp.zeros_like(logits_ref)
-    logits_ref[:, :classes] = jnp.broadcast_to(
-        partial / cell_total, (logits_ref.shape[0], classes)
-    )
+    for rank in range(logits_ref.shape[0]):
+        logits_ref[rank, :, :classes] = partial / cell_total
     send.wait()
 
 
@@ -241,11 +239,12 @@
     classes = class_ref.shape[0]
     total[...] = jnp.zeros_like(total)
 
-    rows = logits_ref[...]
-    network = lax.broadcasted_iota(jnp.int32, rows.shape, 0) % 2
-    valid = lax.broadcasted_iota(jnp.int32, (1, rows.shape[1]), 1) < classes
-    teacher = jnp.sum(jnp.where(network == 0, rows, 0.0), axis=0, keepdims=True)
-    student = jnp.sum(jnp.where(network == 1, rows, 0.0), axis=0, keepdims=True)
+    ranks, wide = logits_ref.shape[0], logits_ref.shape[2]
+    valid = lax.broadcasted_iota(jnp.int32, (1, wide), 1) < classes
+    teacher, student = logits_ref[0], logits_ref[1]
+    for rank in range(2, ranks, 2):
+        teacher = teacher + logits_ref[rank]
+        student = student + logits_ref[rank + 1]
     exp_teacher = jnp.where(valid, jnp.exp(teacher), 0.0)
     prob = exp_teacher / jnp.sum(exp_teacher, axis=1, keepdims=True)
     log_sum = jnp.log(
@@ -257,7 +256,7 @@
     student_grad = loss_scale * (jnp.exp(logprob) - prob)
     grad = jnp.where(which_ref[0] == 0, teacher_grad, student_grad)
     grad = jnp.where(valid, grad, 0.0)
-    grad = jnp.broadcast_to(grad, (16, rows.shape[1])).astype(bf16)[:, :classes]
+    grad = jnp.broadcast_to(grad, (16, wide)).astype(bf16)[:, :classes]
     class_copy.wait()
     pooled[...] = contract(grad, class_ref[...], 1, 0)[:1] * (0.5 / (4 * cells))
 
@@ -272,7 +271,7 @@
 
     block_copy.wait()
     head_copy.wait()
-    chunks(head_ref.shape[1], HEAD_CHUNK, head)
+    chunks(head_ref.shape[1], HEAD_CHUNK, 10, head)
     grad_block = total[...]
     grad_ref[...] = grad_block.astype(bf16)
     gated_copy.wait()
@@ -465,15 +464,19 @@
         if start < half_rows:
             end = min(stop, half_rows)
             pieces.append(
-                jnp.where(core_ref[0] == 0, own_ref[start:end, :], other_ref[start:end, :])
+                jnp.where(
+                    core_ref[0] == 0,
+                    own_ref[start:end, :].astype(f32),
+                    other_ref[start:end, :].astype(f32),
+                )
             )
         if stop > half_rows:
             begin = max(start, half_rows)
             pieces.append(
                 jnp.where(
                     core_ref[0] == 0,
-                    other_ref[begin - half_rows : stop - half_rows, :],
-                    own_ref[begin - half_rows : stop - half_rows, :],
+                    other_ref[begin - half_rows : stop - half_rows, :].astype(f32),
+                    own_ref[begin - half_rows : stop - half_rows, :].astype(f32),
                 )
             )
         return pieces[0] if len(pieces) == 1 else jnp.concatenate(pieces, axis=0)
@@ -553,7 +556,7 @@
         in_specs=[ANY] + [VMEM] * 3 + [ANY] * 4,
         out_specs=[VMEM, ANY, VMEM],
         out_shape=[
-            jax.ShapeDtypeStruct((ranks, up_to(classes, LANES)), f32),
+            jax.ShapeDtypeStruct((ranks, 1, up_to(classes, LANES)), f32),
             jax.ShapeDtypeStruct((cells, broad), bf16),
             jax.ShapeDtypeStruct((cells, channels), bf16),
         ],
@@ -637,10 +640,9 @@
     swap = [(0, 1), (1, 0)]
     keep = lax.dynamic_index_in_dim(halves, core, 0, False)
     send = lax.dynamic_index_in_dim(halves, 1 - core, 0, False)
-    pieces = lax.all_to_all(
-        keep + lax.ppermute(send, "core", swap), ("x", "y"), 0, 0, tiled=True
-    )
-    piece = jnp.sum(pieces, axis=0)
+    both = (keep + lax.ppermute(send, "core", swap)).astype(bf16)
+    pieces = lax.all_to_all(both, ("x", "y"), 0, 0, tiled=True)
+    piece = jnp.sum(pieces.astype(f32), axis=0)
     for step in (1, 2):
         piece = piece + lax.ppermute(piece, "space", [(i, i ^ step) for i in range(space)])
     copies = jnp.broadcast_to(piece[None], pieces.shape)

time: 192 us -> 181 us (0.943)
  blocking collectives: 60.5 us -> 54.2 us
  Pallas kernels: 65.3 us -> 62.5 us
    all_to_all x1, blocking collectives: 24.1 us -> 18 us  [shards(): pieces = lax.all_to_all(both, ('x', 'y'), 0, 0, tiled=True)]
    pallas_call x1, Pallas kernels: 13.5 us -> 11.3 us  [shards(): pl.pallas_call(head_grad_kernel, in_specs=[SMEM, VMEM] + [ANY] * 5, out_s...]
where the time goes in v4:
time: 181 us
  Pallas kernels  62.5 us (35%)
  blocking collectives  54.2 us (30%)
  starting transfers between devices  29.7 us (16%)
  waiting for transfers between devices  24 us (13%)
  local copies, waits for them, and re-layouts  7.85 us (4%)
    pallas_call x1, Pallas kernels, shards(): pl.pallas_call(backward_kernel, in_specs=[SMEM] + [VMEM] * 4 + [ANY] * 3...  25.6 us
    all_to_all x1, blocking collectives, shards(): pieces = lax.all_to_all(both, ('x', 'y'), 0, 0, tiled=True)  18 us
    all_to_all x1, blocking collectives, shards(): gathered = lax.all_to_all(copies, ('x', 'y'), 0, 0, tiled=True)  17 us
    pallas_call x1, Pallas kernels, shards(): pl.pallas_call(forward_kernel, in_specs=[VMEM] * 5, out_specs=[ANY] * 4 +...  12.7 us
    pallas_call x1, Pallas kernels, shards(): pl.pallas_call(head_grad_kernel, in_specs=[SMEM, VMEM] + [ANY] * 5, out_s...  11.3 us
    psum x1, blocking collectives, shards(): squeeze = lax.psum(squeeze, 'space')  11 us
    pallas_call x1, Pallas kernels, shards(): pl.pallas_call(head_kernel, in_specs=[ANY] + [VMEM] * 3 + [ANY] * 4, out_...  9.94 us
    psum x1, blocking collectives, shards(): gate_grad = lax.psum(gate_grad, 'space')  8.1 us
  transfers between devices with their start and end apart: 7, of which 6 were waited for; matrix products, arithmetic and copies ran while one was open for 2% of the time, Pallas kernels for 0%

profile of v4, /device:TPU:1, one launch (start us, length us, event | category | flops | bytes accessed | tf_op | source)
XLA Modules:
  0.0 180.9 jit_solution(3419212161249639373)
XLA Ops:
  0.6 0.0 copy-start.4
  0.6 0.0 copy-start.10
  0.7 0.0 copy-start.7
  0.7 0.0 copy-start.6
  0.7 1.3 copy.13
  2.0 5.7 %collective-permute-start = (bf16[2,100,176]{2,1,0:T(8,128)(2,1)S(1)}, bf16[2,100,176]{2,1,0:T(8,128)(2,1)S(1)}, u32[]{:S(2)}, u32[]{:S(2)}) collective-permute-start(bf16[2,100,176]{2,1,0:T(8,128)(2,1)S(1)} %get-tuple-element.38), channel_id=1, source_target_pairs={{0,1},{1,2},{2,3},{4,5},{5,6},{6,7},{8,9},{9,10},{10,11},{12,13},{... | collective-permute-start | bytes 211208 | tf_op jit(solution)/shard_map/ppermute | solution.py:512
  7.7 0.0 copy-start.5
  7.7 1.4 collective-permute-start.1
  9.2 0.0 copy-done.4
  9.2 0.0 copy-done.10
  9.3 0.1 convert_element_type.29
  9.3 0.0 copy-done.7
  9.3 0.0 copy-done.6
  9.3 0.9 pad_convert_fusion
  10.2 0.7 pad_convert_fusion.2.depth_ref
  10.9 0.8 pad.24.expand_ref.expand_in
  11.6 0.0 copy-done.2
  11.6 0.0 copy-done.5
  11.6 0.8 pad.31.project_in
  12.4 0.0 collective-permute-done.before_ref
  12.4 6.8 %collective-permute-done.1.after_ref = bf16[2,100,176]{2,1,0:T(8,128)(2,1)S(1)} collective-permute-done((bf16[2,100,176]{2,1,0:T(8,128)(2,1)S(1)}, bf16[2,100,176]{2,1,0:T(8,128)(2,1)S(1)}, u32[]{:S(2)}, u32[]{:S(2)}) %collective-permute-start.1) | collective-permute-done | bytes 70432 | tf_op jit(solution)/shard_map/ppermute | solution.py:513
  19.2 0.6 copy-done.9
  19.9 12.7 %expand_depthwise.1 = (bf16[1600,176]{1,0:T(8,128)(2,1)}, bf16[176,1600]{1,0:T(8,128)(2,1)}, bf16[800,176]{1,0:T(8,128)(2,1)}, f32[800,1152]{1,0:T(8,128)}, f32[1,1152]{1,0:T(1,128)}) custom-call(bf16[8,100,176]{2,1,0:T(8,128)(2,1)} %bitcast.41, bf16[2,100,176]{2,1,0:T(8,128)(2,1)} %copy-done.8, bf16[2,100,176]{2,1,0:T(8,128)(2,1)} %copy-done.9, ...), custom_call_target="tpu_custom_call" | custom-call | tf_op jit(solution)/shard_map/expand_depthwise/pallas_call | solution.py:527
  32.6 11.0 %psum.14.squeeze_ref = f32[1,1152]{1,0:T(1,128)} all-reduce(f32[1,1152]{1,0:T(1,128)} %get-tuple-element.22), channel_id=1, replica_groups=mesh['pipe'=2,'x'=4,'y'=4,'core'=2,'space'=4] {'space'}, use_global_device_ids=true, to_apply=%region_0.1 | all-reduce | flops 1152 | bytes 9216 | tf_op jit(solution)/shard_map/psum | solution.py:551
  43.6 9.9 %project_head.1 = (f32[8,1,512]{2,1,0:T(1,128)}, bf16[800,1152]{1,0:T(8,128)(2,1)}, bf16[800,176]{1,0:T(8,128)(2,1)}) custom-call(f32[800,1152]{1,0:T(8,128)} %get-tuple-element.21.half_in, f32[1,1152]{1,0:T(1,128)} %psum.14.squeeze_ref, f32[48,1152]{1,0:T(8,128)} %get-tuple-element.40.reduce_ref, f32[48,1152]{1,0:T(8,128)} %get-tuple-element.39.excite_ref, ...), custom_call_target="tpu_custom_call" | custom-call | tf_op jit(solution)/shard_map/project_head/pallas_call | solution.py:554
  53.5 4.6 %all-to-all-start = ((f32[8,1,512]{2,1,0:T(1,128)}), f32[8,1,512]{2,1,0:T(1,128)S(1)}, u32[]{:S(2)}, u32[]{:S(2)}) async-start(f32[8,1,512]{2,1,0:T(1,128)} %get-tuple-element.24), calls=%async_computation | async-start | bytes 32768 | tf_op jit(solution)/shard_map/all_to_all | solution.py:578
  58.1 6.6 %all-to-all-done.logits_ref = f32[8,1,512]{2,1,0:T(1,128)S(1)} async-done(((f32[8,1,512]{2,1,0:T(1,128)}), f32[8,1,512]{2,1,0:T(1,128)S(1)}, u32[]{:S(2)}, u32[]{:S(2)}) %all-to-all-start) | async-done | bytes 16416 | tf_op jit(solution)/shard_map/all_to_all | solution.py:578
  64.7 0.6 copy-done.11
  65.3 11.3 %head_grad.1 = (bf16[800,176]{1,0:T(8,128)(2,1)}, f32[176,1152]{1,0:T(8,128)}, f32[1,1152]{1,0:T(1,128)}) custom-call(s32[1]{0:T(128)} %bitcast.2.which_ref, f32[8,1,512]{2,1,0:T(1,128)} %copy-done.11, bf16[800,176]{1,0:T(8,128)(2,1)} %get-tuple-element.25.block_in, bf16[800,1152]{1,0:T(8,128)(2,1)} %get-tuple-element.26.gated_in, ...), custom_call_target="tpu_custom_call" | custom-call | tf_op jit(solution)/shard_map/head_grad/pallas_call | solution.py:583
  76.7 8.1 %psum.15.gate_grad_ref = f32[1,1152]{1,0:T(1,128)} all-reduce(f32[1,1152]{1,0:T(1,128)} %get-tuple-element.27), channel_id=1, replica_groups=mesh['pipe'=2,'x'=4,'y'=4,'core'=2,'space'=4] {'space'}, use_global_device_ids=true, to_apply=%region_1.2 | all-reduce | flops 1152 | bytes 9216 | tf_op jit(solution)/shard_map/psum | solution.py:605
  84.8 25.6 %depthwise_grad.1 = f32[512,1152]{1,0:T(8,128)} custom-call(s32[1]{0:T(128)} %bitcast.1.space_ref, f32[1,1152]{1,0:T(1,128)} %psum.15.gate_grad_ref, f32[1,1152]{1,0:T(1,128)} %psum.14.squeeze_ref, f32[48,1152]{1,0:T(8,128)} %get-tuple-element.40.reduce_ref, f32[48,1152]{1,0:T(8,128)} %get-tuple-element.39.excite_ref, ...), custom_call_target="tpu_custom_call" | custom-call | tf_op jit(solution)/shard_map/depthwise_grad/pallas_call | solution.py:611
  110.4 2.5 %dynamic-slice_bitcast_fusion = f32[16,16,1152]{2,1,0:T(8,128)} fusion(f32[2,16,16,1152]{3,2,1,0:T(8,128)} %bitcast.36, s32[]{:T(128)S(6)} %select_n.8), kind=kLoop, calls=%fused_computation.3 | loop fusion | bytes 2359300 | tf_op jit(solution)/shard_map/jit(dynamic_index_in_dim)/squeeze | solution.py:642
  112.9 6.5 %collective-permute-start.2 = (f32[16,16,1152]{2,1,0:T(8,128)}, f32[16,16,1152]{2,1,0:T(8,128)S(1)}, u32[]{:S(2)}, u32[]{:S(2)}) collective-permute-start(f32[16,16,1152]{2,1,0:T(8,128)} %dynamic-slice_bitcast_fusion), channel_id=1, source_target_pairs={{0,4},{4,0},{1,5},{5,1},{2,6},{6,2},{3,7},{7,3},{8,12},{12,8},{9,1... | collective-permute-start | bytes 3538952 | tf_op jit(solution)/shard_map/ppermute | solution.py:643
  119.5 2.7 %collective-permute-done.2 = f32[16,16,1152]{2,1,0:T(8,128)S(1)} collective-permute-done((f32[16,16,1152]{2,1,0:T(8,128)}, f32[16,16,1152]{2,1,0:T(8,128)S(1)}, u32[]{:S(2)}, u32[]{:S(2)}) %collective-permute-start.2) | collective-permute-done | bytes 1179680 | tf_op jit(solution)/shard_map/ppermute | solution.py:643
  122.1 0.0 copy-done
  122.1 0.1 fusion
  122.3 18.0 %all_to_all.15 = bf16[16,16,1152]{2,1,0:T(8,128)(2,1)S(1)} all-to-all(bf16[16,16,1152]{2,1,0:T(8,128)(2,1)S(1)} %fusion), channel_id=1, replica_groups=mesh['pipe'=2,'x'=4,'y'=4,'core'=2,'space'=4] {'x','y'}, dimensions={0} | all-to-all | bytes 1179648 | tf_op jit(solution)/shard_map/all_to_all | solution.py:644
  140.3 0.1 convert_reduce_fusion
  140.4 2.0 %collective-permute-start.3 = (f32[16,1152]{1,0:T(8,128)S(1)}, f32[16,1152]{1,0:T(8,128)S(1)}, u32[]{:S(2)}, u32[]{:S(2)}) collective-permute-start(f32[16,1152]{1,0:T(8,128)S(1)} %convert_reduce_fusion), channel_id=1, source_target_pairs={{0,1},{1,0},{2,3},{3,2},{4,5},{5,4},{6,7},{7,6},{8,9},{9,8},{10,11... | collective-permute-start | bytes 221192 | tf_op jit(solution)/shard_map/ppermute | solution.py:647
  142.4 2.2 %collective-permute-done.3 = f32[16,1152]{1,0:T(8,128)S(1)} collective-permute-done((f32[16,1152]{1,0:T(8,128)S(1)}, f32[16,1152]{1,0:T(8,128)S(1)}, u32[]{:S(2)}, u32[]{:S(2)}) %collective-permute-start.3) | collective-permute-done | bytes 73760 | tf_op jit(solution)/shard_map/ppermute | solution.py:647
  144.6 4.1 %collective-permute-start.4 = (f32[16,1152]{1,0:T(8,128)S(1)}, f32[16,1152]{1,0:T(8,128)S(1)}, u32[]{:S(2)}, u32[]{:S(2)}) collective-permute-start(f32[16,1152]{1,0:T(8,128)S(1)} %add.34), channel_id=1, source_target_pairs={{0,2},{1,3},{2,0},{3,1},{4,6},{5,7},{6,4},{7,5},{8,10},{9,11},{10,... | collective-permute-start | bytes 221192 | tf_op jit(solution)/shard_map/ppermute | solution.py:647
  148.6 3.2 %collective-permute-done.4 = f32[16,1152]{1,0:T(8,128)S(1)} collective-permute-done((f32[16,1152]{1,0:T(8,128)S(1)}, f32[16,1152]{1,0:T(8,128)S(1)}, u32[]{:S(2)}, u32[]{:S(2)}) %collective-permute-start.4) | collective-permute-done | bytes 73760 | tf_op jit(solution)/shard_map/ppermute | solution.py:647
  151.9 0.1 broadcast_in_dim.2
  152.0 17.0 %all_to_all.16 = f32[16,16,1152]{2,1,0:T(8,128)S(1)} all-to-all(f32[16,16,1152]{2,1,0:T(8,128)S(1)} %broadcast_in_dim.2), channel_id=1, replica_groups=mesh['pipe'=2,'x'=4,'y'=4,'core'=2,'space'=4] {'x','y'}, dimensions={0} | all-to-all | bytes 2359296 | tf_op jit(solution)/shard_map/all_to_all | solution.py:649
  169.0 5.4 %collective-permute-start.5 = (f32[16,16,1152]{2,1,0:T(8,128)S(1)}, f32[16,16,1152]{2,1,0:T(8,128)S(1)}, u32[]{:S(2)}, u32[]{:S(2)}) collective-permute-start(f32[16,16,1152]{2,1,0:T(8,128)S(1)} %all_to_all.16), channel_id=1, source_target_pairs={{0,4},{4,0},{1,5},{5,1},{2,6},{6,2},{3,7},{7,3},{8,12},{12,8},{9,1... | collective-permute-start | bytes 3538952 | tf_op jit(solution)/shard_map/ppermute | solution.py:650
  174.4 2.5 %collective-permute-done.5 = f32[16,16,1152]{2,1,0:T(8,128)S(1)} collective-permute-done((f32[16,16,1152]{2,1,0:T(8,128)S(1)}, f32[16,16,1152]{2,1,0:T(8,128)S(1)}, u32[]{:S(2)}, u32[]{:S(2)}) %collective-permute-start.5) | collective-permute-done | bytes 1179680 | tf_op jit(solution)/shard_map/ppermute | solution.py:650
  176.9 1.0 copy-done.3
  177.9 3.0 %unpack.1 = (f32[1,176,1056]{2,1,0:T(8,128)}, f32[5,5,1,1056]{3,2,1,0:T(1,128)}, f32[44,1,1056]{2,1,0:T(1,128)}, f32[44,1,1056]{2,1,0:T(1,128)}, f32[1,176,1056]{2,1,0:T(8,128)}) custom-call(s32[1]{0:T(128)} %bitcast.core_ref, f32[256,1152]{1,0:T(8,128)} %bitcast.40, f32[256,1152]{1,0:T(8,128)} %bitcast.42), custom_call_target="tpu_custom_call" | custom-call | tf_op jit(solution)/shard_map/unpack/pallas_call | solution.py:651
  (13 shorter events, 0.1 us)
Async XLA Ops:
  0.6 8.5 %copy-start.4 = (bf16[1,176,1056]{2,1,0:T(8,128)(2,1)S(1)}, bf16[1,176,1056]{2,1,0:T(8,128)(2,1)}, u32[]{:S(2)}) copy-start(bf16[1,176,1056]{2,1,0:T(8,128)(2,1)} %param.9) | copy-start | bytes 1115140
  0.6 8.6 %copy-start.10 = (bf16[1,5,5,1056]{3,2,1,0:T(8,128)(2,1)S(1)}, bf16[1,5,5,1056]{3,2,1,0:T(8,128)(2,1)}, u32[]{:S(2)}) copy-start(bf16[1,5,5,1056]{3,2,1,0:T(8,128)(2,1)} %param.10) | copy-start | bytes 158404
  0.7 8.7 %copy-start.7 = (bf16[1,1056,44]{1,2,0:T(8,128)(2,1)S(1)}, bf16[1,1056,44]{1,2,0:T(8,128)(2,1)}, u32[]{:S(2)}) copy-start(bf16[1,1056,44]{1,2,0:T(8,128)(2,1)} %param.11) | copy-start | bytes 278788
  0.7 8.7 %copy-start.6 = (bf16[1,44,1056]{2,1,0:T(8,128)(2,1)S(1)}, bf16[1,44,1056]{2,1,0:T(8,128)(2,1)}, u32[]{:S(2)}) copy-start(bf16[1,44,1056]{2,1,0:T(8,128)(2,1)} %param.12) | copy-start | bytes 278788
  2.0 9.7 %copy-start.2 = (bf16[1,1,8,100,176]{4,3,2,1,0:T(8,128)(2,1)}, bf16[1,1,8,100,176]{4,3,2,1,0:T(8,128)(2,1)S(1)}, u32[]{:S(2)}) copy-start(bf16[1,1,8,100,176]{4,3,2,1,0:T(8,128)(2,1)S(1)} %copy.13) | copy-start | bytes 844804
  2.0 10.4 %collective-permute-start = (bf16[2,100,176]{2,1,0:T(8,128)(2,1)S(1)}, bf16[2,100,176]{2,1,0:T(8,128)(2,1)S(1)}, u32[]{:S(2)}, u32[]{:S(2)}) collective-permute-start(bf16[2,100,176]{2,1,0:T(8,128)(2,1)S(1)} %get-tuple-element.38), channel_id=1, source_target_pairs={{0,1},{1,2},{2,3},{4,5},{5,6},{6,7},{8,9},{9,10},{10,11},{12,13},{... | collective-permute-start | bytes 211208 | tf_op jit(solution)/shard_map/ppermute | solution.py:512
  7.7 3.9 %copy-start.5 = (bf16[1,1056,176]{1,2,0:T(8,128)(2,1)S(1)}, bf16[1,1056,176]{1,2,0:T(8,128)(2,1)}, u32[]{:S(2)}) copy-start(bf16[1,1056,176]{1,2,0:T(8,128)(2,1)} %param.13) | copy-start | bytes 1115140
  7.7 11.5 %collective-permute-start.1 = (bf16[2,100,176]{2,1,0:T(8,128)(2,1)S(1)}, bf16[2,100,176]{2,1,0:T(8,128)(2,1)S(1)}, u32[]{:S(2)}, u32[]{:S(2)}) collective-permute-start(bf16[2,100,176]{2,1,0:T(8,128)(2,1)S(1)} %get-tuple-element.37), channel_id=1, source_target_pairs={{1,0},{2,1},{3,2},{5,4},{6,5},{7,6},{9,8},{10,9},{11,10},{13,12},{... | collective-permute-start | bytes 211208 | tf_op jit(solution)/shard_map/ppermute | solution.py:513
  12.4 6.8 %copy-start.8 = (bf16[2,100,176]{2,1,0:T(8,128)(2,1)}, bf16[2,100,176]{2,1,0:T(8,128)(2,1)S(1)}, u32[]{:S(2)}) copy-start(bf16[2,100,176]{2,1,0:T(8,128)(2,1)S(1)} %collective-permute-done.before_ref) | copy-start | bytes 211204
  19.2 0.6 copy-start.9
  53.5 11.2 %all-to-all-start = ((f32[8,1,512]{2,1,0:T(1,128)}), f32[8,1,512]{2,1,0:T(1,128)S(1)}, u32[]{:S(2)}, u32[]{:S(2)}) async-start(f32[8,1,512]{2,1,0:T(1,128)} %get-tuple-element.24), calls=%async_computation | async-start | bytes 32768 | tf_op jit(solution)/shard_map/all_to_all | solution.py:578
  64.7 0.6 copy-start.11
  110.4 11.8 %copy-start = (f32[512,1152]{1,0:T(8,128)S(1)}, f32[512,1152]{1,0:T(8,128)}, u32[]{:S(2)}) copy-start(f32[512,1152]{1,0:T(8,128)} %depthwise_grad.1) | copy-start | bytes 7077892
  112.9 9.2 %collective-permute-start.2 = (f32[16,16,1152]{2,1,0:T(8,128)}, f32[16,16,1152]{2,1,0:T(8,128)S(1)}, u32[]{:S(2)}, u32[]{:S(2)}) collective-permute-start(f32[16,16,1152]{2,1,0:T(8,128)} %dynamic-slice_bitcast_fusion), channel_id=1, source_target_pairs={{0,4},{4,0},{1,5},{5,1},{2,6},{6,2},{3,7},{7,3},{8,12},{12,8},{9,1... | collective-permute-start | bytes 3538952 | tf_op jit(solution)/shard_map/ppermute | solution.py:643
  140.4 4.2 %collective-permute-start.3 = (f32[16,1152]{1,0:T(8,128)S(1)}, f32[16,1152]{1,0:T(8,128)S(1)}, u32[]{:S(2)}, u32[]{:S(2)}) collective-permute-start(f32[16,1152]{1,0:T(8,128)S(1)} %convert_reduce_fusion), channel_id=1, source_target_pairs={{0,1},{1,0},{2,3},{3,2},{4,5},{5,4},{6,7},{7,6},{8,9},{9,8},{10,11... | collective-permute-start | bytes 221192 | tf_op jit(solution)/shard_map/ppermute | solution.py:647
  144.6 7.3 %collective-permute-start.4 = (f32[16,1152]{1,0:T(8,128)S(1)}, f32[16,1152]{1,0:T(8,128)S(1)}, u32[]{:S(2)}, u32[]{:S(2)}) collective-permute-start(f32[16,1152]{1,0:T(8,128)S(1)} %add.34), channel_id=1, source_target_pairs={{0,2},{1,3},{2,0},{3,1},{4,6},{5,7},{6,4},{7,5},{8,10},{9,11},{10,... | collective-permute-start | bytes 221192 | tf_op jit(solution)/shard_map/ppermute | solution.py:647
  169.0 7.9 %copy-start.1 = (f32[16,16,1152]{2,1,0:T(8,128)}, f32[16,16,1152]{2,1,0:T(8,128)S(1)}, u32[]{:S(2)}) copy-start(f32[16,16,1152]{2,1,0:T(8,128)S(1)} %all_to_all.16) | copy-start | bytes 3538948
  169.0 7.9 %collective-permute-start.5 = (f32[16,16,1152]{2,1,0:T(8,128)S(1)}, f32[16,16,1152]{2,1,0:T(8,128)S(1)}, u32[]{:S(2)}, u32[]{:S(2)}) collective-permute-start(f32[16,16,1152]{2,1,0:T(8,128)S(1)} %all_to_all.16), channel_id=1, source_target_pairs={{0,4},{4,0},{1,5},{5,1},{2,6},{6,2},{3,7},{7,3},{8,12},{12,8},{9,1... | collective-permute-start | bytes 3538952 | tf_op jit(solution)/shard_map/ppermute | solution.py:650
  176.9 1.0 copy-start.3

commit v5 on v4

--- a/solution.py
+++ b/solution.py
@@ -284,14 +284,20 @@
 
 
 def backward_kernel(
-    space_ref, gate_grad_ref, squeeze_ref, reduce_ref, excite_ref, cells_in, cells_t_in,
+    place_ref, gate_grad_ref, squeeze_ref, reduce_ref, excite_ref, cells_in, cells_t_in,
     expand_in, depth_ref, half_in, grad_in, project_in, project_grad_in,
+    keep_ref, send_ref,
     out_ref,
     cells_ref, cells_t_ref, expand_ref, half_ref, grad_ref, project_ref, gate_row, pool_row,
     expanded, slope, grad_depth, grad_expand, sems,
 ):
     channels = grad_in.shape[1]
-    depth_base = 2 * channels
+    peers, share, hidden = keep_ref.shape
+    half_rows = peers * share
+    depth_base = channels
+    excite_base = channels + depth_ref.shape[0]
+    project_base = half_rows
+    reduce_base = half_rows + channels
     arriving = started(
         (cells_in, cells_ref, sems.at[0]),
         (expand_in, expand_ref, sems.at[1]),
@@ -299,16 +305,15 @@
         (project_in, project_ref, sems.at[3]),
         (half_in, half_ref, sems.at[4]),
         (cells_t_in, cells_t_ref, sems.at[5]),
-        (project_grad_in, out_ref.at[channels:depth_base, :], sems.at[6]),
+        (project_grad_in, out_ref.at[project_base:reduce_base, :], sems.at[6]),
     )
     cells = half_ref.shape[0]
     columns = cells // 8
     reduced_rows = reduce_ref.shape[0]
     extent, margin = 5, 2
     cell_total = 4 * cells
-    excite_base = depth_base + up_to(extent * extent, 8)
-    reduce_base = excite_base + reduced_rows
-    end = reduce_base + reduced_rows
+    excite_end = excite_base + reduced_rows
+    reduce_end = reduce_base + reduced_rows
 
     squeeze = squeeze_ref[...] / cell_total
     reduced_in, reduced, gate = gate_of(squeeze, reduce_ref[...], excite_ref[...])
@@ -320,11 +325,12 @@
     back_pool = jnp.sum(reduce_ref[...] * grad_reduced, axis=0, keepdims=True)
     gate_row[...] = 0.25 * gate
     pool_row[...] = back_pool * (0.25 / cell_total)
-    once = jnp.where(space_ref[0] == 0, 1.0, 0.0)
-    out_ref[excite_base:reduce_base, :] = reduced * (grad_excite * once)
-    out_ref[reduce_base:end, :] = grad_reduced * (squeeze * once)
-    if end < out_ref.shape[0]:
-        out_ref[end:, :] = jnp.zeros((out_ref.shape[0] - end, out_ref.shape[1]), f32)
+    once = jnp.where(place_ref[0] == 0, 1.0, 0.0)
+    out_ref[excite_base:excite_end, :] = reduced * (grad_excite * once)
+    out_ref[reduce_base:reduce_end, :] = grad_reduced * (squeeze * once)
+    for first, last in ((excite_end, half_rows), (reduce_end, 2 * half_rows)):
+        if first < last:
+            out_ref[first:last, :] = jnp.zeros((last - first, out_ref.shape[1]), f32)
     edge = jnp.zeros((margin, 16, BAND), f32)
     expanded[:margin] = edge
     expanded[margin + columns :] = edge
@@ -341,6 +347,12 @@
             cells_ref, cells_t_ref, expand_ref, depth_ref, half_ref, grad_ref, project_ref,
             out_ref, gate_row, pool_row, expanded, slope, grad_depth, grad_expand,
         )
+
+    core = place_ref[1]
+    mine = pl.ds(pl.multiple_of(core * half_rows, half_rows), half_rows)
+    theirs = pl.ds(pl.multiple_of((1 - core) * half_rows, half_rows), half_rows)
+    keep_ref[...] = out_ref[mine, :][:, :hidden].reshape(keep_ref.shape)
+    send_ref[...] = out_ref[theirs, :][:, :hidden].astype(bf16).reshape(send_ref.shape)
 
 
 def backward_band(
@@ -449,49 +461,34 @@
 
 
 def unpack_kernel(
-    core_ref, own_ref, other_ref, expand_ref, depth_ref, reduce_ref, excite_ref, project_ref
+    core_ref, own_ref, other_ref,
+    expand_ref, depth_ref, reduce_ref, excite_ref, project_ref,
 ):
-    channels, hidden = expand_ref.shape[1:]
+    channels = expand_ref.shape[1]
     extent = depth_ref.shape[0]
     reduced = excite_ref.shape[0]
-    depth_base = 2 * channels
-    excite_base = depth_base + up_to(extent * extent, 8)
-    reduce_base = excite_base + up_to(reduced, 8)
-    half_rows = own_ref.shape[0]
-
-    def rows(start, stop):
-        pieces = []
-        if start < half_rows:
-            end = min(stop, half_rows)
-            pieces.append(
-                jnp.where(
-                    core_ref[0] == 0,
-                    own_ref[start:end, :].astype(f32),
-                    other_ref[start:end, :].astype(f32),
-                )
-            )
-        if stop > half_rows:
-            begin = max(start, half_rows)
-            pieces.append(
-                jnp.where(
-                    core_ref[0] == 0,
-                    other_ref[begin - half_rows : stop - half_rows, :].astype(f32),
-                    own_ref[begin - half_rows : stop - half_rows, :].astype(f32),
-                )
-            )
-        return pieces[0] if len(pieces) == 1 else jnp.concatenate(pieces, axis=0)
-
-    expand_ref[0] = rows(0, channels)[:, :hidden]
-    project_ref[0] = rows(channels, depth_base)[:, :hidden]
-    depth = rows(depth_base, excite_base)[:, :hidden]
-    for i in range(extent):
-        for j in range(extent):
-            depth_ref[i, j] = depth[i * extent + j : i * extent + j + 1]
-    excite = rows(excite_base, reduce_base)[:, :hidden]
-    reduce = rows(reduce_base, reduce_base + up_to(reduced, 8))[:, :hidden]
-    for row in range(reduced):
-        excite_ref[row] = excite[row : row + 1]
-        reduce_ref[row] = reduce[row : row + 1]
+    excite_base = up_to(extent * extent, 8)
+
+    def arrange(first, second):
+        expand_ref[0] = first[:channels, :]
+        project_ref[0] = second[:channels, :]
+        for i in range(extent):
+            for j in range(extent):
+                row = channels + i * extent + j
+                depth_ref[i, j] = first[row : row + 1, :]
+        for r in range(reduced):
+            row = channels + excite_base + r
+            excite_ref[r] = first[row : row + 1, :]
+            row = channels + r
+            reduce_ref[r] = second[row : row + 1, :]
+
+    @pl.when(core_ref[0] == 0)
+    def even():
+        arrange(own_ref, other_ref)
+
+    @pl.when(core_ref[0] != 0)
+    def odd():
+        arrange(other_ref, own_ref)
 
 
 def shards(views, w_expand, w_depth, w_reduce, w_excite, w_project, w_head, w_class):
@@ -605,15 +602,18 @@
     gate_grad = lax.psum(gate_grad, "space")
 
     peers = lax.axis_size("x") * lax.axis_size("y")
-    used = 2 * channels + depth_rows + 2 * tall
-    share = up_to(-(-used // (2 * peers)), 8)
-    rows = 2 * peers * share
-    packed = pl.pallas_call(
+    share = up_to(-(-(channels + depth_rows + tall) // peers), 16)
+    half_rows = peers * share
+    keep, send = pl.pallas_call(
         backward_kernel,
         in_specs=[SMEM] + [VMEM] * 4 + [ANY] * 3 + [VMEM] + [ANY] * 4,
-        out_specs=VMEM,
-        out_shape=jax.ShapeDtypeStruct((rows, broad), f32),
+        out_specs=[VMEM, VMEM],
+        out_shape=[
+            jax.ShapeDtypeStruct((peers, share, hidden), f32),
+            jax.ShapeDtypeStruct((peers, share, hidden), bf16),
+        ],
         scratch_shapes=[
+            pltpu.VMEM((2 * half_rows, broad), f32),
             pltpu.VMEM((16 * columns, channels), bf16),
             pltpu.VMEM((channels, 16 * columns), bf16),
             pltpu.VMEM((channels, broad), bf16),
@@ -631,26 +631,22 @@
         compiler_params=PARAMS,
         name="depthwise_grad",
     )(
-        index("space"), gate_grad, squeeze, reduce_t, excite_w, cell_rows, cells_t,
+        jnp.concatenate([index("space"), index("core")]), gate_grad, squeeze, reduce_t, excite_w, cell_rows, cells_t,
         expand_w, depth_w, half, grad_block, project_t, project_grad,
     )
 
-    halves = packed.reshape(2, peers, share, broad)
-    core = lax.axis_index("core")
     swap = [(0, 1), (1, 0)]
-    keep = lax.dynamic_index_in_dim(halves, core, 0, False)
-    send = lax.dynamic_index_in_dim(halves, 1 - core, 0, False)
-    both = (keep + lax.ppermute(send, "core", swap)).astype(bf16)
+    both = (keep + lax.ppermute(send, "core", swap).astype(f32)).astype(bf16)
     pieces = lax.all_to_all(both, ("x", "y"), 0, 0, tiled=True)
     piece = jnp.sum(pieces.astype(f32), axis=0)
-    for step in (1, 2):
+    for step in (1, 3):
         piece = piece + lax.ppermute(piece, "space", [(i, i ^ step) for i in range(space)])
     copies = jnp.broadcast_to(piece[None], pieces.shape)
     gathered = lax.all_to_all(copies, ("x", "y"), 0, 0, tiled=True)
     remote = lax.ppermute(gathered, "core", swap)
     g_expand, g_depth, g_reduce, g_excite, g_project = pl.pallas_call(
         unpack_kernel,
-        in_specs=[SMEM] + [VMEM] * 2,
+        in_specs=[SMEM, VMEM, VMEM],
         out_specs=[VMEM] * 5,
         out_shape=[
             jax.ShapeDtypeStruct((1, channels, hidden), f32),
@@ -659,9 +655,9 @@
             jax.ShapeDtypeStruct((reduced, 1, hidden), f32),
             jax.ShapeDtypeStruct((1, channels, hidden), f32),
         ],
-        compiler_params=PARAMS,
+        compiler_params=pltpu.CompilerParams(vmem_limit_bytes=24 * 1024 * 1024),
         name="unpack",
-    )(index("core"), gathered.reshape(peers * share, broad), remote.reshape(peers * share, broad))
+    )(index("core"), gathered.reshape(half_rows, hidden), remote.reshape(half_rows, hidden))
     return (
         g_expand,
         g_depth.transpose(2, 0, 1, 3),

time: 181 us -> 175 us (0.967)
  local copies, waits for them, and re-layouts: 7.85 us -> 4.38 us
  starting transfers between devices: 29.7 us -> 27.8 us
  other arithmetic: 1.8 us -> 3.66 us
    squeeze x1 -> x0, local copies, waits for them, and re-layouts: 2.55 us -> none  [shards(): send = lax.dynamic_index_in_dim(halves, 1 - core, 0, False)]
    ppermute x2, starting transfers between devices: 6.03 us -> 4.16 us  [shards(): lax.ppermute(piece, 'space', [(i, i ^ step) for i in range(space)])]
where the time goes in v5:
time: 175 us
  Pallas kernels  61.1 us (35%)
  blocking collectives  54.2 us (31%)
  starting transfers between devices  27.8 us (16%)
  waiting for transfers between devices  22.6 us (13%)
  local copies, waits for them, and re-layouts  4.38 us (3%)
  other arithmetic  3.66 us (2%)
    pallas_call x1, Pallas kernels, shards(): pl.pallas_call(backward_kernel, in_specs=[SMEM] + [VMEM] * 4 + [ANY] * 3...  25.6 us
    all_to_all x1, blocking collectives, shards(): pieces = lax.all_to_all(both, ('x', 'y'), 0, 0, tiled=True)  18.1 us
    all_to_all x1, blocking collectives, shards(): gathered = lax.all_to_all(copies, ('x', 'y'), 0, 0, tiled=True)  17 us
    pallas_call x1, Pallas kernels, shards(): pl.pallas_call(forward_kernel, in_specs=[VMEM] * 5, out_specs=[ANY] * 4 +...  12.7 us
    pallas_call x1, Pallas kernels, shards(): pl.pallas_call(head_grad_kernel, in_specs=[SMEM, VMEM] + [ANY] * 5, out_s...  11.3 us
    psum x1, blocking collectives, shards(): squeeze = lax.psum(squeeze, 'space')  11 us
    pallas_call x1, Pallas kernels, shards(): pl.pallas_call(head_kernel, in_specs=[ANY] + [VMEM] * 3 + [ANY] * 4, out_...  9.93 us
    psum x1, blocking collectives, shards(): gate_grad = lax.psum(gate_grad, 'space')  8.11 us
  transfers between devices with their start and end apart: 7, of which 6 were waited for; matrix products, arithmetic and copies ran while one was open for 2% of the time, Pallas kernels for 0%

profile of v5, /device:TPU:1, one launch (start us, length us, event | category | flops | bytes accessed | tf_op | source)
XLA Modules:
  0.0 174.6 jit_solution(4089875943331980655)
XLA Ops:
  0.6 0.0 copy-start.1
  0.6 0.0 copy-start.7
  0.7 0.0 copy-start.4
  0.7 0.0 copy-start.3
  0.7 1.3 copy.13
  2.0 0.0 copy-start
  2.0 5.7 %collective-permute-start = (bf16[2,100,176]{2,1,0:T(8,128)(2,1)S(1)}, bf16[2,100,176]{2,1,0:T(8,128)(2,1)S(1)}, u32[]{:S(2)}, u32[]{:S(2)}) collective-permute-start(bf16[2,100,176]{2,1,0:T(8,128)(2,1)S(1)} %get-tuple-element.42), channel_id=1, source_target_pairs={{0,1},{1,2},{2,3},{4,5},{5,6},{6,7},{8,9},{9,10},{10,11},{12,13},{... | collective-permute-start | bytes 211208 | tf_op jit(solution)/shard_map/ppermute | solution.py:509
  7.7 0.0 copy-start.2
  7.7 1.4 collective-permute-start.1
  9.2 0.0 copy-done.1
  9.2 0.0 copy-done.7
  9.3 0.1 convert_element_type.32
  9.3 0.0 copy-done.4
  9.3 0.0 copy-done.3
  9.3 0.9 pad_convert_fusion
  10.2 0.7 pad_convert_fusion.2.depth_ref
  10.9 0.8 pad.24.expand_ref.expand_in
  11.7 0.0 copy-done
  11.7 0.0 copy-done.2
  11.7 0.8 pad.31.project_in
  12.5 0.0 collective-permute-done.before_ref
  12.5 6.7 %collective-permute-done.1.after_ref = bf16[2,100,176]{2,1,0:T(8,128)(2,1)S(1)} collective-permute-done((bf16[2,100,176]{2,1,0:T(8,128)(2,1)S(1)}, bf16[2,100,176]{2,1,0:T(8,128)(2,1)S(1)}, u32[]{:S(2)}, u32[]{:S(2)}) %collective-permute-start.1) | collective-permute-done | bytes 70432 | tf_op jit(solution)/shard_map/ppermute | solution.py:510
  19.2 0.0 copy-done.5
  19.2 0.6 copy-done.6
  19.9 12.7 %expand_depthwise.1 = (bf16[1600,176]{1,0:T(8,128)(2,1)}, bf16[176,1600]{1,0:T(8,128)(2,1)}, bf16[800,176]{1,0:T(8,128)(2,1)}, f32[800,1152]{1,0:T(8,128)}, f32[1,1152]{1,0:T(1,128)}) custom-call(bf16[8,100,176]{2,1,0:T(8,128)(2,1)} %bitcast.33, bf16[2,100,176]{2,1,0:T(8,128)(2,1)} %copy-done.5, bf16[2,100,176]{2,1,0:T(8,128)(2,1)} %copy-done.6, ...), custom_call_target="tpu_custom_call" | custom-call | tf_op jit(solution)/shard_map/expand_depthwise/pallas_call | solution.py:524
  32.6 11.0 %psum.14.squeeze_ref = f32[1,1152]{1,0:T(1,128)} all-reduce(f32[1,1152]{1,0:T(1,128)} %get-tuple-element.24), channel_id=1, replica_groups=mesh['pipe'=2,'x'=4,'y'=4,'core'=2,'space'=4] {'space'}, use_global_device_ids=true, to_apply=%region_0.1 | all-reduce | flops 1152 | bytes 9216 | tf_op jit(solution)/shard_map/psum | solution.py:548
  43.6 9.9 %project_head.1 = (f32[8,1,512]{2,1,0:T(1,128)}, bf16[800,1152]{1,0:T(8,128)(2,1)}, bf16[800,176]{1,0:T(8,128)(2,1)}) custom-call(f32[800,1152]{1,0:T(8,128)} %get-tuple-element.23.half_in, f32[1,1152]{1,0:T(1,128)} %psum.14.squeeze_ref, f32[48,1152]{1,0:T(8,128)} %get-tuple-element.44.reduce_ref, f32[48,1152]{1,0:T(8,128)} %get-tuple-element.43.excite_ref, ...), custom_call_target="tpu_custom_call" | custom-call | tf_op jit(solution)/shard_map/project_head/pallas_call | solution.py:551
  53.5 4.6 %all-to-all-start = ((f32[8,1,512]{2,1,0:T(1,128)}), f32[8,1,512]{2,1,0:T(1,128)S(1)}, u32[]{:S(2)}, u32[]{:S(2)}) async-start(f32[8,1,512]{2,1,0:T(1,128)} %get-tuple-element.26), calls=%async_computation | async-start | bytes 32768 | tf_op jit(solution)/shard_map/all_to_all | solution.py:575
  58.1 0.6 pad_add_fusion.place_ref
  58.7 6.0 %all-to-all-done.logits_ref = f32[8,1,512]{2,1,0:T(1,128)S(1)} async-done(((f32[8,1,512]{2,1,0:T(1,128)}), f32[8,1,512]{2,1,0:T(1,128)S(1)}, u32[]{:S(2)}, u32[]{:S(2)}) %all-to-all-start) | async-done | bytes 16416 | tf_op jit(solution)/shard_map/all_to_all | solution.py:575
  64.7 0.6 copy-done.8
  65.3 11.3 %head_grad.1 = (bf16[800,176]{1,0:T(8,128)(2,1)}, f32[176,1152]{1,0:T(8,128)}, f32[1,1152]{1,0:T(1,128)}) custom-call(s32[1]{0:T(128)} %bitcast.2.which_ref, f32[8,1,512]{2,1,0:T(1,128)} %copy-done.8, bf16[800,176]{1,0:T(8,128)(2,1)} %get-tuple-element.27.block_in, bf16[800,1152]{1,0:T(8,128)(2,1)} %get-tuple-element.28.gated_in, ...), custom_call_target="tpu_custom_call" | custom-call | tf_op jit(solution)/shard_map/head_grad/pallas_call | solution.py:580
  76.7 8.1 %psum.15.gate_grad_ref = f32[1,1152]{1,0:T(1,128)} all-reduce(f32[1,1152]{1,0:T(1,128)} %get-tuple-element.29), channel_id=1, replica_groups=mesh['pipe'=2,'x'=4,'y'=4,'core'=2,'space'=4] {'space'}, use_global_device_ids=true, to_apply=%region_1.2 | all-reduce | flops 1152 | bytes 9216 | tf_op jit(solution)/shard_map/psum | solution.py:602
  84.8 25.6 %depthwise_grad.1 = (f32[16,16,1056]{2,1,0:T(8,128)}, bf16[16,16,1056]{2,1,0:T(8,128)(2,1)}) custom-call(s32[2]{0:T(128)} %pad_add_fusion.place_ref, f32[1,1152]{1,0:T(1,128)} %psum.15.gate_grad_ref, f32[1,1152]{1,0:T(1,128)} %psum.14.squeeze_ref, f32[48,1152]{1,0:T(8,128)} %get-tuple-element.44.reduce_ref, f32[48,1152]{1,0:T(8,128)} %get-tuple-element.43.excite_ref, ...), custom_call_target="tpu_custom_call" | custom-call | tf_op jit(solution)/shard_map/depthwise_grad/pallas_call | solution.py:607
  110.4 6.6 %collective-permute-start.2 = (bf16[16,16,1056]{2,1,0:T(8,128)(2,1)}, bf16[16,16,1056]{2,1,0:T(8,128)(2,1)S(1)}, u32[]{:S(2)}, u32[]{:S(2)}) collective-permute-start(bf16[16,16,1056]{2,1,0:T(8,128)(2,1)} %get-tuple-element.35), channel_id=1, source_target_pairs={{0,4},{4,0},{1,5},{5,1},{2,6},{6,2},{3,7},{7,3},{8,12},{12,8},{9,1... | collective-permute-start | bytes 1622024 | tf_op jit(solution)/shard_map/ppermute | solution.py:639
  116.9 1.8 %collective-permute-done.2 = bf16[16,16,1056]{2,1,0:T(8,128)(2,1)S(1)} collective-permute-done((bf16[16,16,1056]{2,1,0:T(8,128)(2,1)}, bf16[16,16,1056]{2,1,0:T(8,128)(2,1)S(1)}, u32[]{:S(2)}, u32[]{:S(2)}) %collective-permute-start.2) | collective-permute-done | bytes 540704 | tf_op jit(solution)/shard_map/ppermute | solution.py:639
  118.8 1.4 add_convert_fusion
  120.1 18.1 %all_to_all.15 = bf16[16,16,1056]{2,1,0:T(8,128)(2,1)S(1)} all-to-all(bf16[16,16,1056]{2,1,0:T(8,128)(2,1)S(1)} %add_convert_fusion), channel_id=1, replica_groups=mesh['pipe'=2,'x'=4,'y'=4,'core'=2,'space'=4] {'x','y'}, dimensions={0} | all-to-all | bytes 1081344 | tf_op jit(solution)/shard_map/all_to_all | solution.py:640
  138.2 0.1 convert_reduce_fusion
  138.3 2.1 %collective-permute-start.3 = (f32[16,1056]{1,0:T(8,128)S(1)}, f32[16,1056]{1,0:T(8,128)S(1)}, u32[]{:S(2)}, u32[]{:S(2)}) collective-permute-start(f32[16,1056]{1,0:T(8,128)S(1)} %convert_reduce_fusion), channel_id=1, source_target_pairs={{0,1},{1,0},{2,3},{3,2},{4,5},{5,4},{6,7},{7,6},{8,9},{9,8},{10,11... | collective-permute-start | bytes 202760 | tf_op jit(solution)/shard_map/ppermute | solution.py:643
  140.4 2.1 %collective-permute-done.3 = f32[16,1056]{1,0:T(8,128)S(1)} collective-permute-done((f32[16,1056]{1,0:T(8,128)S(1)}, f32[16,1056]{1,0:T(8,128)S(1)}, u32[]{:S(2)}, u32[]{:S(2)}) %collective-permute-start.3) | collective-permute-done | bytes 67616 | tf_op jit(solution)/shard_map/ppermute | solution.py:643
  142.5 2.0 %collective-permute-start.4 = (f32[16,1056]{1,0:T(8,128)S(1)}, f32[16,1056]{1,0:T(8,128)S(1)}, u32[]{:S(2)}, u32[]{:S(2)}) collective-permute-start(f32[16,1056]{1,0:T(8,128)S(1)} %add.24), channel_id=1, source_target_pairs={{0,3},{1,2},{2,1},{3,0},{4,7},{5,6},{6,5},{7,4},{8,11},{9,10},{10,... | collective-permute-start | bytes 202760 | tf_op jit(solution)/shard_map/ppermute | solution.py:643
  144.5 3.5 %collective-permute-done.4 = f32[16,1056]{1,0:T(8,128)S(1)} collective-permute-done((f32[16,1056]{1,0:T(8,128)S(1)}, f32[16,1056]{1,0:T(8,128)S(1)}, u32[]{:S(2)}, u32[]{:S(2)}) %collective-permute-start.4) | collective-permute-done | bytes 67616 | tf_op jit(solution)/shard_map/ppermute | solution.py:643
  148.0 0.1 broadcast_in_dim.2
  148.1 17.0 %all_to_all.16 = f32[16,16,1056]{2,1,0:T(8,128)S(1)} all-to-all(f32[16,16,1056]{2,1,0:T(8,128)S(1)} %broadcast_in_dim.2), channel_id=1, replica_groups=mesh['pipe'=2,'x'=4,'y'=4,'core'=2,'space'=4] {'x','y'}, dimensions={0} | all-to-all | bytes 2162688 | tf_op jit(solution)/shard_map/all_to_all | solution.py:645
  165.1 5.4 %collective-permute-start.5 = (f32[16,16,1056]{2,1,0:T(8,128)S(1)}, f32[16,16,1056]{2,1,0:T(8,128)S(1)}, u32[]{:S(2)}, u32[]{:S(2)}) collective-permute-start(f32[16,16,1056]{2,1,0:T(8,128)S(1)} %all_to_all.16), channel_id=1, source_target_pairs={{0,4},{4,0},{1,5},{5,1},{2,6},{6,2},{3,7},{7,3},{8,12},{12,8},{9,1... | collective-permute-start | bytes 3244040 | tf_op jit(solution)/shard_map/ppermute | solution.py:646
  170.5 2.5 %collective-permute-done.5 = f32[16,16,1056]{2,1,0:T(8,128)S(1)} collective-permute-done((f32[16,16,1056]{2,1,0:T(8,128)S(1)}, f32[16,16,1056]{2,1,0:T(8,128)S(1)}, u32[]{:S(2)}, u32[]{:S(2)}) %collective-permute-start.5) | collective-permute-done | bytes 1081376 | tf_op jit(solution)/shard_map/ppermute | solution.py:646
  173.0 1.6 unpack.1
  (7 shorter events, 0.1 us)
Async XLA Ops:
  0.6 8.5 %copy-start.1 = (bf16[1,176,1056]{2,1,0:T(8,128)(2,1)S(1)}, bf16[1,176,1056]{2,1,0:T(8,128)(2,1)}, u32[]{:S(2)}) copy-start(bf16[1,176,1056]{2,1,0:T(8,128)(2,1)} %param.9) | copy-start | bytes 1115140
  0.6 8.6 %copy-start.7 = (bf16[1,5,5,1056]{3,2,1,0:T(8,128)(2,1)S(1)}, bf16[1,5,5,1056]{3,2,1,0:T(8,128)(2,1)}, u32[]{:S(2)}) copy-start(bf16[1,5,5,1056]{3,2,1,0:T(8,128)(2,1)} %param.10) | copy-start | bytes 158404
  0.7 8.7 %copy-start.4 = (bf16[1,1056,44]{1,2,0:T(8,128)(2,1)S(1)}, bf16[1,1056,44]{1,2,0:T(8,128)(2,1)}, u32[]{:S(2)}) copy-start(bf16[1,1056,44]{1,2,0:T(8,128)(2,1)} %param.11) | copy-start | bytes 278788
  0.7 8.7 %copy-start.3 = (bf16[1,44,1056]{2,1,0:T(8,128)(2,1)S(1)}, bf16[1,44,1056]{2,1,0:T(8,128)(2,1)}, u32[]{:S(2)}) copy-start(bf16[1,44,1056]{2,1,0:T(8,128)(2,1)} %param.12) | copy-start | bytes 278788
  2.0 9.7 %copy-start = (bf16[1,1,8,100,176]{4,3,2,1,0:T(8,128)(2,1)}, bf16[1,1,8,100,176]{4,3,2,1,0:T(8,128)(2,1)S(1)}, u32[]{:S(2)}) copy-start(bf16[1,1,8,100,176]{4,3,2,1,0:T(8,128)(2,1)S(1)} %copy.13) | copy-start | bytes 844804
  2.0 10.5 %collective-permute-start = (bf16[2,100,176]{2,1,0:T(8,128)(2,1)S(1)}, bf16[2,100,176]{2,1,0:T(8,128)(2,1)S(1)}, u32[]{:S(2)}, u32[]{:S(2)}) collective-permute-start(bf16[2,100,176]{2,1,0:T(8,128)(2,1)S(1)} %get-tuple-element.42), channel_id=1, source_target_pairs={{0,1},{1,2},{2,3},{4,5},{5,6},{6,7},{8,9},{9,10},{10,11},{12,13},{... | collective-permute-start | bytes 211208 | tf_op jit(solution)/shard_map/ppermute | solution.py:509
  7.7 3.9 %copy-start.2 = (bf16[1,1056,176]{1,2,0:T(8,128)(2,1)S(1)}, bf16[1,1056,176]{1,2,0:T(8,128)(2,1)}, u32[]{:S(2)}) copy-start(bf16[1,1056,176]{1,2,0:T(8,128)(2,1)} %param.13) | copy-start | bytes 1115140
  7.7 11.5 %collective-permute-start.1 = (bf16[2,100,176]{2,1,0:T(8,128)(2,1)S(1)}, bf16[2,100,176]{2,1,0:T(8,128)(2,1)S(1)}, u32[]{:S(2)}, u32[]{:S(2)}) collective-permute-start(bf16[2,100,176]{2,1,0:T(8,128)(2,1)S(1)} %get-tuple-element.41), channel_id=1, source_target_pairs={{1,0},{2,1},{3,2},{5,4},{6,5},{7,6},{9,8},{10,9},{11,10},{13,12},{... | collective-permute-start | bytes 211208 | tf_op jit(solution)/shard_map/ppermute | solution.py:510
  12.5 6.7 %copy-start.5 = (bf16[2,100,176]{2,1,0:T(8,128)(2,1)}, bf16[2,100,176]{2,1,0:T(8,128)(2,1)S(1)}, u32[]{:S(2)}) copy-start(bf16[2,100,176]{2,1,0:T(8,128)(2,1)S(1)} %collective-permute-done.before_ref) | copy-start | bytes 211204
  19.2 0.6 copy-start.6
  53.5 11.2 %all-to-all-start = ((f32[8,1,512]{2,1,0:T(1,128)}), f32[8,1,512]{2,1,0:T(1,128)S(1)}, u32[]{:S(2)}, u32[]{:S(2)}) async-start(f32[8,1,512]{2,1,0:T(1,128)} %get-tuple-element.26), calls=%async_computation | async-start | bytes 32768 | tf_op jit(solution)/shard_map/all_to_all | solution.py:575
  64.7 0.6 copy-start.8
  110.4 8.4 %collective-permute-start.2 = (bf16[16,16,1056]{2,1,0:T(8,128)(2,1)}, bf16[16,16,1056]{2,1,0:T(8,128)(2,1)S(1)}, u32[]{:S(2)}, u32[]{:S(2)}) collective-permute-start(bf16[16,16,1056]{2,1,0:T(8,128)(2,1)} %get-tuple-element.35), channel_id=1, source_target_pairs={{0,4},{4,0},{1,5},{5,1},{2,6},{6,2},{3,7},{7,3},{8,12},{12,8},{9,1... | collective-permute-start | bytes 1622024 | tf_op jit(solution)/shard_map/ppermute | solution.py:639
  138.3 4.2 %collective-permute-start.3 = (f32[16,1056]{1,0:T(8,128)S(1)}, f32[16,1056]{1,0:T(8,128)S(1)}, u32[]{:S(2)}, u32[]{:S(2)}) collective-permute-start(f32[16,1056]{1,0:T(8,128)S(1)} %convert_reduce_fusion), channel_id=1, source_target_pairs={{0,1},{1,0},{2,3},{3,2},{4,5},{5,4},{6,7},{7,6},{8,9},{9,8},{10,11... | collective-permute-start | bytes 202760 | tf_op jit(solution)/shard_map/ppermute | solution.py:643
  142.5 5.5 %collective-permute-start.4 = (f32[16,1056]{1,0:T(8,128)S(1)}, f32[16,1056]{1,0:T(8,128)S(1)}, u32[]{:S(2)}, u32[]{:S(2)}) collective-permute-start(f32[16,1056]{1,0:T(8,128)S(1)} %add.24), channel_id=1, source_target_pairs={{0,3},{1,2},{2,1},{3,0},{4,7},{5,6},{6,5},{7,4},{8,11},{9,10},{10,... | collective-permute-start | bytes 202760 | tf_op jit(solution)/shard_map/ppermute | solution.py:643
  165.1 7.9 %collective-permute-start.5 = (f32[16,16,1056]{2,1,0:T(8,128)S(1)}, f32[16,16,1056]{2,1,0:T(8,128)S(1)}, u32[]{:S(2)}, u32[]{:S(2)}) collective-permute-start(f32[16,16,1056]{2,1,0:T(8,128)S(1)} %all_to_all.16), channel_id=1, source_target_pairs={{0,4},{4,0},{1,5},{5,1},{2,6},{6,2},{3,7},{7,3},{8,12},{12,8},{9,1... | collective-permute-start | bytes 3244040 | tf_op jit(solution)/shard_map/ppermute | solution.py:646

commit v6 on v5

--- a/solution.py
+++ b/solution.py
@@ -10,9 +10,9 @@
 f32 = jnp.float32
 bf16 = jnp.bfloat16
 LANES = 128
-BAND = 384
+BAND = 1152
 HEAD_CHUNK = 512
-STRIP = 50
+STRIP = 100
 WIDE = 100
 TAPS = 50
 VMEM = pl.BlockSpec(memory_space=pltpu.VMEM)

time: 175 us -> 173 us (0.989)
  Pallas kernels: 61.1 us -> 58.8 us
    pallas_call x1, Pallas kernels: 25.6 us -> 23.4 us  [shards(): pl.pallas_call(backward_kernel, in_specs=[SMEM] + [VMEM] * 4 + [ANY] * 3...]
where the time goes in v6:
time: 173 us; the launch traced here: 172 us
  Pallas kernels  58.8 us (34%)
  blocking collectives  54.4 us (31%)
  starting transfers between devices  27.8 us (16%)
  waiting for transfers between devices  22.6 us (13%)
  local copies, waits for them, and re-layouts  4.38 us (3%)
  other arithmetic  3.66 us (2%)
    pallas_call x1, Pallas kernels, shards(): pl.pallas_call(backward_kernel, in_specs=[SMEM] + [VMEM] * 4 + [ANY] * 3...  23.4 us
    all_to_all x1, blocking collectives, shards(): pieces = lax.all_to_all(both, ('x', 'y'), 0, 0, tiled=True)  18 us
    all_to_all x1, blocking collectives, shards(): gathered = lax.all_to_all(copies, ('x', 'y'), 0, 0, tiled=True)  17 us
    pallas_call x1, Pallas kernels, shards(): pl.pallas_call(forward_kernel, in_specs=[VMEM] * 5, out_specs=[ANY] * 4 +...  12.5 us
    pallas_call x1, Pallas kernels, shards(): pl.pallas_call(head_grad_kernel, in_specs=[SMEM, VMEM] + [ANY] * 5, out_s...  11.3 us
    psum x1, blocking collectives, shards(): squeeze = lax.psum(squeeze, 'space')  11 us
    pallas_call x1, Pallas kernels, shards(): pl.pallas_call(head_kernel, in_specs=[ANY] + [VMEM] * 3 + [ANY] * 4, out_...  9.93 us
    psum x1, blocking collectives, shards(): gate_grad = lax.psum(gate_grad, 'space')  8.33 us
  transfers between devices with their start and end apart: 7, of which 6 were waited for; matrix products, arithmetic and copies ran while one was open for 2% of the time, Pallas kernels for 0%

profile of v6, /device:TPU:1, one launch (start us, length us, event | category | flops | bytes accessed | tf_op | source)
XLA Modules:
  0.0 172.4 jit_solution(9736361206189217472)
XLA Ops:
  0.6 0.0 copy-start.1
  0.6 0.0 copy-start.7
  0.7 0.0 copy-start.4
  0.7 0.0 copy-start.3
  0.7 1.3 copy.13
  2.0 0.0 copy-start
  2.0 5.7 %collective-permute-start = (bf16[2,100,176]{2,1,0:T(8,128)(2,1)S(1)}, bf16[2,100,176]{2,1,0:T(8,128)(2,1)S(1)}, u32[]{:S(2)}, u32[]{:S(2)}) collective-permute-start(bf16[2,100,176]{2,1,0:T(8,128)(2,1)S(1)} %get-tuple-element.42), channel_id=1, source_target_pairs={{0,1},{1,2},{2,3},{4,5},{5,6},{6,7},{8,9},{9,10},{10,11},{12,13},{... | collective-permute-start | bytes 211208 | tf_op jit(solution)/shard_map/ppermute | solution.py:509
  7.7 0.0 copy-start.2
  7.7 1.4 collective-permute-start.1
  9.2 0.0 copy-done.1
  9.2 0.0 copy-done.7
  9.3 0.1 convert_element_type.32
  9.3 0.0 copy-done.4
  9.3 0.0 copy-done.3
  9.3 0.9 pad_convert_fusion
  10.2 0.7 pad_convert_fusion.2.depth_ref
  10.9 0.8 pad.24.expand_ref.expand_in
  11.7 0.0 copy-done
  11.7 0.0 copy-done.2
  11.7 0.8 pad.31.project_in
  12.5 0.0 collective-permute-done.before_ref
  12.5 6.7 %collective-permute-done.1.after_ref = bf16[2,100,176]{2,1,0:T(8,128)(2,1)S(1)} collective-permute-done((bf16[2,100,176]{2,1,0:T(8,128)(2,1)S(1)}, bf16[2,100,176]{2,1,0:T(8,128)(2,1)S(1)}, u32[]{:S(2)}, u32[]{:S(2)}) %collective-permute-start.1) | collective-permute-done | bytes 70432 | tf_op jit(solution)/shard_map/ppermute | solution.py:510
  19.2 0.0 copy-done.5
  19.2 0.6 copy-done.6
  19.9 12.5 %expand_depthwise.1 = (bf16[1600,176]{1,0:T(8,128)(2,1)}, bf16[176,1600]{1,0:T(8,128)(2,1)}, bf16[800,176]{1,0:T(8,128)(2,1)}, f32[800,1152]{1,0:T(8,128)}, f32[1,1152]{1,0:T(1,128)}) custom-call(bf16[8,100,176]{2,1,0:T(8,128)(2,1)} %bitcast.33, bf16[2,100,176]{2,1,0:T(8,128)(2,1)} %copy-done.5, bf16[2,100,176]{2,1,0:T(8,128)(2,1)} %copy-done.6, ...), custom_call_target="tpu_custom_call" | custom-call | tf_op jit(solution)/shard_map/expand_depthwise/pallas_call | solution.py:524
  32.4 11.0 %psum.14.squeeze_ref = f32[1,1152]{1,0:T(1,128)} all-reduce(f32[1,1152]{1,0:T(1,128)} %get-tuple-element.24), channel_id=1, replica_groups=mesh['pipe'=2,'x'=4,'y'=4,'core'=2,'space'=4] {'space'}, use_global_device_ids=true, to_apply=%region_0.1 | all-reduce | flops 1152 | bytes 9216 | tf_op jit(solution)/shard_map/psum | solution.py:548
  43.4 9.9 %project_head.1 = (f32[8,1,512]{2,1,0:T(1,128)}, bf16[800,1152]{1,0:T(8,128)(2,1)}, bf16[800,176]{1,0:T(8,128)(2,1)}) custom-call(f32[800,1152]{1,0:T(8,128)} %get-tuple-element.23.half_in, f32[1,1152]{1,0:T(1,128)} %psum.14.squeeze_ref, f32[48,1152]{1,0:T(8,128)} %get-tuple-element.44.reduce_ref, f32[48,1152]{1,0:T(8,128)} %get-tuple-element.43.excite_ref, ...), custom_call_target="tpu_custom_call" | custom-call | tf_op jit(solution)/shard_map/project_head/pallas_call | solution.py:551
  53.3 4.6 %all-to-all-start = ((f32[8,1,512]{2,1,0:T(1,128)}), f32[8,1,512]{2,1,0:T(1,128)S(1)}, u32[]{:S(2)}, u32[]{:S(2)}) async-start(f32[8,1,512]{2,1,0:T(1,128)} %get-tuple-element.26), calls=%async_computation | async-start | bytes 32768 | tf_op jit(solution)/shard_map/all_to_all | solution.py:575
  57.9 0.6 pad_add_fusion.place_ref
  58.5 6.0 %all-to-all-done.logits_ref = f32[8,1,512]{2,1,0:T(1,128)S(1)} async-done(((f32[8,1,512]{2,1,0:T(1,128)}), f32[8,1,512]{2,1,0:T(1,128)S(1)}, u32[]{:S(2)}, u32[]{:S(2)}) %all-to-all-start) | async-done | bytes 16416 | tf_op jit(solution)/shard_map/all_to_all | solution.py:575
  64.5 0.6 copy-done.8
  65.1 11.3 %head_grad.1 = (bf16[800,176]{1,0:T(8,128)(2,1)}, f32[176,1152]{1,0:T(8,128)}, f32[1,1152]{1,0:T(1,128)}) custom-call(s32[1]{0:T(128)} %bitcast.2.which_ref, f32[8,1,512]{2,1,0:T(1,128)} %copy-done.8, bf16[800,176]{1,0:T(8,128)(2,1)} %get-tuple-element.27.block_in, bf16[800,1152]{1,0:T(8,128)(2,1)} %get-tuple-element.28.gated_in, ...), custom_call_target="tpu_custom_call" | custom-call | tf_op jit(solution)/shard_map/head_grad/pallas_call | solution.py:580
  76.5 8.3 %psum.15.gate_grad_ref = f32[1,1152]{1,0:T(1,128)} all-reduce(f32[1,1152]{1,0:T(1,128)} %get-tuple-element.29), channel_id=1, replica_groups=mesh['pipe'=2,'x'=4,'y'=4,'core'=2,'space'=4] {'space'}, use_global_device_ids=true, to_apply=%region_1.2 | all-reduce | flops 1152 | bytes 9216 | tf_op jit(solution)/shard_map/psum | solution.py:602
  84.8 23.4 %depthwise_grad.1 = (f32[16,16,1056]{2,1,0:T(8,128)}, bf16[16,16,1056]{2,1,0:T(8,128)(2,1)}) custom-call(s32[2]{0:T(128)} %pad_add_fusion.place_ref, f32[1,1152]{1,0:T(1,128)} %psum.15.gate_grad_ref, f32[1,1152]{1,0:T(1,128)} %psum.14.squeeze_ref, f32[48,1152]{1,0:T(8,128)} %get-tuple-element.44.reduce_ref, f32[48,1152]{1,0:T(8,128)} %get-tuple-element.43.excite_ref, ...), custom_call_target="tpu_custom_call" | custom-call | tf_op jit(solution)/shard_map/depthwise_grad/pallas_call | solution.py:607
  108.2 6.6 %collective-permute-start.2 = (bf16[16,16,1056]{2,1,0:T(8,128)(2,1)}, bf16[16,16,1056]{2,1,0:T(8,128)(2,1)S(1)}, u32[]{:S(2)}, u32[]{:S(2)}) collective-permute-start(bf16[16,16,1056]{2,1,0:T(8,128)(2,1)} %get-tuple-element.35), channel_id=1, source_target_pairs={{0,4},{4,0},{1,5},{5,1},{2,6},{6,2},{3,7},{7,3},{8,12},{12,8},{9,1... | collective-permute-start | bytes 1622024 | tf_op jit(solution)/shard_map/ppermute | solution.py:639
  114.8 1.8 %collective-permute-done.2 = bf16[16,16,1056]{2,1,0:T(8,128)(2,1)S(1)} collective-permute-done((bf16[16,16,1056]{2,1,0:T(8,128)(2,1)}, bf16[16,16,1056]{2,1,0:T(8,128)(2,1)S(1)}, u32[]{:S(2)}, u32[]{:S(2)}) %collective-permute-start.2) | collective-permute-done | bytes 540704 | tf_op jit(solution)/shard_map/ppermute | solution.py:639
  116.6 1.4 add_convert_fusion
  118.0 18.0 %all_to_all.15 = bf16[16,16,1056]{2,1,0:T(8,128)(2,1)S(1)} all-to-all(bf16[16,16,1056]{2,1,0:T(8,128)(2,1)S(1)} %add_convert_fusion), channel_id=1, replica_groups=mesh['pipe'=2,'x'=4,'y'=4,'core'=2,'space'=4] {'x','y'}, dimensions={0} | all-to-all | bytes 1081344 | tf_op jit(solution)/shard_map/all_to_all | solution.py:640
  136.0 0.1 convert_reduce_fusion
  136.1 2.1 %collective-permute-start.3 = (f32[16,1056]{1,0:T(8,128)S(1)}, f32[16,1056]{1,0:T(8,128)S(1)}, u32[]{:S(2)}, u32[]{:S(2)}) collective-permute-start(f32[16,1056]{1,0:T(8,128)S(1)} %convert_reduce_fusion), channel_id=1, source_target_pairs={{0,1},{1,0},{2,3},{3,2},{4,5},{5,4},{6,7},{7,6},{8,9},{9,8},{10,11... | collective-permute-start | bytes 202760 | tf_op jit(solution)/shard_map/ppermute | solution.py:643
  138.2 2.1 %collective-permute-done.3 = f32[16,1056]{1,0:T(8,128)S(1)} collective-permute-done((f32[16,1056]{1,0:T(8,128)S(1)}, f32[16,1056]{1,0:T(8,128)S(1)}, u32[]{:S(2)}, u32[]{:S(2)}) %collective-permute-start.3) | collective-permute-done | bytes 67616 | tf_op jit(solution)/shard_map/ppermute | solution.py:643
  140.3 2.0 %collective-permute-start.4 = (f32[16,1056]{1,0:T(8,128)S(1)}, f32[16,1056]{1,0:T(8,128)S(1)}, u32[]{:S(2)}, u32[]{:S(2)}) collective-permute-start(f32[16,1056]{1,0:T(8,128)S(1)} %add.24), channel_id=1, source_target_pairs={{0,3},{1,2},{2,1},{3,0},{4,7},{5,6},{6,5},{7,4},{8,11},{9,10},{10,... | collective-permute-start | bytes 202760 | tf_op jit(solution)/shard_map/ppermute | solution.py:643
  142.4 3.5 %collective-permute-done.4 = f32[16,1056]{1,0:T(8,128)S(1)} collective-permute-done((f32[16,1056]{1,0:T(8,128)S(1)}, f32[16,1056]{1,0:T(8,128)S(1)}, u32[]{:S(2)}, u32[]{:S(2)}) %collective-permute-start.4) | collective-permute-done | bytes 67616 | tf_op jit(solution)/shard_map/ppermute | solution.py:643
  145.9 0.1 broadcast_in_dim.2
  145.9 17.0 %all_to_all.16 = f32[16,16,1056]{2,1,0:T(8,128)S(1)} all-to-all(f32[16,16,1056]{2,1,0:T(8,128)S(1)} %broadcast_in_dim.2), channel_id=1, replica_groups=mesh['pipe'=2,'x'=4,'y'=4,'core'=2,'space'=4] {'x','y'}, dimensions={0} | all-to-all | bytes 2162688 | tf_op jit(solution)/shard_map/all_to_all | solution.py:645
  163.0 5.4 %collective-permute-start.5 = (f32[16,16,1056]{2,1,0:T(8,128)S(1)}, f32[16,16,1056]{2,1,0:T(8,128)S(1)}, u32[]{:S(2)}, u32[]{:S(2)}) collective-permute-start(f32[16,16,1056]{2,1,0:T(8,128)S(1)} %all_to_all.16), channel_id=1, source_target_pairs={{0,4},{4,0},{1,5},{5,1},{2,6},{6,2},{3,7},{7,3},{8,12},{12,8},{9,1... | collective-permute-start | bytes 3244040 | tf_op jit(solution)/shard_map/ppermute | solution.py:646
  168.4 2.5 %collective-permute-done.5 = f32[16,16,1056]{2,1,0:T(8,128)S(1)} collective-permute-done((f32[16,16,1056]{2,1,0:T(8,128)S(1)}, f32[16,16,1056]{2,1,0:T(8,128)S(1)}, u32[]{:S(2)}, u32[]{:S(2)}) %collective-permute-start.5) | collective-permute-done | bytes 1081376 | tf_op jit(solution)/shard_map/ppermute | solution.py:646
  170.8 1.6 unpack.1
  (7 shorter events, 0.1 us)
Async XLA Ops:
  0.6 8.5 %copy-start.1 = (bf16[1,176,1056]{2,1,0:T(8,128)(2,1)S(1)}, bf16[1,176,1056]{2,1,0:T(8,128)(2,1)}, u32[]{:S(2)}) copy-start(bf16[1,176,1056]{2,1,0:T(8,128)(2,1)} %param.9) | copy-start | bytes 1115140
  0.6 8.6 %copy-start.7 = (bf16[1,5,5,1056]{3,2,1,0:T(8,128)(2,1)S(1)}, bf16[1,5,5,1056]{3,2,1,0:T(8,128)(2,1)}, u32[]{:S(2)}) copy-start(bf16[1,5,5,1056]{3,2,1,0:T(8,128)(2,1)} %param.10) | copy-start | bytes 158404
  0.7 8.7 %copy-start.4 = (bf16[1,1056,44]{1,2,0:T(8,128)(2,1)S(1)}, bf16[1,1056,44]{1,2,0:T(8,128)(2,1)}, u32[]{:S(2)}) copy-start(bf16[1,1056,44]{1,2,0:T(8,128)(2,1)} %param.11) | copy-start | bytes 278788
  0.7 8.7 %copy-start.3 = (bf16[1,44,1056]{2,1,0:T(8,128)(2,1)S(1)}, bf16[1,44,1056]{2,1,0:T(8,128)(2,1)}, u32[]{:S(2)}) copy-start(bf16[1,44,1056]{2,1,0:T(8,128)(2,1)} %param.12) | copy-start | bytes 278788
  2.0 9.7 %copy-start = (bf16[1,1,8,100,176]{4,3,2,1,0:T(8,128)(2,1)}, bf16[1,1,8,100,176]{4,3,2,1,0:T(8,128)(2,1)S(1)}, u32[]{:S(2)}) copy-start(bf16[1,1,8,100,176]{4,3,2,1,0:T(8,128)(2,1)S(1)} %copy.13) | copy-start | bytes 844804
  2.0 10.5 %collective-permute-start = (bf16[2,100,176]{2,1,0:T(8,128)(2,1)S(1)}, bf16[2,100,176]{2,1,0:T(8,128)(2,1)S(1)}, u32[]{:S(2)}, u32[]{:S(2)}) collective-permute-start(bf16[2,100,176]{2,1,0:T(8,128)(2,1)S(1)} %get-tuple-element.42), channel_id=1, source_target_pairs={{0,1},{1,2},{2,3},{4,5},{5,6},{6,7},{8,9},{9,10},{10,11},{12,13},{... | collective-permute-start | bytes 211208 | tf_op jit(solution)/shard_map/ppermute | solution.py:509
  7.7 3.9 %copy-start.2 = (bf16[1,1056,176]{1,2,0:T(8,128)(2,1)S(1)}, bf16[1,1056,176]{1,2,0:T(8,128)(2,1)}, u32[]{:S(2)}) copy-start(bf16[1,1056,176]{1,2,0:T(8,128)(2,1)} %param.13) | copy-start | bytes 1115140
  7.7 11.5 %collective-permute-start.1 = (bf16[2,100,176]{2,1,0:T(8,128)(2,1)S(1)}, bf16[2,100,176]{2,1,0:T(8,128)(2,1)S(1)}, u32[]{:S(2)}, u32[]{:S(2)}) collective-permute-start(bf16[2,100,176]{2,1,0:T(8,128)(2,1)S(1)} %get-tuple-element.41), channel_id=1, source_target_pairs={{1,0},{2,1},{3,2},{5,4},{6,5},{7,6},{9,8},{10,9},{11,10},{13,12},{... | collective-permute-start | bytes 211208 | tf_op jit(solution)/shard_map/ppermute | solution.py:510
  12.5 6.7 %copy-start.5 = (bf16[2,100,176]{2,1,0:T(8,128)(2,1)}, bf16[2,100,176]{2,1,0:T(8,128)(2,1)S(1)}, u32[]{:S(2)}) copy-start(bf16[2,100,176]{2,1,0:T(8,128)(2,1)S(1)} %collective-permute-done.before_ref) | copy-start | bytes 211204
  19.2 0.6 copy-start.6
  53.3 11.2 %all-to-all-start = ((f32[8,1,512]{2,1,0:T(1,128)}), f32[8,1,512]{2,1,0:T(1,128)S(1)}, u32[]{:S(2)}, u32[]{:S(2)}) async-start(f32[8,1,512]{2,1,0:T(1,128)} %get-tuple-element.26), calls=%async_computation | async-start | bytes 32768 | tf_op jit(solution)/shard_map/all_to_all | solution.py:575
  64.5 0.6 copy-start.8
  108.2 8.4 %collective-permute-start.2 = (bf16[16,16,1056]{2,1,0:T(8,128)(2,1)}, bf16[16,16,1056]{2,1,0:T(8,128)(2,1)S(1)}, u32[]{:S(2)}, u32[]{:S(2)}) collective-permute-start(bf16[16,16,1056]{2,1,0:T(8,128)(2,1)} %get-tuple-element.35), channel_id=1, source_target_pairs={{0,4},{4,0},{1,5},{5,1},{2,6},{6,2},{3,7},{7,3},{8,12},{12,8},{9,1... | collective-permute-start | bytes 1622024 | tf_op jit(solution)/shard_map/ppermute | solution.py:639
  136.1 4.2 %collective-permute-start.3 = (f32[16,1056]{1,0:T(8,128)S(1)}, f32[16,1056]{1,0:T(8,128)S(1)}, u32[]{:S(2)}, u32[]{:S(2)}) collective-permute-start(f32[16,1056]{1,0:T(8,128)S(1)} %convert_reduce_fusion), channel_id=1, source_target_pairs={{0,1},{1,0},{2,3},{3,2},{4,5},{5,4},{6,7},{7,6},{8,9},{9,8},{10,11... | collective-permute-start | bytes 202760 | tf_op jit(solution)/shard_map/ppermute | solution.py:643
  140.3 5.5 %collective-permute-start.4 = (f32[16,1056]{1,0:T(8,128)S(1)}, f32[16,1056]{1,0:T(8,128)S(1)}, u32[]{:S(2)}, u32[]{:S(2)}) collective-permute-start(f32[16,1056]{1,0:T(8,128)S(1)} %add.24), channel_id=1, source_target_pairs={{0,3},{1,2},{2,1},{3,0},{4,7},{5,6},{6,5},{7,4},{8,11},{9,10},{10,... | collective-permute-start | bytes 202760 | tf_op jit(solution)/shard_map/ppermute | solution.py:643
  163.0 7.9 %collective-permute-start.5 = (f32[16,16,1056]{2,1,0:T(8,128)S(1)}, f32[16,16,1056]{2,1,0:T(8,128)S(1)}, u32[]{:S(2)}, u32[]{:S(2)}) collective-permute-start(f32[16,16,1056]{2,1,0:T(8,128)S(1)} %all_to_all.16), channel_id=1, source_target_pairs={{0,4},{4,0},{1,5},{5,1},{2,6},{6,2},{3,7},{7,3},{8,12},{12,8},{9,1... | collective-permute-start | bytes 3244040 | tf_op jit(solution)/shard_map/ppermute | solution.py:646

commit v7 on v6

--- a/solution.py
+++ b/solution.py
@@ -351,7 +351,7 @@
     core = place_ref[1]
     mine = pl.ds(pl.multiple_of(core * half_rows, half_rows), half_rows)
     theirs = pl.ds(pl.multiple_of((1 - core) * half_rows, half_rows), half_rows)
-    keep_ref[...] = out_ref[mine, :][:, :hidden].reshape(keep_ref.shape)
+    keep_ref[...] = out_ref[mine, :][:, :hidden].astype(bf16).reshape(keep_ref.shape)
     send_ref[...] = out_ref[theirs, :][:, :hidden].astype(bf16).reshape(send_ref.shape)
 
 
@@ -609,7 +609,7 @@
         in_specs=[SMEM] + [VMEM] * 4 + [ANY] * 3 + [VMEM] + [ANY] * 4,
         out_specs=[VMEM, VMEM],
         out_shape=[
-            jax.ShapeDtypeStruct((peers, share, hidden), f32),
+            jax.ShapeDtypeStruct((peers, share, hidden), bf16),
             jax.ShapeDtypeStruct((peers, share, hidden), bf16),
         ],
         scratch_shapes=[
@@ -636,7 +636,8 @@
     )
 
     swap = [(0, 1), (1, 0)]
-    both = (keep + lax.ppermute(send, "core", swap).astype(f32)).astype(bf16)
+    received = lax.ppermute(send, "core", swap)
+    both = (keep.astype(f32) + received.astype(f32)).astype(bf16)
     pieces = lax.all_to_all(both, ("x", "y"), 0, 0, tiled=True)
     piece = jnp.sum(pieces.astype(f32), axis=0)
     for step in (1, 3):

time: 173 us -> 173 us (level)
  no operation moved by 1% of the time
where the time goes in v7:
time: 173 us; the launch traced here: 172 us
  Pallas kernels  58.5 us (34%)
  blocking collectives  54.4 us (31%)
  starting transfers between devices  27.8 us (16%)
  waiting for transfers between devices  22.6 us (13%)
  local copies, waits for them, and re-layouts  4.38 us (3%)
  other arithmetic  3.49 us (2%)
    pallas_call x1, Pallas kernels, shards(): pl.pallas_call(backward_kernel, in_specs=[SMEM] + [VMEM] * 4 + [ANY] * 3...  23.2 us
    all_to_all x1, blocking collectives, shards(): pieces = lax.all_to_all(both, ('x', 'y'), 0, 0, tiled=True)  18 us
    all_to_all x1, blocking collectives, shards(): gathered = lax.all_to_all(copies, ('x', 'y'), 0, 0, tiled=True)  17 us
    pallas_call x1, Pallas kernels, shards(): pl.pallas_call(forward_kernel, in_specs=[VMEM] * 5, out_specs=[ANY] * 4 +...  12.5 us
    pallas_call x1, Pallas kernels, shards(): pl.pallas_call(head_grad_kernel, in_specs=[SMEM, VMEM] + [ANY] * 5, out_s...  11.3 us
    psum x1, blocking collectives, shards(): squeeze = lax.psum(squeeze, 'space')  11 us
    pallas_call x1, Pallas kernels, shards(): pl.pallas_call(head_kernel, in_specs=[ANY] + [VMEM] * 3 + [ANY] * 4, out_...  9.93 us
    psum x1, blocking collectives, shards(): gate_grad = lax.psum(gate_grad, 'space')  8.33 us
  transfers between devices with their start and end apart: 7, of which 6 were waited for; matrix products, arithmetic and copies ran while one was open for 2% of the time, Pallas kernels for 0%

profile of v7, /device:TPU:1, one launch (start us, length us, event | category | flops | bytes accessed | tf_op | source)
XLA Modules:
  0.0 172.0 jit_solution(2673241850758895302)
XLA Ops:
  0.6 0.0 copy-start.1
  0.6 0.0 copy-start.7
  0.7 0.0 copy-start.4
  0.7 0.0 copy-start.3
  0.7 1.3 copy.13
  2.0 0.0 copy-start
  2.0 5.7 %collective-permute-start = (bf16[2,100,176]{2,1,0:T(8,128)(2,1)S(1)}, bf16[2,100,176]{2,1,0:T(8,128)(2,1)S(1)}, u32[]{:S(2)}, u32[]{:S(2)}) collective-permute-start(bf16[2,100,176]{2,1,0:T(8,128)(2,1)S(1)} %get-tuple-element.42), channel_id=1, source_target_pairs={{0,1},{1,2},{2,3},{4,5},{5,6},{6,7},{8,9},{9,10},{10,11},{12,13},{... | collective-permute-start | bytes 211208 | tf_op jit(solution)/shard_map/ppermute | solution.py:509
  7.7 0.0 copy-start.2
  7.7 1.4 collective-permute-start.1
  9.2 0.0 copy-done.1
  9.2 0.0 copy-done.7
  9.3 0.1 convert_element_type.35
  9.3 0.0 copy-done.4
  9.3 0.0 copy-done.3
  9.3 0.9 pad_convert_fusion
  10.2 0.7 pad_convert_fusion.2.depth_ref
  10.9 0.8 pad.24.expand_ref.expand_in
  11.7 0.0 copy-done
  11.7 0.0 copy-done.2
  11.7 0.8 pad.31.project_in
  12.5 0.0 collective-permute-done.before_ref
  12.5 6.7 %collective-permute-done.1.after_ref = bf16[2,100,176]{2,1,0:T(8,128)(2,1)S(1)} collective-permute-done((bf16[2,100,176]{2,1,0:T(8,128)(2,1)S(1)}, bf16[2,100,176]{2,1,0:T(8,128)(2,1)S(1)}, u32[]{:S(2)}, u32[]{:S(2)}) %collective-permute-start.1) | collective-permute-done | bytes 70432 | tf_op jit(solution)/shard_map/ppermute | solution.py:510
  19.2 0.0 copy-done.5
  19.2 0.6 copy-done.6
  19.9 12.5 %expand_depthwise.1 = (bf16[1600,176]{1,0:T(8,128)(2,1)}, bf16[176,1600]{1,0:T(8,128)(2,1)}, bf16[800,176]{1,0:T(8,128)(2,1)}, f32[800,1152]{1,0:T(8,128)}, f32[1,1152]{1,0:T(1,128)}) custom-call(bf16[8,100,176]{2,1,0:T(8,128)(2,1)} %bitcast.33, bf16[2,100,176]{2,1,0:T(8,128)(2,1)} %copy-done.5, bf16[2,100,176]{2,1,0:T(8,128)(2,1)} %copy-done.6, ...), custom_call_target="tpu_custom_call" | custom-call | tf_op jit(solution)/shard_map/expand_depthwise/pallas_call | solution.py:524
  32.4 11.0 %psum.14.squeeze_ref = f32[1,1152]{1,0:T(1,128)} all-reduce(f32[1,1152]{1,0:T(1,128)} %get-tuple-element.24), channel_id=1, replica_groups=mesh['pipe'=2,'x'=4,'y'=4,'core'=2,'space'=4] {'space'}, use_global_device_ids=true, to_apply=%region_0.1 | all-reduce | flops 1152 | bytes 9216 | tf_op jit(solution)/shard_map/psum | solution.py:548
  43.4 9.9 %project_head.1 = (f32[8,1,512]{2,1,0:T(1,128)}, bf16[800,1152]{1,0:T(8,128)(2,1)}, bf16[800,176]{1,0:T(8,128)(2,1)}) custom-call(f32[800,1152]{1,0:T(8,128)} %get-tuple-element.23.half_in, f32[1,1152]{1,0:T(1,128)} %psum.14.squeeze_ref, f32[48,1152]{1,0:T(8,128)} %get-tuple-element.44.reduce_ref, f32[48,1152]{1,0:T(8,128)} %get-tuple-element.43.excite_ref, ...), custom_call_target="tpu_custom_call" | custom-call | tf_op jit(solution)/shard_map/project_head/pallas_call | solution.py:551
  53.3 4.6 %all-to-all-start = ((f32[8,1,512]{2,1,0:T(1,128)}), f32[8,1,512]{2,1,0:T(1,128)S(1)}, u32[]{:S(2)}, u32[]{:S(2)}) async-start(f32[8,1,512]{2,1,0:T(1,128)} %get-tuple-element.26), calls=%async_computation | async-start | bytes 32768 | tf_op jit(solution)/shard_map/all_to_all | solution.py:575
  57.9 0.6 pad_add_fusion.place_ref
  58.5 6.0 %all-to-all-done.logits_ref = f32[8,1,512]{2,1,0:T(1,128)S(1)} async-done(((f32[8,1,512]{2,1,0:T(1,128)}), f32[8,1,512]{2,1,0:T(1,128)S(1)}, u32[]{:S(2)}, u32[]{:S(2)}) %all-to-all-start) | async-done | bytes 16416 | tf_op jit(solution)/shard_map/all_to_all | solution.py:575
  64.5 0.6 copy-done.8
  65.1 11.3 %head_grad.1 = (bf16[800,176]{1,0:T(8,128)(2,1)}, f32[176,1152]{1,0:T(8,128)}, f32[1,1152]{1,0:T(1,128)}) custom-call(s32[1]{0:T(128)} %bitcast.2.which_ref, f32[8,1,512]{2,1,0:T(1,128)} %copy-done.8, bf16[800,176]{1,0:T(8,128)(2,1)} %get-tuple-element.27.block_in, bf16[800,1152]{1,0:T(8,128)(2,1)} %get-tuple-element.28.gated_in, ...), custom_call_target="tpu_custom_call" | custom-call | tf_op jit(solution)/shard_map/head_grad/pallas_call | solution.py:580
  76.5 8.3 %psum.15.gate_grad_ref = f32[1,1152]{1,0:T(1,128)} all-reduce(f32[1,1152]{1,0:T(1,128)} %get-tuple-element.29), channel_id=1, replica_groups=mesh['pipe'=2,'x'=4,'y'=4,'core'=2,'space'=4] {'space'}, use_global_device_ids=true, to_apply=%region_1.2 | all-reduce | flops 1152 | bytes 9216 | tf_op jit(solution)/shard_map/psum | solution.py:602
  84.8 23.2 %depthwise_grad.1 = (bf16[16,16,1056]{2,1,0:T(8,128)(2,1)}, bf16[16,16,1056]{2,1,0:T(8,128)(2,1)}) custom-call(s32[2]{0:T(128)} %pad_add_fusion.place_ref, f32[1,1152]{1,0:T(1,128)} %psum.15.gate_grad_ref, f32[1,1152]{1,0:T(1,128)} %psum.14.squeeze_ref, f32[48,1152]{1,0:T(8,128)} %get-tuple-element.44.reduce_ref, f32[48,1152]{1,0:T(8,128)} %get-tuple-element.43.excite_ref, ...), custom_call_target="tpu_custom_call" | custom-call | tf_op jit(solution)/shard_map/depthwise_grad/pallas_call | solution.py:607
  108.0 6.6 %collective-permute-start.2 = (bf16[16,16,1056]{2,1,0:T(8,128)(2,1)}, bf16[16,16,1056]{2,1,0:T(8,128)(2,1)S(1)}, u32[]{:S(2)}, u32[]{:S(2)}) collective-permute-start(bf16[16,16,1056]{2,1,0:T(8,128)(2,1)} %get-tuple-element.35), channel_id=1, source_target_pairs={{0,4},{4,0},{1,5},{5,1},{2,6},{6,2},{3,7},{7,3},{8,12},{12,8},{9,1... | collective-permute-start | bytes 1622024 | tf_op jit(solution)/shard_map/ppermute | solution.py:639
  114.6 1.8 %collective-permute-done.2 = bf16[16,16,1056]{2,1,0:T(8,128)(2,1)S(1)} collective-permute-done((bf16[16,16,1056]{2,1,0:T(8,128)(2,1)}, bf16[16,16,1056]{2,1,0:T(8,128)(2,1)S(1)}, u32[]{:S(2)}, u32[]{:S(2)}) %collective-permute-start.2) | collective-permute-done | bytes 540704 | tf_op jit(solution)/shard_map/ppermute | solution.py:639
  116.4 1.2 add_convert_fusion
  117.6 18.0 %all_to_all.15 = bf16[16,16,1056]{2,1,0:T(8,128)(2,1)S(1)} all-to-all(bf16[16,16,1056]{2,1,0:T(8,128)(2,1)S(1)} %add_convert_fusion), channel_id=1, replica_groups=mesh['pipe'=2,'x'=4,'y'=4,'core'=2,'space'=4] {'x','y'}, dimensions={0} | all-to-all | bytes 1081344 | tf_op jit(solution)/shard_map/all_to_all | solution.py:641
  135.7 0.1 convert_reduce_fusion
  135.7 2.1 %collective-permute-start.3 = (f32[16,1056]{1,0:T(8,128)S(1)}, f32[16,1056]{1,0:T(8,128)S(1)}, u32[]{:S(2)}, u32[]{:S(2)}) collective-permute-start(f32[16,1056]{1,0:T(8,128)S(1)} %convert_reduce_fusion), channel_id=1, source_target_pairs={{0,1},{1,0},{2,3},{3,2},{4,5},{5,4},{6,7},{7,6},{8,9},{9,8},{10,11... | collective-permute-start | bytes 202760 | tf_op jit(solution)/shard_map/ppermute | solution.py:644
  137.9 2.1 %collective-permute-done.3 = f32[16,1056]{1,0:T(8,128)S(1)} collective-permute-done((f32[16,1056]{1,0:T(8,128)S(1)}, f32[16,1056]{1,0:T(8,128)S(1)}, u32[]{:S(2)}, u32[]{:S(2)}) %collective-permute-start.3) | collective-permute-done | bytes 67616 | tf_op jit(solution)/shard_map/ppermute | solution.py:644
  140.0 2.0 %collective-permute-start.4 = (f32[16,1056]{1,0:T(8,128)S(1)}, f32[16,1056]{1,0:T(8,128)S(1)}, u32[]{:S(2)}, u32[]{:S(2)}) collective-permute-start(f32[16,1056]{1,0:T(8,128)S(1)} %add.24), channel_id=1, source_target_pairs={{0,3},{1,2},{2,1},{3,0},{4,7},{5,6},{6,5},{7,4},{8,11},{9,10},{10,... | collective-permute-start | bytes 202760 | tf_op jit(solution)/shard_map/ppermute | solution.py:644
  142.0 3.5 %collective-permute-done.4 = f32[16,1056]{1,0:T(8,128)S(1)} collective-permute-done((f32[16,1056]{1,0:T(8,128)S(1)}, f32[16,1056]{1,0:T(8,128)S(1)}, u32[]{:S(2)}, u32[]{:S(2)}) %collective-permute-start.4) | collective-permute-done | bytes 67616 | tf_op jit(solution)/shard_map/ppermute | solution.py:644
  145.5 0.1 broadcast_in_dim.2
  145.6 17.0 %all_to_all.16 = f32[16,16,1056]{2,1,0:T(8,128)S(1)} all-to-all(f32[16,16,1056]{2,1,0:T(8,128)S(1)} %broadcast_in_dim.2), channel_id=1, replica_groups=mesh['pipe'=2,'x'=4,'y'=4,'core'=2,'space'=4] {'x','y'}, dimensions={0} | all-to-all | bytes 2162688 | tf_op jit(solution)/shard_map/all_to_all | solution.py:646
  162.6 5.4 %collective-permute-start.5 = (f32[16,16,1056]{2,1,0:T(8,128)S(1)}, f32[16,16,1056]{2,1,0:T(8,128)S(1)}, u32[]{:S(2)}, u32[]{:S(2)}) collective-permute-start(f32[16,16,1056]{2,1,0:T(8,128)S(1)} %all_to_all.16), channel_id=1, source_target_pairs={{0,4},{4,0},{1,5},{5,1},{2,6},{6,2},{3,7},{7,3},{8,12},{12,8},{9,1... | collective-permute-start | bytes 3244040 | tf_op jit(solution)/shard_map/ppermute | solution.py:647
  168.0 2.5 %collective-permute-done.5 = f32[16,16,1056]{2,1,0:T(8,128)S(1)} collective-permute-done((f32[16,16,1056]{2,1,0:T(8,128)S(1)}, f32[16,16,1056]{2,1,0:T(8,128)S(1)}, u32[]{:S(2)}, u32[]{:S(2)}) %collective-permute-start.5) | collective-permute-done | bytes 1081376 | tf_op jit(solution)/shard_map/ppermute | solution.py:647
  170.4 1.6 unpack.1
  (7 shorter events, 0.1 us)
Async XLA Ops:
  0.6 8.5 %copy-start.1 = (bf16[1,176,1056]{2,1,0:T(8,128)(2,1)S(1)}, bf16[1,176,1056]{2,1,0:T(8,128)(2,1)}, u32[]{:S(2)}) copy-start(bf16[1,176,1056]{2,1,0:T(8,128)(2,1)} %param.9) | copy-start | bytes 1115140
  0.6 8.6 %copy-start.7 = (bf16[1,5,5,1056]{3,2,1,0:T(8,128)(2,1)S(1)}, bf16[1,5,5,1056]{3,2,1,0:T(8,128)(2,1)}, u32[]{:S(2)}) copy-start(bf16[1,5,5,1056]{3,2,1,0:T(8,128)(2,1)} %param.10) | copy-start | bytes 158404
  0.7 8.7 %copy-start.4 = (bf16[1,1056,44]{1,2,0:T(8,128)(2,1)S(1)}, bf16[1,1056,44]{1,2,0:T(8,128)(2,1)}, u32[]{:S(2)}) copy-start(bf16[1,1056,44]{1,2,0:T(8,128)(2,1)} %param.11) | copy-start | bytes 278788
  0.7 8.7 %copy-start.3 = (bf16[1,44,1056]{2,1,0:T(8,128)(2,1)S(1)}, bf16[1,44,1056]{2,1,0:T(8,128)(2,1)}, u32[]{:S(2)}) copy-start(bf16[1,44,1056]{2,1,0:T(8,128)(2,1)} %param.12) | copy-start | bytes 278788
  2.0 9.7 %copy-start = (bf16[1,1,8,100,176]{4,3,2,1,0:T(8,128)(2,1)}, bf16[1,1,8,100,176]{4,3,2,1,0:T(8,128)(2,1)S(1)}, u32[]{:S(2)}) copy-start(bf16[1,1,8,100,176]{4,3,2,1,0:T(8,128)(2,1)S(1)} %copy.13) | copy-start | bytes 844804
  2.0 10.5 %collective-permute-start = (bf16[2,100,176]{2,1,0:T(8,128)(2,1)S(1)}, bf16[2,100,176]{2,1,0:T(8,128)(2,1)S(1)}, u32[]{:S(2)}, u32[]{:S(2)}) collective-permute-start(bf16[2,100,176]{2,1,0:T(8,128)(2,1)S(1)} %get-tuple-element.42), channel_id=1, source_target_pairs={{0,1},{1,2},{2,3},{4,5},{5,6},{6,7},{8,9},{9,10},{10,11},{12,13},{... | collective-permute-start | bytes 211208 | tf_op jit(solution)/shard_map/ppermute | solution.py:509
  7.7 3.9 %copy-start.2 = (bf16[1,1056,176]{1,2,0:T(8,128)(2,1)S(1)}, bf16[1,1056,176]{1,2,0:T(8,128)(2,1)}, u32[]{:S(2)}) copy-start(bf16[1,1056,176]{1,2,0:T(8,128)(2,1)} %param.13) | copy-start | bytes 1115140
  7.7 11.5 %collective-permute-start.1 = (bf16[2,100,176]{2,1,0:T(8,128)(2,1)S(1)}, bf16[2,100,176]{2,1,0:T(8,128)(2,1)S(1)}, u32[]{:S(2)}, u32[]{:S(2)}) collective-permute-start(bf16[2,100,176]{2,1,0:T(8,128)(2,1)S(1)} %get-tuple-element.41), channel_id=1, source_target_pairs={{1,0},{2,1},{3,2},{5,4},{6,5},{7,6},{9,8},{10,9},{11,10},{13,12},{... | collective-permute-start | bytes 211208 | tf_op jit(solution)/shard_map/ppermute | solution.py:510
  12.5 6.7 %copy-start.5 = (bf16[2,100,176]{2,1,0:T(8,128)(2,1)}, bf16[2,100,176]{2,1,0:T(8,128)(2,1)S(1)}, u32[]{:S(2)}) copy-start(bf16[2,100,176]{2,1,0:T(8,128)(2,1)S(1)} %collective-permute-done.before_ref) | copy-start | bytes 211204
  19.2 0.6 copy-start.6
  53.3 11.2 %all-to-all-start = ((f32[8,1,512]{2,1,0:T(1,128)}), f32[8,1,512]{2,1,0:T(1,128)S(1)}, u32[]{:S(2)}, u32[]{:S(2)}) async-start(f32[8,1,512]{2,1,0:T(1,128)} %get-tuple-element.26), calls=%async_computation | async-start | bytes 32768 | tf_op jit(solution)/shard_map/all_to_all | solution.py:575
  64.5 0.6 copy-start.8
  108.0 8.4 %collective-permute-start.2 = (bf16[16,16,1056]{2,1,0:T(8,128)(2,1)}, bf16[16,16,1056]{2,1,0:T(8,128)(2,1)S(1)}, u32[]{:S(2)}, u32[]{:S(2)}) collective-permute-start(bf16[16,16,1056]{2,1,0:T(8,128)(2,1)} %get-tuple-element.35), channel_id=1, source_target_pairs={{0,4},{4,0},{1,5},{5,1},{2,6},{6,2},{3,7},{7,3},{8,12},{12,8},{9,1... | collective-permute-start | bytes 1622024 | tf_op jit(solution)/shard_map/ppermute | solution.py:639
  135.7 4.2 %collective-permute-start.3 = (f32[16,1056]{1,0:T(8,128)S(1)}, f32[16,1056]{1,0:T(8,128)S(1)}, u32[]{:S(2)}, u32[]{:S(2)}) collective-permute-start(f32[16,1056]{1,0:T(8,128)S(1)} %convert_reduce_fusion), channel_id=1, source_target_pairs={{0,1},{1,0},{2,3},{3,2},{4,5},{5,4},{6,7},{7,6},{8,9},{9,8},{10,11... | collective-permute-start | bytes 202760 | tf_op jit(solution)/shard_map/ppermute | solution.py:644
  140.0 5.5 %collective-permute-start.4 = (f32[16,1056]{1,0:T(8,128)S(1)}, f32[16,1056]{1,0:T(8,128)S(1)}, u32[]{:S(2)}, u32[]{:S(2)}) collective-permute-start(f32[16,1056]{1,0:T(8,128)S(1)} %add.24), channel_id=1, source_target_pairs={{0,3},{1,2},{2,1},{3,0},{4,7},{5,6},{6,5},{7,4},{8,11},{9,10},{10,... | collective-permute-start | bytes 202760 | tf_op jit(solution)/shard_map/ppermute | solution.py:644
  162.6 7.9 %collective-permute-start.5 = (f32[16,16,1056]{2,1,0:T(8,128)S(1)}, f32[16,16,1056]{2,1,0:T(8,128)S(1)}, u32[]{:S(2)}, u32[]{:S(2)}) collective-permute-start(f32[16,16,1056]{2,1,0:T(8,128)S(1)} %all_to_all.16), channel_id=1, source_target_pairs={{0,4},{4,0},{1,5},{5,1},{2,6},{6,2},{3,7},{7,3},{8,12},{12,8},{9,1... | collective-permute-start | bytes 3244040 | tf_op jit(solution)/shard_map/ppermute | solution.py:647
